TPU v7x, 32 devices: a whole 2x2x4 slice. The times are simulated.
32 devices in a mesh: dp: 4 (over y, core), seq: 8 (over z, x).
Axes of the slice: x: 2, y: 2, z: 4, core: 2. Of those that a mesh axis runs over, the one named last changes fastest.
Arguments:
- hidden: bfloat16 [2, 8192, 2048], P(None, ('dp', 'seq')), may hold values from -6 to 6
- lengths: int32 [2, 4, 3], P(None, 'dp'), may hold values from 1 to 1024, 2048 in all within a row
- token_order: int32 [2, 4, 2048], P(None, 'dp'), may hold values from 0 to 2047, each once within a row
- norm_gain: bfloat16 [2, 2048], P(None, ('dp', 'seq')), may hold values from 0.099609375 to 1.8984375
- in_weight: bfloat16 [2, 2048, 8512], P(None, ('dp', 'seq')), may hold values from -0.125 to 0.125
- conv_weight: bfloat16 [2, 4, 4352], P(None, None, ('dp', 'seq')), may hold values from -0.5 to 0.5
- conv_bias: bfloat16 [2, 4352], P(None, ('dp', 'seq')), may hold values from -0.5 to 0.5
- dt_bias: float32 [2, 64], P(None, 'seq'), may hold values from -4 to -1
- log_decay: float32 [2, 64], P(None, 'seq'), may hold values from -4 to 2.5
- skip_gain: float32 [2, 64], P(None, 'seq'), may hold values from 0.2 to 3.3
- gate_gain: bfloat16 [2, 4096], P(None, ('dp', 'seq')), may hold values from 0.099609375 to 1.8984375
- out_weight: bfloat16 [2, 4096, 2048], P(None, None, ('dp', 'seq')), may hold values from -0.09375 to 0.09375
- cotangent: bfloat16 [2, 8192, 2048], P(None, ('dp', 'seq')), may hold values from -6 to 6
Outputs:
- block_out: bfloat16 [2, 8192, 2048], P(None, ('dp', 'seq'))
- grad_hidden: float32 [2, 8192, 2048], P(None, ('dp', 'seq'))
- grad_normgain: float32 [2, 2048], P(None, ('dp', 'seq'))
- grad_inproj: float32 [2, 2048, 8512], P(None, ('dp', 'seq'))
- grad_convtaps: float32 [2, 4, 4352], P(None, None, ('dp', 'seq'))
- grad_convbias: float32 [2, 4352], P(None, ('dp', 'seq'))
- grad_stepbias: float32 [2, 64], P(None, 'seq')
- grad_decay: float32 [2, 64], P(None, 'seq')
- grad_skip: float32 [2, 64], P(None, 'seq')
- grad_gategain: float32 [2, 4096], P(None, ('dp', 'seq'))
- grad_outproj: float32 [2, 4096, 2048], P(None, None, ('dp', 'seq'))
Inputs may be any that keep to these rules, and one draw needn't show every extreme that they name: For each group and micro-batch the 3 lengths sum to 2048, and the longest has exactly 1024 tokens. `token_order`: for each group and micro-batch a permutation of the packed positions.
All inputs are finite; a program needn't handle non-finite values.
Results may differ from a plain program's by a relative error of at most 0.023.
Values may be sent and summed in bfloat16 or wider, within the bound.
No kernel may reach another device: no remote copies, remote signals or barrier semaphores. Data moves between devices by JAX's collectives and lax.ppermute only.
A program may use at most 512 MiB of HBM per device.

v0:
```python
import jax
import jax.numpy as jnp
from jax import lax
from jax.sharding import PartitionSpec as P

D = 2048
DI = 4096
P_SIZE = 64
N = 128
CONV = 4
BLOCK = 256


HIGH = lax.Precision.HIGHEST
EPS = 1e-05


def segments_of(sizes, total):
    ends = jnp.cumsum(sizes)
    places = jnp.arange(total, dtype=jnp.int32)
    return jnp.sum((places[:, None] >= ends[None, :]).astype(jnp.int32), axis=1)


def inverse_of(perm):
    count = perm.shape[0]
    return jnp.zeros((count,), jnp.int32).at[perm].set(jnp.arange(count, dtype=jnp.int32))


def causal_conv(values, segs, taps, shift):
    width = taps.shape[0]
    total = values.shape[0]
    padded = jnp.concatenate(
        [jnp.zeros((width - 1, values.shape[1]), values.dtype), values], axis=0
    )
    segpad = jnp.concatenate([jnp.full((width - 1,), -1, jnp.int32), segs])
    result = jnp.zeros_like(values) + shift[None, :]
    for place in range(width):
        same = (segpad[place : place + total] == segs).astype(values.dtype)
        result = result + taps[place][None, :] * padded[place : place + total] * same[:, None]
    return result


def scan_blocks(inputs, steps, rates, bmat, cmat, segs, block):
    total, heads, size = inputs.shape
    states = bmat.shape[1]
    count = total // block
    places = jnp.arange(block, dtype=jnp.int32)
    lower = (places[:, None] >= places[None, :]).astype(inputs.dtype)

    def advance(carry, piece):
        state, before = carry
        xblock, sblock, bblock, cblock, gblock = piece
        logs = sblock * rates[:, None]
        cums = jnp.dot(logs, lower.T, precision=HIGH)
        same = ((gblock[:, None] == gblock[None, :]) & (lower > 0)).astype(inputs.dtype)
        diffs = cums[:, :, None] - cums[:, None, :]
        decays = jnp.exp(jnp.where(same[None, :, :] > 0, diffs, 0.0)) * same[None, :, :]
        scores = jnp.dot(cblock, bblock.T, precision=HIGH)
        weights = scores[None, :, :] * decays * sblock[:, None, :]
        inner = jnp.einsum("hij,hjp->hip", weights, xblock, precision=HIGH)
        keep = (gblock == before).astype(inputs.dtype)
        into = jnp.exp(cums) * keep[None, :]
        carried = jnp.einsum("in,hpn->hip", cblock, state, precision=HIGH) * into[:, :, None]
        final = gblock[block - 1]
        tail = (
            jnp.exp(cums[:, block - 1][:, None] - cums)
            * (gblock == final).astype(inputs.dtype)[None, :]
            * sblock
        )
        fresh = jnp.einsum("hj,hjp,jn->hpn", tail, xblock, bblock, precision=HIGH)
        state = state * (jnp.exp(cums[:, block - 1]) * keep[block - 1])[:, None, None] + fresh
        return ((state, final), inner + carried)

    pieces = (
        inputs.reshape(count, block, heads, size).transpose(0, 2, 1, 3),
        steps.reshape(count, block, heads).transpose(0, 2, 1),
        bmat.reshape(count, block, states),
        cmat.reshape(count, block, states),
        segs.reshape(count, block),
    )
    start = (jnp.zeros((heads, size, states), inputs.dtype), jnp.array(-1, jnp.int32))
    finish, outputs = lax.scan(jax.checkpoint(advance), start, pieces)
    return outputs.transpose(0, 2, 1, 3).reshape(total, heads, size)


def mixer_heads(
    xpart, bcraw, stepraw, taps_x, shift_x, taps_bc, shift_bc, step_bias, decay_log, skip, segs
):
    total, width = xpart.shape
    heads = stepraw.shape[1]
    states = bcraw.shape[1] // 2
    acts = jax.nn.silu(causal_conv(xpart, segs, taps_x, shift_x))
    bcact = jax.nn.silu(causal_conv(bcraw, segs, taps_bc, shift_bc))
    steps = jax.nn.softplus(stepraw + step_bias[None, :])
    rates = -jnp.exp(decay_log)
    values = acts.reshape(total, heads, width // heads)
    mixed = scan_blocks(values, steps, rates, bcact[:, :states], bcact[:, states:], segs, BLOCK)
    mixed = mixed + skip[None, :, None] * values
    return mixed.reshape(total, width)


def pre_norm(rows, gain):
    return rows * lax.rsqrt(jnp.mean(rows * rows, axis=1, keepdims=True) + EPS) * gain[None, :]


def contract_rows(left, right):
    return lax.dot_general(
        left, right, (((0,), (0,)), ((), ())), preferred_element_type=jnp.float32
    )


def contract_cols(left, right):
    return lax.dot_general(
        left, right, (((1,), (1,)), ((), ())), preferred_element_type=jnp.float32
    )


def fetch(
    layer,
    in_weight,
    out_weight,
    conv_weight,
    conv_bias,
    norm_gain,
    gate_gain,
    groups,
    own_width,
    own_heads,
):
    w_in = in_weight[layer]
    rows_here = w_in.shape[0]
    gate_cols = w_in[:, :DI].reshape(rows_here, groups, own_width)
    input_cols = w_in[:, DI : 2 * DI].reshape(rows_here, groups, own_width)
    state_cols = jnp.broadcast_to(
        w_in[:, 2 * DI : 2 * DI + 2 * N][:, None, :], (rows_here, groups, 2 * N)
    )
    step_cols = w_in[:, 2 * DI + 2 * N :].reshape(rows_here, groups, own_heads)
    pieces = jnp.concatenate([gate_cols, input_cols, step_cols, state_cols], axis=2).reshape(
        rows_here, -1
    )
    out_rows = out_weight[layer].T
    sent_in, sent_out = (
        lax.all_to_all(pieces, "seq", split_axis=1, concat_axis=0, tiled=True),
        lax.all_to_all(out_rows, "seq", split_axis=1, concat_axis=0, tiled=True),
    )
    w_cols, out_cols = (
        lax.all_gather(sent_in, "dp", axis=0, tiled=True),
        lax.all_gather(sent_out, "dp", axis=0, tiled=True),
    )
    norm_scale, taps, shift, gate_scale = (
        lax.all_gather(norm_gain[layer], ("dp", "seq"), axis=0, tiled=True),
        lax.all_gather(conv_weight[layer], ("dp", "seq"), axis=1, tiled=True),
        lax.all_gather(conv_bias[layer], ("dp", "seq"), axis=0, tiled=True),
        lax.all_gather(gate_gain[layer], ("dp", "seq"), axis=0, tiled=True),
    )
    return (w_cols, out_cols, norm_scale, taps, shift, gate_scale)


def head_params(taps, shift, layer, offset, own_width, dt_bias, log_decay, skip_gain):
    taps_x = lax.dynamic_slice_in_dim(taps, offset, own_width, 1).astype(jnp.float32)
    shift_x = lax.dynamic_slice_in_dim(shift, offset, own_width, 0).astype(jnp.float32)
    taps_bc = taps[:, DI:].astype(jnp.float32)
    shift_bc = shift[DI:].astype(jnp.float32)
    return (taps_x, shift_x, taps_bc, shift_bc, dt_bias[layer], log_decay[layer], skip_gain[layer])


def per_device(
    hidden,
    lengths,
    token_order,
    norm_gain,
    in_weight,
    conv_weight,
    conv_bias,
    dt_bias,
    log_decay,
    skip_gain,
    gate_gain,
    out_weight,
    cotangent,
):
    micro = hidden.shape[0]
    layers = in_weight.shape[0]
    groups = lax.axis_size("seq")
    own_heads = dt_bias.shape[1]
    own_width = own_heads * P_SIZE
    own_cols = 2 * own_width + own_heads
    offset = lax.axis_index("seq") * own_width
    tok_here = hidden.shape[1]
    group_tok = token_order.shape[2]
    orders = [token_order[batch, 0] for batch in range(micro)]
    inverses = [inverse_of(orders[batch]) for batch in range(micro)]
    segments = [segments_of(lengths[batch, 0], group_tok) for batch in range(micro)]
    states = [hidden[batch].astype(jnp.float32) for batch in range(micro)]
    record = []

    def load(layer):
        return fetch(
            layer,
            in_weight,
            out_weight,
            conv_weight,
            conv_bias,
            norm_gain,
            gate_gain,
            groups,
            own_width,
            own_heads,
        )

    for layer in range(layers):
        kept = []
        for batch in range(micro):
            weights = load(layer)
            w_cols, out_cols, norm_scale, taps, shift, gate_scale = weights
            rows = states[batch]
            normed = pre_norm(rows, norm_scale.astype(jnp.float32)).astype(jnp.bfloat16)
            bc_piece = jnp.dot(
                normed, w_cols[:, own_cols:], preferred_element_type=jnp.float32
            ).astype(jnp.bfloat16)
            normed_all, bc_all = (
                lax.all_gather(normed, "seq", axis=0, tiled=True),
                lax.all_gather(bc_piece, "seq", axis=0, tiled=True),
            )
            proj = jnp.dot(
                normed_all, w_cols[:, :own_cols], preferred_element_type=jnp.float32
            ).astype(jnp.bfloat16)
            gatez = proj[:, :own_width]
            inverse = inverses[batch]
            head_in = (
                proj[:, own_width : 2 * own_width][inverse],
                bc_all[inverse],
                proj[:, 2 * own_width :][inverse],
            )
            local = head_params(
                taps, shift, layer, offset, own_width, dt_bias, log_decay, skip_gain
            )
            mixed = mixer_heads(
                head_in[0].astype(jnp.float32),
                head_in[1].astype(jnp.float32),
                head_in[2].astype(jnp.float32),
                local[0],
                local[1],
                local[2],
                local[3],
                local[4],
                local[5],
                local[6],
                segments[batch],
            )
            mixbar = mixed[orders[batch]].astype(jnp.bfloat16)
            gated = mixbar.astype(jnp.float32) * jax.nn.silu(gatez.astype(jnp.float32))
            totals = lax.psum(jnp.sum(gated * gated, axis=1), "seq")
            factor = lax.rsqrt(totals / DI + EPS)
            gain_own = lax.dynamic_slice_in_dim(gate_scale, offset, own_width, 0).astype(
                jnp.float32
            )
            normed2 = (gated * factor[:, None] * gain_own[None, :]).astype(jnp.bfloat16)

            def out_term(start, count, values=normed2, matrix=out_cols):
                return contract_cols(values, matrix)

            branch = lax.psum_scatter(
                out_term(jnp.int32(0), lax.axis_size("seq") * tok_here),
                "seq",
                scatter_dimension=0,
                tiled=True,
            )
            states[batch] = rows + branch
            kept.append((rows, normed, normed_all, proj, head_in, mixbar, factor, normed2))
        record.append(kept)
    block_out = jnp.stack([states[batch] for batch in range(micro)]).astype(jnp.bfloat16)
    grads_rows = [cotangent[batch].astype(jnp.float32) for batch in range(micro)]
    results = [None] * layers
    for layer in reversed(range(layers)):
        outt_acc = jnp.zeros((D, own_width), jnp.float32)
        cols_acc = jnp.zeros((D, own_cols), jnp.float32)
        state_acc = jnp.zeros((D, 2 * N), jnp.float32)
        taps_x_acc = jnp.zeros((CONV, own_width), jnp.float32)
        shift_x_acc = jnp.zeros((own_width,), jnp.float32)
        taps_bc_acc = jnp.zeros((CONV, 2 * N), jnp.float32)
        shift_bc_acc = jnp.zeros((2 * N,), jnp.float32)
        norm_acc = jnp.zeros((D,), jnp.float32)
        gate_acc = jnp.zeros((own_width,), jnp.float32)
        sbias_acc = jnp.zeros((own_heads,), jnp.float32)
        decay_acc = jnp.zeros((own_heads,), jnp.float32)
        skip_acc = jnp.zeros((own_heads,), jnp.float32)
        for batch in range(micro):
            weights = load(layer)
            w_cols, out_cols, norm_scale, taps, shift, gate_scale = weights
            rows, normed, normed_all, proj, head_in, mixbar, factor, normed2 = record[layer][batch]
            gout = grads_rows[batch].astype(jnp.bfloat16)
            gout_all = lax.all_gather(gout, "seq", axis=0, tiled=True)
            outt_acc = outt_acc + contract_rows(gout_all, normed2)
            gnormed2 = jnp.dot(gout_all, out_cols, preferred_element_type=jnp.float32)
            gatez = proj[:, :own_width].astype(jnp.float32)
            sigma = jax.nn.sigmoid(gatez)
            active = gatez * sigma
            mixval = mixbar.astype(jnp.float32)
            gated = mixval * active
            gain_own = lax.dynamic_slice_in_dim(gate_scale, offset, own_width, 0).astype(
                jnp.float32
            )
            upstream = gnormed2 * gain_own[None, :]
            gate_acc = gate_acc + jnp.sum(gated * factor[:, None] * gnormed2, axis=0)
            inner = lax.psum(jnp.sum(gated * upstream, axis=1), "seq")
            dgated = (
                factor[:, None] * upstream
                - gated * (factor * factor * factor * inner / DI)[:, None]
            )
            gmix = dgated * active
            ggate = dgated * mixval * sigma * (1.0 + gatez * (1.0 - sigma))
            gmix_packed = gmix.astype(jnp.bfloat16)[inverses[batch]].astype(jnp.float32)
            local = head_params(
                taps, shift, layer, offset, own_width, dt_bias, log_decay, skip_gain
            )
            segs = segments[batch]
            unused_mix, pull_mix = jax.vjp(
                lambda *values: mixer_heads(*values, segs),
                head_in[0].astype(jnp.float32),
                head_in[1].astype(jnp.float32),
                head_in[2].astype(jnp.float32),
                local[0],
                local[1],
                local[2],
                local[3],
                local[4],
                local[5],
                local[6],
            )
            parts = pull_mix(gmix_packed)
            order = orders[batch]
            gbc_piece = lax.psum_scatter(
                parts[1][order].astype(jnp.bfloat16), "seq", scatter_dimension=0, tiled=True
            )
            gproj = jnp.concatenate(
                [
                    ggate.astype(jnp.bfloat16),
                    parts[0][order].astype(jnp.bfloat16),
                    parts[2][order].astype(jnp.bfloat16),
                ],
                axis=1,
            )

            def input_term(start, count, values=gproj, matrix=w_cols[:, :own_cols]):
                return contract_cols(values, matrix)

            gnormed = lax.psum_scatter(
                input_term(jnp.int32(0), lax.axis_size("seq") * tok_here),
                "seq",
                scatter_dimension=0,
                tiled=True,
            )
            gnormed = gnormed + contract_cols(gbc_piece, w_cols[:, own_cols:])
            cols_acc = cols_acc + contract_rows(normed_all, gproj)
            state_acc = state_acc + contract_rows(normed, gbc_piece)
            taps_x_acc = taps_x_acc + parts[3]
            shift_x_acc = shift_x_acc + parts[4]
            taps_bc_acc = taps_bc_acc + parts[5]
            shift_bc_acc = shift_bc_acc + parts[6]
            sbias_acc = sbias_acc + parts[7]
            decay_acc = decay_acc + parts[8]
            skip_acc = skip_acc + parts[9]
            unused_norm, pull_norm = jax.vjp(pre_norm, rows, norm_scale.astype(jnp.float32))
            grows, norm_part = pull_norm(gnormed)
            norm_acc = norm_acc + norm_part
            grads_rows[batch] = grads_rows[batch] + grows
        grad_cols = jnp.concatenate([cols_acc, state_acc], axis=1)
        summed_cols, summed_out = (
            lax.psum_scatter(
                grad_cols.astype(jnp.bfloat16), "dp", scatter_dimension=0, tiled=True
            ).astype(jnp.float32),
            lax.psum_scatter(
                outt_acc.astype(jnp.bfloat16), "dp", scatter_dimension=0, tiled=True
            ).astype(jnp.float32),
        )
        back_cols, back_out = (
            lax.all_to_all(
                summed_cols.astype(jnp.bfloat16), "seq", split_axis=0, concat_axis=1, tiled=True
            ).astype(summed_cols.dtype),
            lax.all_to_all(
                summed_out.astype(jnp.bfloat16), "seq", split_axis=0, concat_axis=1, tiled=True
            ).astype(summed_out.dtype),
        )
        rows_here = back_cols.shape[0]
        split = back_cols.reshape(rows_here, groups, own_cols + 2 * N)
        grad_in = jnp.concatenate(
            [
                split[:, :, :own_width].reshape(rows_here, DI),
                split[:, :, own_width : 2 * own_width].reshape(rows_here, DI),
                jnp.sum(split[:, :, own_cols:], axis=1),
                split[:, :, 2 * own_width : own_cols].reshape(rows_here, groups * own_heads),
            ],
            axis=1,
        )
        grad_out = back_out.T
        taps_full = jnp.zeros((CONV, DI + 2 * N), jnp.float32)
        taps_full = lax.dynamic_update_slice_in_dim(taps_full, taps_x_acc, offset, 1)
        taps_full = lax.dynamic_update_slice_in_dim(taps_full, taps_bc_acc, DI, 1)
        shift_full = jnp.zeros((DI + 2 * N,), jnp.float32)
        shift_full = lax.dynamic_update_slice_in_dim(shift_full, shift_x_acc, offset, 0)
        shift_full = lax.dynamic_update_slice_in_dim(shift_full, shift_bc_acc, DI, 0)
        gate_full = lax.dynamic_update_slice_in_dim(
            jnp.zeros((DI,), jnp.float32), gate_acc, offset, 0
        )
        grad_norm, grad_taps, grad_shift, grad_gate = (
            lax.psum_scatter(norm_acc, ("dp", "seq"), scatter_dimension=0, tiled=True),
            lax.psum_scatter(taps_full, ("dp", "seq"), scatter_dimension=1, tiled=True),
            lax.psum_scatter(shift_full, ("dp", "seq"), scatter_dimension=0, tiled=True),
            lax.psum_scatter(gate_full, ("dp", "seq"), scatter_dimension=0, tiled=True),
        )
        grad_sbias, grad_dlog, grad_skipped = lax.psum((sbias_acc, decay_acc, skip_acc), "dp")
        results[layer] = (
            grad_norm,
            grad_in,
            grad_taps,
            grad_shift,
            grad_sbias,
            grad_dlog,
            grad_skipped,
            grad_gate,
            grad_out,
        )
    grad_hidden = jnp.stack([grads_rows[batch] for batch in range(micro)])
    stacked = [
        jnp.stack([results[layer][member] for layer in range(layers)]) for member in range(9)
    ]
    return (
        block_out,
        grad_hidden,
        stacked[0],
        stacked[1],
        stacked[2],
        stacked[3],
        stacked[4],
        stacked[5],
        stacked[6],
        stacked[7],
        stacked[8],
    )


def solution(mesh):
    return jax.shard_map(
        per_device,
        mesh=mesh,
        in_specs=(
            P(None, ("dp", "seq"), None),
            P(None, "dp", None),
            P(None, "dp", None),
            P(None, ("dp", "seq")),
            P(None, ("dp", "seq"), None),
            P(None, None, ("dp", "seq")),
            P(None, ("dp", "seq")),
            P(None, "seq"),
            P(None, "seq"),
            P(None, "seq"),
            P(None, ("dp", "seq")),
            P(None, None, ("dp", "seq")),
            P(None, ("dp", "seq"), None),
        ),
        out_specs=(
            P(None, ("dp", "seq"), None),
            P(None, ("dp", "seq"), None),
            P(None, ("dp", "seq")),
            P(None, ("dp", "seq"), None),
            P(None, None, ("dp", "seq")),
            P(None, ("dp", "seq")),
            P(None, "seq"),
            P(None, "seq"),
            P(None, "seq"),
            P(None, ("dp", "seq")),
            P(None, None, ("dp", "seq")),
        ),
        check_vma=False,
    )
```

profile of v0, /device:TPU:0, one launch (start us, length us, event | category | flops | bytes accessed | tf_op | source)
XLA Modules:
  0.0 6358.0 jit_solution(6139275376336512803)
XLA Ops:
  16.8 41.9 all_to_all.82
  59.7 40.0 all-reduce.109
  116.1 98.9 %all-gather.2 = bf16[1,4,4352]{1,0,2:T(2,128)(2,1)S(1)} all-gather(bf16[1,4,136]{1,0,2:T(2,128)(2,1)S(1)} %copy.637), channel_id=4, replica_groups=mesh['dp'=4,'seq'=8] {'dp','seq'}, dimensions={2}, use_global_device_ids=true | all-gather | bytes 35904 | tf_op jit(solution)/shard_map/all_gather | solution.py:152
  217.8 63.9 %all-gather.3 = bf16[1,4096]{1,0:T(2,128)(2,1)S(1)} all-gather(bf16[1,128]{1,0:T(2,128)(2,1)S(1)} %get-tuple-element.3268), channel_id=5, replica_groups=mesh['dp'=4,'seq'=8] {'dp','seq'}, dimensions={1}, use_global_device_ids=true | all-gather | bytes 8448 | tf_op jit(solution)/shard_map/all_gather | solution.py:154
  281.7 103.0 %all-gather.6 = bf16[1,4,4352]{1,0,2:T(2,128)(2,1)S(1)} all-gather(bf16[1,4,136]{1,0,2:T(2,128)(2,1)S(1)} %copy.639), channel_id=8, replica_groups=mesh['dp'=4,'seq'=8] {'dp','seq'}, dimensions={2}, use_global_device_ids=true | all-gather | bytes 35904 | tf_op jit(solution)/shard_map/all_gather | solution.py:152
  446.5 12.8 convolution_convert_fusion.1
  462.0 19.5 all-gather.27.cloned.1.call-done
  481.5 12.9 convolution_convert_fusion.3
  567.0 104.9 %while.242 = (s32[]{:T(128)}, f32[8,64,128]{2,1,0:T(8,128)S(1)}, s32[]{:T(128)}, f32[8,8,256,64]{2,3,1,0:T(8,128)}, f32[8,8,256]{2,1,0:T(8,128)S(1)}, /*index=5*...) while((s32[]{:T(128)}, f32[8,64,128]{2,1,0:T(8,128)S(1)}, ...), condition=%wide.region_20.21_spmd.clone.clone, body=%wide.region_19.20_spmd.clone.clone.sunk | while | flops 916139264 | bytes 5231787 | solution.py:82
  681.9 104.6 %while.240 = (s32[]{:T(128)}, f32[8,64,128]{2,1,0:T(8,128)S(1)}, s32[]{:T(128)}, f32[8,8,256,64]{2,3,1,0:T(8,128)}, f32[8,8,256]{2,1,0:T(8,128)S(1)}, /*index=5*...) while((s32[]{:T(128)}, f32[8,64,128]{2,1,0:T(8,128)S(1)}, ...), condition=%wide.region_5.6_spmd.clone.clone, body=%wide.region_4.5_spmd.clone.clone.sunk | while | flops 916139264 | bytes 5231787 | solution.py:82
  852.6 34.1 all-reduce.107
  886.8 13.4 fusion.666
  923.4 71.0 %all_to_all.83 = bf16[64,8,1288]{2,0,1:T(8,128)(2,1)} all-to-all(bf16[64,8,1288]{2,0,1:T(8,128)(2,1)S(1)} %concatenate.46), channel_id=1, replica_groups=mesh['dp'=4,'seq'=8] {'seq'}, dimensions={1} | all-to-all | bytes 2637824 | tf_op jit(solution)/shard_map/all_to_all | solution.py:143
  994.6 28.1 all_to_all.84
  1026.1 196.3 %reduce-scatter.23.cloned.1.call-done = f32[256,2048]{1,0:T(8,128)} async-done(((f32[2048,2048]{1,0:T(8,128)}), f32[256,2048]{1,0:T(8,128)}) %reduce-scatter.23.cloned.1.call-update) | async-done | bytes 2097168 | tf_op jit(solution)/shard_map/reduce_scatter | solution.py:263
  1222.4 286.0 %reduce-scatter.19.cloned.1.call-done = f32[256,2048]{1,0:T(8,128)} async-done(((f32[2048,2048]{1,0:T(8,128)}), f32[256,2048]{1,0:T(8,128)}) %reduce-scatter.19.cloned.1.call-update) | async-done | bytes 2097168 | tf_op jit(solution)/shard_map/reduce_scatter | solution.py:263
  1513.6 38.8 all-gather.37.cloned.1.call-done
  1570.2 67.7 %all-gather.7 = bf16[1,4096]{1,0:T(2,128)(2,1)S(1)} all-gather(bf16[1,128]{1,0:T(2,128)(2,1)S(1)} %copy-done.320), channel_id=9, replica_groups=mesh['dp'=4,'seq'=8] {'dp','seq'}, dimensions={1}, use_global_device_ids=true | all-gather | bytes 8448 | tf_op jit(solution)/shard_map/all_gather | solution.py:154
  1638.5 65.7 %all-gather.57.cloned.1.call-done = bf16[1,2048,2048]{2,1,0:T(8,128)(2,1)} async-done(((bf16[1,256,2048]{2,1,0:T(8,128)(2,1)}), bf16[1,2048,2048]{2,1,0:T(8,128)(2,1)}) %all-gather.57.cloned.1.call-update) | async-done | bytes 8388624 | tf_op jit(solution)/shard_map/all_gather | solution.py:293
  1714.7 29.8 all-gather.39.cloned.1.call-done
  1755.9 29.7 all-gather.49.cloned.1.call-done
  1805.1 106.2 %all-gather.47.cloned.1.call-done = bf16[2048,2048]{1,0:T(8,128)(2,1)} async-done(((bf16[256,2048]{1,0:T(8,128)(2,1)}), bf16[2048,2048]{1,0:T(8,128)(2,1)}) %all-gather.47.cloned.1.call-update) | async-done | bytes 8388624 | tf_op jit(solution)/shard_map/all_gather | solution.py:222
  1911.3 12.8 convolution_convert_fusion
  1927.6 108.8 %all-gather.35.cloned.1.call-done = bf16[2048,2048]{1,0:T(8,128)(2,1)} async-done(((bf16[256,2048]{1,0:T(8,128)(2,1)}), bf16[2048,2048]{1,0:T(8,128)(2,1)}) %all-gather.35.cloned.1.call-update) | async-done | bytes 8388624 | tf_op jit(solution)/shard_map/all_gather | solution.py:222
  2036.4 12.8 convolution_convert_fusion.2
  2123.7 115.9 %while.243 = (s32[]{:T(128)}, f32[8,64,128]{2,1,0:T(8,128)S(1)}, s32[]{:T(128)}, f32[8,8,256,64]{2,3,1,0:T(8,128)}, f32[8,8,256]{2,1,0:T(8,128)S(1)}, /*index=5*...) while((s32[]{:T(128)}, f32[8,64,128]{2,1,0:T(8,128)S(1)}, ...), condition=%wide.region_26.27_spmd.clone.clone, body=%wide.region_25.26_spmd.clone.clone.sunk | while | flops 916139264 | bytes 5231787 | solution.py:82
  2249.6 115.6 %while.241 = (s32[]{:T(128)}, f32[8,64,128]{2,1,0:T(8,128)S(1)}, s32[]{:T(128)}, f32[8,8,256,64]{2,3,1,0:T(8,128)}, f32[8,8,256]{2,1,0:T(8,128)S(1)}, /*index=5*...) while((s32[]{:T(128)}, f32[8,64,128]{2,1,0:T(8,128)S(1)}, ...), condition=%wide.region_11.12_spmd.clone.clone, body=%wide.region_10.11_spmd.clone.clone.sunk | while | flops 916139264 | bytes 5231787 | solution.py:82
  2436.8 34.2 all-reduce.106
  2472.6 56.5 while.236
  2529.1 16.3 multiply_reduce_fusion.21
  2545.4 33.2 all-reduce.105
  2578.7 12.4 fusion.511
  2617.3 181.3 %while.237 = (s32[]{:T(128)}, f32[8]{0:T(128)S(1)}, f32[8,64,128]{2,1,0:T(8,128)S(1)}, f32[8,8,256,64]{2,3,1,0:T(8,128)}, f32[8,8,256]{2,1,0:T(8,128)S(1)}, /*in...) while((s32[]{:T(128)}, f32[8]{0:T(128)S(1)}, ...), condition=%wide.region_77.79_spmd.clone, body=%wide.region_68.78_spmd.clone.sunk | while | flops 2139016192 | bytes 17142804 | solution.py:82
  2822.3 58.1 while.232
  2885.2 180.5 %while.233 = (s32[]{:T(128)}, f32[8]{0:T(128)S(1)}, f32[8,64,128]{2,1,0:T(8,128)S(1)}, f32[8,8,256,64]{2,3,1,0:T(8,128)}, f32[8,8,256]{2,1,0:T(8,128)S(1)}, /*in...) while((s32[]{:T(128)}, f32[8]{0:T(128)S(1)}, ...), condition=%wide.region_43.45_spmd.clone, body=%wide.region_34.44_spmd.clone.sunk | while | flops 2139016192 | bytes 17142804 | solution.py:82
  3102.4 16.2 broadcast_multiply_fusion.1
  3166.4 17.9 fusion.546
  3231.1 17.0 fusion.548
  3260.4 204.0 %reduce-scatter.35.cloned.1.call-done = f32[256,2048]{1,0:T(8,128)} async-done(((f32[2048,2048]{1,0:T(8,128)}), f32[256,2048]{1,0:T(8,128)}) %reduce-scatter.35.cloned.1.call-update) | async-done | bytes 2097168 | tf_op jit(solution)/shard_map/reduce_scatter | solution.py:348
  3468.5 61.8 reduce-scatter.29.cloned.1.call-done
  3530.4 285.8 %reduce-scatter.27.cloned.1.call-done = f32[256,2048]{1,0:T(8,128)} async-done(((f32[2048,2048]{1,0:T(8,128)}), f32[256,2048]{1,0:T(8,128)}) %reduce-scatter.27.cloned.1.call-update) | async-done | bytes 2097168 | tf_op jit(solution)/shard_map/reduce_scatter | solution.py:348
  3822.9 278.8 %reduce-scatter.25.cloned.1.call-done = f32[256,2048]{1,0:T(8,128)} async-done(((f32[2048,2048]{1,0:T(8,128)}), f32[256,2048]{1,0:T(8,128)}) %reduce-scatter.25.cloned.1.call-update) | async-done | bytes 2097168 | tf_op jit(solution)/shard_map/reduce_scatter | solution.py:263
  4111.9 71.0 %while.234 = (s32[]{:T(128)}, f32[8,64,128]{2,1,0:T(8,128)S(1)}, s32[]{:T(128)}, f32[8,8,64,128]{3,2,1,0:T(8,128)S(1)}, s32[8]{0:T(128)}, /*index=5*/f32[8,8,256...) while((s32[]{:T(128)}, f32[8,64,128]{2,1,0:T(8,128)S(1)}, ...), condition=%wide.region_50.52_spmd.clone, body=%wide.region_49.51_spmd.clone.sunk | while | flops 208151056 | bytes 1758134 | solution.py:82
  4186.9 56.9 while.238
  4255.0 102.3 %all-gather.51.cloned.1.call-done = bf16[2048,2048]{1,0:T(8,128)(2,1)} async-done(((bf16[256,2048]{1,0:T(8,128)(2,1)}), bf16[2048,2048]{1,0:T(8,128)(2,1)}) %all-gather.51.cloned.1.call-update) | async-done | bytes 8388624 | tf_op jit(solution)/shard_map/all_gather | solution.py:293
  4357.3 15.9 multiply_reduce_fusion.23
  4373.2 34.7 all-reduce.104
  4408.0 12.5 fusion.508
  4447.5 209.0 %while.235 = (s32[]{:T(128)}, f32[8]{0:T(128)}, f32[8,64,128]{2,1,0:T(8,128)S(1)}, f32[8,8,256,64]{2,3,1,0:T(8,128)}, f32[8,8,256]{2,1,0:T(8,128)}, /*index=5*/f...) while((s32[]{:T(128)}, f32[8]{0:T(128)}, ...), condition=%wide.region_60.62_spmd.clone, body=%wide.region_51.61_spmd.clone.sunk | while | flops 2139016192 | bytes 17175108 | solution.py:82
  4682.7 188.4 %while.239 = (s32[]{:T(128)}, f32[8]{0:T(128)S(1)}, f32[8,64,128]{2,1,0:T(8,128)S(1)}, f32[8,8,256,64]{2,3,1,0:T(8,128)}, f32[8,8,256]{2,1,0:T(8,128)S(1)}, /*in...) while((s32[]{:T(128)}, f32[8]{0:T(128)S(1)}, ...), condition=%wide.region_94.96_spmd.clone, body=%wide.region_85.95_spmd.clone.sunk | while | flops 2139016192 | bytes 17142804 | solution.py:82
  4932.8 14.9 fusion.596
  4947.7 15.5 fusion.505
  4983.8 17.0 multiply_reduce_fusion.34
  5000.9 17.1 multiply_reduce_fusion.30
  5088.8 14.9 fusion.595
  5132.9 15.8 fusion.504
  5159.1 18.6 fusion.552
  5179.3 16.9 fusion.554
  5237.0 20.4 all-to-all-done.5
  5299.9 54.3 all-reduce.115.cloned.1.call-done
  5368.5 275.4 %reduce-scatter.39.cloned.1.call-done = f32[256,2048]{1,0:T(8,128)} async-done(((f32[2048,2048]{1,0:T(8,128)}), f32[256,2048]{1,0:T(8,128)}) %reduce-scatter.39.cloned.1.call-update) | async-done | bytes 2097168 | tf_op jit(solution)/shard_map/reduce_scatter | solution.py:348
  5647.9 281.5 %reduce-scatter.31.cloned.1.call-done = f32[256,2048]{1,0:T(8,128)} async-done(((f32[2048,2048]{1,0:T(8,128)}), f32[256,2048]{1,0:T(8,128)}) %reduce-scatter.31.cloned.1.call-update) | async-done | bytes 2097168 | tf_op jit(solution)/shard_map/reduce_scatter | solution.py:348
  5941.3 274.1 %reduce-scatter.21.cloned.1.call-done = f32[256,2048]{1,0:T(8,128)} async-done(((f32[2048,2048]{1,0:T(8,128)}), f32[256,2048]{1,0:T(8,128)}) %reduce-scatter.21.cloned.1.call-update) | async-done | bytes 2097168 | tf_op jit(solution)/shard_map/reduce_scatter | solution.py:263
  6224.0 120.6 %all-reduce.113.cloned.1.call-done = (f32[2048]{0:T(1024)}, f32[2048]{0:T(1024)}, f32[4352]{0:T(1024)}, f32[4352]{0:T(1024)}, f32[4096]{0:T(1024)}, /*index=5*/f32[4096]{0:T(1024)}) async-done(((f32[2048]{0:T(1024)}, f32[2048]{0:T(1024)}, f32[4352]{0:T(1024)}, f32[4352]{0:T(1024)}, f32[4096]{0:T(1024)}, /*index=5*/f32[4096]{0:T(1024)}), (f32[2048]{0:T(1024)}, f32[2048]{0:T(1024)}, f32[4352]{0:T(1024)}, ...) | async-done | bytes 83984
  (3063 shorter events, 2450.8 us)
Async XLA Ops:
  7.2 94.6 %all-gather.29.cloned.1.call-start = ((), (), s32[]{:S(2)}) async-start(), calls=%async_computation.25 | async-start | bytes 7208960 | tf_op jit(solution)/shard_map/all_gather | solution.py:147
  58.7 356.2 %all-gather.31.cloned.1.call-start = ((), (), s32[]{:S(2)}) async-start(), calls=%async_computation.26 | async-start | bytes 1179648 | tf_op jit(solution)/shard_map/all_gather | solution.py:223
  104.9 321.4 %all-gather.45.cloned.1.call-start = ((), (), s32[]{:S(2)}) async-start(), calls=%async_computation.35 | async-start | bytes 1179648 | tf_op jit(solution)/shard_map/all_gather | solution.py:223
  107.7 338.8 %all-gather.43.cloned.1.call-start = ((), (), s32[]{:S(2)}) async-start(), calls=%async_computation.34 | async-start | bytes 9437184 | tf_op jit(solution)/shard_map/all_gather | solution.py:222
  108.3 373.2 %all-gather.27.cloned.1.call-start = ((), (), s32[]{:S(2)}) async-start(), calls=%async_computation.24 | async-start | bytes 9437184 | tf_op jit(solution)/shard_map/all_gather | solution.py:222
  110.6 303.4 %all-to-all-start.1 = ((bf16[64,8,512]{2,0,1:T(8,128)(2,1)}), bf16[64,8,512]{2,0,1:T(8,128)(2,1)S(1)}, u32[]{:S(2)}, u32[]{:S(2)}) async-start(bf16[64,8,512]{2,0,1:T(8,128)(2,1)} %bitcast.987), calls=%async_computation.1 | async-start | bytes 1048576 | tf_op jit(solution)/shard_map/all_to_all | solution.py:144
  115.7 771.1 %all-gather.33.cloned.1.call-start = ((), (), s32[]{:S(2)}) async-start(), calls=%async_computation.27 | async-start | bytes 2621440 | tf_op jit(solution)/shard_map/all_gather | solution.py:148
  396.9 415.7 %copy-start.134 = (s32[2048]{0:T(1024)}, s32[2048]{0:T(1024)S(1)}, u32[]{:S(2)}) copy-start(s32[2048]{0:T(1024)S(1)} %broadcast_clamp_fusion) | copy-start | bytes 24580
  413.8 2180.2 %copy-start.143 = (s32[2048]{0:T(1024)}, s32[2048]{0:T(1024)S(1)}, u32[]{:S(2)}) copy-start(s32[2048]{0:T(1024)S(1)} %fusion.638) | copy-start | bytes 24580
  413.8 1675.3 %copy-start.145 = (s32[2048]{0:T(1024)}, s32[2048]{0:T(1024)S(1)}, u32[]{:S(2)}) copy-start(s32[2048]{0:T(1024)S(1)} %fusion.637) | copy-start | bytes 24580
  413.9 1688.7 %copy-start.116 = (f32[2048]{0:T(1024)}, f32[2048]{0:T(1024)S(1)}, u32[]{:S(2)}) copy-start(f32[2048]{0:T(1024)S(1)} %get-tuple-element.3203) | copy-start | bytes 24580
  413.9 1688.7 %copy-start.119 = (f32[2048]{0:T(1024)}, f32[2048]{0:T(1024)S(1)}, u32[]{:S(2)}) copy-start(f32[2048]{0:T(1024)S(1)} %get-tuple-element.3204) | copy-start | bytes 24580
  414.0 1688.7 %copy-start.122 = (f32[2048]{0:T(1024)}, f32[2048]{0:T(1024)S(1)}, u32[]{:S(2)}) copy-start(f32[2048]{0:T(1024)S(1)} %get-tuple-element.3205) | copy-start | bytes 24580
  414.0 1688.7 %copy-start.125 = (f32[2048]{0:T(1024)}, f32[2048]{0:T(1024)S(1)}, u32[]{:S(2)}) copy-start(f32[2048]{0:T(1024)S(1)} %get-tuple-element.3283) | copy-start | bytes 24580
  414.0 1688.7 %copy-start.128 = (f32[2048]{0:T(1024)}, f32[2048]{0:T(1024)S(1)}, u32[]{:S(2)}) copy-start(f32[2048]{0:T(1024)S(1)} %get-tuple-element.3284) | copy-start | bytes 24580
  414.0 1688.7 %copy-start.131 = (f32[2048]{0:T(1024)}, f32[2048]{0:T(1024)S(1)}, u32[]{:S(2)}) copy-start(f32[2048]{0:T(1024)S(1)} %get-tuple-element.3285) | copy-start | bytes 24580
  414.8 807.5 %reduce-scatter.23.cloned.1.call-start = ((), (), s32[]{:S(2)}) async-start(), calls=%async_computation.36 | async-start | bytes 18874368 | tf_op jit(solution)/shard_map/reduce_scatter | solution.py:263
  900.2 608.1 %reduce-scatter.19.cloned.1.call-start = ((), (), s32[]{:S(2)}) async-start(), calls=%async_computation.28 | async-start | bytes 18874368 | tf_op jit(solution)/shard_map/reduce_scatter | solution.py:263
  912.7 639.7 %all-gather.37.cloned.1.call-start = ((), (), s32[]{:S(2)}) async-start(), calls=%async_computation.30 | async-start | bytes 7208960 | tf_op jit(solution)/shard_map/all_gather | solution.py:147
  994.5 644.0 %all-gather.41.cloned.1.call-start = ((), (), s32[]{:S(2)}) async-start(), calls=%async_computation.32 | async-start | bytes 2621440 | tf_op jit(solution)/shard_map/all_gather | solution.py:148
  1022.7 485.6 %copy-start.23 = (bf16[2,256,2048]{2,1,0:T(8,128)(2,1)S(1)}, bf16[2,256,2048]{2,1,0:T(8,128)(2,1)}, u32[]{:S(2)}) copy-start(bf16[2,256,2048]{2,1,0:T(8,128)(2,1)} %param.38) | copy-start | bytes 6291460
  1022.7 681.5 %all-gather.57.cloned.1.call-start = ((), (), s32[]{:S(2)}) async-start(), calls=%async_computation.55 | async-start | bytes 9437184 | tf_op jit(solution)/shard_map/all_gather | solution.py:293
  1026.0 718.5 %all-gather.39.cloned.1.call-start = ((), (), s32[]{:S(2)}) async-start(), calls=%async_computation.31 | async-start | bytes 1179648 | tf_op jit(solution)/shard_map/all_gather | solution.py:223
  1026.1 485.7 %copy-start.152 = (f32[2048]{0:T(1024)}, f32[2048]{0:T(1024)S(1)}, u32[]{:S(2)}) copy-start(f32[2048]{0:T(1024)S(1)} %convert_element_type.839) | copy-start | bytes 24580
  1555.0 230.6 %all-gather.49.cloned.1.call-start = ((), (), s32[]{:S(2)}) async-start(), calls=%async_computation.38 | async-start | bytes 1179648 | tf_op jit(solution)/shard_map/all_gather | solution.py:223
  1557.7 353.6 %all-gather.47.cloned.1.call-start = ((), (), s32[]{:S(2)}) async-start(), calls=%async_computation.37 | async-start | bytes 9437184 | tf_op jit(solution)/shard_map/all_gather | solution.py:222
  1558.3 478.1 %all-gather.35.cloned.1.call-start = ((), (), s32[]{:S(2)}) async-start(), calls=%async_computation.29 | async-start | bytes 9437184 | tf_op jit(solution)/shard_map/all_gather | solution.py:222
  1558.9 970.2 %all-gather.55.cloned.1.call-start = ((), (), s32[]{:S(2)}) async-start(), calls=%async_computation.54 | async-start | bytes 9437184 | tf_op jit(solution)/shard_map/all_gather | solution.py:293
  1559.5 1700.9 %reduce-scatter.37.cloned.1.call-start = ((), (), s32[]{:S(2)}) async-start(), calls=%async_computation.46 | async-start | bytes 1179648 | tf_op jit(solution)/shard_map/reduce_scatter | solution.py:333
  1570.0 532.7 %copy-start.222 = (f32[512]{0:T(512)}, f32[512]{0:T(512)S(1)}, u32[]{:S(2)}) copy-start(f32[512]{0:T(512)S(1)} %get-tuple-element.2631) | copy-start | bytes 6148
  1570.0 532.7 %copy-start.224 = (f32[512]{0:T(512)}, f32[512]{0:T(512)S(1)}, u32[]{:S(2)}) copy-start(f32[512]{0:T(512)S(1)} %get-tuple-element.2632) | copy-start | bytes 6148
  1570.0 532.7 %copy-start.226 = (f32[512]{0:T(512)}, f32[512]{0:T(512)S(1)}, u32[]{:S(2)}) copy-start(f32[512]{0:T(512)S(1)} %get-tuple-element.2633) | copy-start | bytes 6148
  1570.0 532.7 %copy-start.228 = (f32[512]{0:T(512)}, f32[512]{0:T(512)S(1)}, u32[]{:S(2)}) copy-start(f32[512]{0:T(512)S(1)} %get-tuple-element.2634) | copy-start | bytes 6148
  1570.2 810.1 %copy-start.230 = (f32[512]{0:T(512)}, f32[512]{0:T(512)S(1)}, u32[]{:S(2)}) copy-start(f32[512]{0:T(512)S(1)} %mul.4015) | copy-start | bytes 6148
  3102.3 362.2 %reduce-scatter.35.cloned.1.call-start = ((), (), s32[]{:S(2)}) async-start(), calls=%async_computation.45 | async-start | bytes 18874368 | tf_op jit(solution)/shard_map/reduce_scatter | solution.py:348
  3184.3 346.0 %reduce-scatter.29.cloned.1.call-start = ((), (), s32[]{:S(2)}) async-start(), calls=%async_computation.41 | async-start | bytes 1179648 | tf_op jit(solution)/shard_map/reduce_scatter | solution.py:333
  3197.5 618.6 %reduce-scatter.27.cloned.1.call-start = ((), (), s32[]{:S(2)}) async-start(), calls=%async_computation.40 | async-start | bytes 18874368 | tf_op jit(solution)/shard_map/reduce_scatter | solution.py:348
  3248.1 853.6 %reduce-scatter.25.cloned.1.call-start = ((), (), s32[]{:S(2)}) async-start(), calls=%async_computation.39 | async-start | bytes 18874368 | tf_op jit(solution)/shard_map/reduce_scatter | solution.py:263
  3260.3 555.8 %copy-start.9 = (f32[256,2048]{1,0:T(8,128)S(1)}, f32[256,2048]{1,0:T(8,128)}, u32[]{:S(2)}) copy-start(f32[256,2048]{1,0:T(8,128)} %copy-done.8) | copy-start | bytes 6291460
  3260.3 555.8 %copy-start.153 = (f32[2048]{0:T(1024)S(1)}, f32[2048]{0:T(1024)}, u32[]{:S(2)}) copy-start(f32[2048]{0:T(1024)} %copy-done.152) | copy-start | bytes 24580
  3260.3 555.8 %copy-start.197 = (f32[256]{0:T(256)S(1)}, f32[256]{0:T(256)}, u32[]{:S(2)}) copy-start(f32[256]{0:T(256)} %copy-done.196) | copy-start | bytes 3076
  3260.4 555.8 %copy-start.200 = (f32[256]{0:T(256)S(1)}, f32[256]{0:T(256)}, u32[]{:S(2)}) copy-start(f32[256]{0:T(256)} %copy-done.199) | copy-start | bytes 3076
  3260.4 983.5 %all-gather.53.cloned.1.call-start = ((), (), s32[]{:S(2)}) async-start(), calls=%async_computation.47 | async-start | bytes 9437184 | tf_op jit(solution)/shard_map/all_gather | solution.py:293
  4107.7 249.6 %all-gather.51.cloned.1.call-start = ((), (), s32[]{:S(2)}) async-start(), calls=%async_computation.42 | async-start | bytes 9437184 | tf_op jit(solution)/shard_map/all_gather | solution.py:293
  4111.0 1037.7 %reduce-scatter.33.cloned.1.call-start = ((), (), s32[]{:S(2)}) async-start(), calls=%async_computation.44 | async-start | bytes 1179648 | tf_op jit(solution)/shard_map/reduce_scatter | solution.py:333
  4902.0 249.5 %reduce-scatter.41.cloned.1.call-start = ((), (), s32[]{:S(2)}) async-start(), calls=%async_computation.49 | async-start | bytes 1179648 | tf_op jit(solution)/shard_map/reduce_scatter | solution.py:333
  4914.6 294.1 %reduce-scatter.49.cloned.1.call-start = ((), (), s32[]{:S(2)}) async-start(), calls=%async_computation.53 | async-start | bytes 2621440 | tf_op jit(solution)/shard_map/reduce_scatter | solution.py:373
  4932.7 281.7 %reduce-scatter.45.cloned.1.call-start = ((), (), s32[]{:S(2)}) async-start(), calls=%async_computation.51 | async-start | bytes 6594560 | tf_op jit(solution)/shard_map/reduce_scatter | solution.py:370
  4968.0 295.5 %reduce-scatter.47.cloned.1.call-start = ((), (), s32[]{:S(2)}) async-start(), calls=%async_computation.52 | async-start | bytes 2621440 | tf_op jit(solution)/shard_map/reduce_scatter | solution.py:373
  5088.7 182.6 %reduce-scatter.43.cloned.1.call-start = ((), (), s32[]{:S(2)}) async-start(), calls=%async_computation.50 | async-start | bytes 6594560 | tf_op jit(solution)/shard_map/reduce_scatter | solution.py:370
  5157.5 196.7 %all-reduce.115.cloned.1.call-start = ((), (), s32[]{:S(2)}) async-start(), calls=%async_computation.57 | async-start | bytes 278528
  5158.9 485.0 %reduce-scatter.39.cloned.1.call-start = ((), (), s32[]{:S(2)}) async-start(), calls=%async_computation.48 | async-start | bytes 18874368 | tf_op jit(solution)/shard_map/reduce_scatter | solution.py:348
  5177.8 751.7 %reduce-scatter.31.cloned.1.call-start = ((), (), s32[]{:S(2)}) async-start(), calls=%async_computation.43 | async-start | bytes 18874368 | tf_op jit(solution)/shard_map/reduce_scatter | solution.py:348
  5196.3 1019.1 %reduce-scatter.21.cloned.1.call-start = ((), (), s32[]{:S(2)}) async-start(), calls=%async_computation.33 | async-start | bytes 18874368 | tf_op jit(solution)/shard_map/reduce_scatter | solution.py:263
  5210.8 14.3 all-to-all-start.7
  5225.1 32.3 all-to-all-start.5
  5263.5 17.7 all-to-all-start.6
  5281.2 76.6 %all-to-all-start.4 = ((bf16[8,64,1288]{2,1,0:T(8,128)(2,1)}), bf16[8,64,1288]{2,1,0:T(8,128)(2,1)}, u32[]{:S(2)}, u32[]{:S(2)}) async-start(bf16[8,64,1288]{2,1,0:T(8,128)(2,1)} %bitcast.122), calls=%async_computation.17 | async-start | bytes 2883584 | tf_op jit(solution)/shard_map/all_to_all | solution.py:378
  5291.7 1052.9 %all-reduce.113.cloned.1.call-start = ((), (), s32[]{:S(2)}) async-start(), calls=%async_computation.56 | async-start | bytes 180224
  5368.5 561.0 %copy-start.24 = (bf16[2,256,2048]{2,1,0:T(8,128)(2,1)S(1)}, bf16[2,256,2048]{2,1,0:T(8,128)(2,1)}, u32[]{:S(2)}) copy-start(bf16[2,256,2048]{2,1,0:T(8,128)(2,1)} %param.38) | copy-start | bytes 6291460
  5368.5 561.0 %copy-start.165 = (f32[2048]{0:T(1024)S(1)}, f32[2048]{0:T(1024)}, u32[]{:S(2)}) copy-start(f32[2048]{0:T(1024)} %copy-done.164) | copy-start | bytes 24580
  5368.5 561.0 %copy-start.166 = (bf16[256,256]{1,0:T(8,128)(2,1)S(1)}, bf16[256,256]{1,0:T(8,128)(2,1)}, u32[]{:S(2)}) copy-start(bf16[256,256]{1,0:T(8,128)(2,1)} %reduce-scatter.33.cloned.1.call-done) | copy-start | bytes 393220
  5368.5 561.0 %copy-start.261 = (f32[256]{0:T(256)S(1)}, f32[256]{0:T(256)}, u32[]{:S(2)}) copy-start(f32[256]{0:T(256)} %copy-done.260) | copy-start | bytes 3076
  5368.5 561.0 %copy-start.263 = (f32[256]{0:T(256)S(1)}, f32[256]{0:T(256)}, u32[]{:S(2)}) copy-start(f32[256]{0:T(256)} %copy-done.262) | copy-start | bytes 3076
  (341 other events, 12022.4 us)
Sparse Core Ops, SparseCore 0:
  58.8 42.9 all-gather.28
  105.0 47.2 all-gather.30
  155.0 47.0 all-gather.44
  204.1 147.6 all-gather.42
  353.7 127.7 all-gather.26
  482.9 20.7 all-gather.32
  900.4 321.9 reduce-scatter.22
  1226.6 281.6 reduce-scatter.18
  1509.9 42.4 all-gather.36
  1553.8 22.5 all-gather.40
  1579.1 125.0 all-gather.56
  1706.2 38.3 all-gather.38
  1746.7 38.9 all-gather.48
  1787.6 123.6 all-gather.46
  1913.3 123.1 all-gather.34
  2038.4 123.1 all-gather.54
  3102.4 60.6 reduce-scatter.36
  3184.5 279.9 reduce-scatter.34
  3467.9 62.4 reduce-scatter.28
  3534.5 281.6 reduce-scatter.26
  3819.9 281.6 reduce-scatter.24
  4107.8 123.9 all-gather.52
  4234.1 123.1 all-gather.50
  4902.1 60.6 reduce-scatter.32
  4966.2 62.3 reduce-scatter.40
  5031.1 30.4 reduce-scatter.48
  5064.0 51.6 reduce-scatter.44
  5118.4 31.3 reduce-scatter.46
  5157.6 49.1 reduce-scatter.42
  5213.2 140.8 all-reduce.114
  5358.4 285.4 reduce-scatter.38
  5647.7 281.7 reduce-scatter.30
  5933.6 281.7 reduce-scatter.20
  6222.7 121.9 all-reduce.112
where the time goes:
time: 6390 us; the launch traced here: 6360 us
  waiting for transfers between devices  2860 us (45%)
  matrix products  1160 us (18%)
  local copies, waits for them, and re-layouts  994 us (16%)
  blocking collectives  656 us (10%)
  other arithmetic  541 us (8%)
  loops' own time  93.4 us (1%)
    reduce_scatter x4, waiting for transfers between devices, per_device(): lax.psum_scatter(input_term(jnp.int32(0), lax.axis_size('seq') * tok_here...  1050 us
    reduce_scatter x4, waiting for transfers between devices, per_device(): lax.psum_scatter(out_term(jnp.int32(0), lax.axis_size('seq') * tok_here),...  1040 us
    dot_general x96, matrix products, advance(): inner = jnp.einsum('hij,hjp->hip', weights, xblock, precision=HIGH)  327 us
    all_gather x4, waiting for transfers between devices, per_device(): lax.all_gather(normed, 'seq', axis=0, tiled=True)  235 us
    all_gather x2, blocking collectives, fetch(): lax.all_gather(conv_weight[layer], ('dp', 'seq'), axis=1, tiled=True)  202 us
    unnamed x36, waiting for transfers between devices  178 us
    all_gather x4, waiting for transfers between devices, per_device(): gout_all = lax.all_gather(gout, 'seq', axis=0, tiled=True)  168 us
    dot_general x128, matrix products, advance(): fresh = jnp.einsum('hj,hjp,jn->hpn', tail, xblock, bblock, precision=HIGH)  162 us
  transfers between devices with their start and end apart: 39, of which 22 were waited for; matrix products, arithmetic and copies ran while one was open for 25% of the time, Pallas kernels for 0%

commit v1 on v0

v1 whole, which is shorter than its diff:
```python
import jax
import jax.numpy as jnp
from jax import lax
from jax.experimental import pallas as pl
from jax.experimental.pallas import tpu as pltpu
from jax.sharding import Mesh
from jax.sharding import PartitionSpec as P

DI = 4096
N = 128
CONV = 4
EPS = 1e-05
PARTS = 1
DEPTH = 4
SWAP = ((0, 1), (1, 0))
CHUNK = 256
LANES = 128
HEAD = 64
FAR = -1e30
VMEM_BYTES = 52 * 1024 * 1024


def sigmoid(v):
    return 0.5 * jnp.tanh(0.5 * v) + 0.5


def dot(a, b):
    return jnp.dot(a, b, preferred_element_type=jnp.float32)


def dot_nt(a, b):
    return lax.dot_general(a, b, (((1,), (1,)), ((), ())), preferred_element_type=jnp.float32)


def dot_tn(a, b):
    return lax.dot_general(a, b, (((0,), (0,)), ((), ())), preferred_element_type=jnp.float32)


def split3(v):
    hi = v.astype(jnp.bfloat16)
    rest = v - hi.astype(jnp.float32)
    mid = rest.astype(jnp.bfloat16)
    lo = (rest - mid.astype(jnp.float32)).astype(jnp.bfloat16)
    return hi, mid, lo


def pack3(v):
    hi, mid, lo = split3(v)
    lane = lax.broadcasted_iota(jnp.int32, v.shape, 1)
    mid = pltpu.roll(mid.astype(jnp.float32), 32, 1)
    lo = pltpu.roll(lo.astype(jnp.float32), 64, 1)
    joined = jnp.where(
        lane < 32, hi.astype(jnp.float32), jnp.where(lane < 64, mid, jnp.where(lane < 96, lo, 0.0))
    )
    return joined.astype(jnp.bfloat16)


def spread(rows_width, per):
    row = lax.broadcasted_iota(jnp.int32, (LANES, rows_width), 0)
    col = lax.broadcasted_iota(jnp.int32, (LANES, rows_width), 1)
    return ((row < 96) & (row % 32 == col // per)).astype(jnp.bfloat16)


def exact_left(matrix, v):
    hi, mid, lo = split3(v)
    return dot(matrix, hi) + dot(matrix, mid) + dot(matrix, lo)


def chunk_setup(st_ref, meta_ref, segrow_ref, hp_ref, chunk, cumb_ref, cumt_ref, mask_ref, wide_ref, tall_ref):
    raw = st_ref[...].astype(jnp.float32) + hp_ref[0:1, :]
    steps = jnp.maximum(raw, 0.0) + jnp.log1p(jnp.exp(-jnp.abs(raw)))
    row = lax.broadcasted_iota(jnp.int32, (chunk, chunk), 0)
    col = lax.broadcasted_iota(jnp.int32, (chunk, chunk), 1)
    lower = (row >= col).astype(jnp.bfloat16)
    cum = exact_left(lower, steps * hp_ref[1:2, :])
    cumb_ref[...] = dot(pack3(cum), tall_ref[...])
    cumt_ref[...] = cum.T
    seg = meta_ref[:, 5:6]
    same = jnp.broadcast_to(seg, (chunk, chunk)) == segrow_ref[0]
    mask_ref[...] = jnp.where(same & (row >= col), 0.0, FAR)
    e = jnp.exp(cum) * meta_ref[:, 3:4]
    decay = jnp.exp(cum[chunk - 1 : chunk, :] - cum) * meta_ref[:, 4:5]
    return raw, steps, cum, e, decay


def conv_parts(pad_ref, sl, chunk, cw, masks):
    here = pad_ref[8 : 8 + chunk, sl]
    back = [pad_ref[8 - m : 8 - m + chunk, sl] * masks[m - 1] for m in (1, 2, 3)]
    pre = cw[4:5, :] + cw[3:4, :] * here
    for m in (1, 2, 3):
        pre = pre + cw[3 - m : 4 - m, :] * back[m - 1]
    return pre, back, here


def forward_kernel(
    gate_ref, x_ref, bc_ref, st_ref, hx_ref, hbc_ref, meta_ref, segrow_ref, cw_ref, cbc_ref, hp_ref, s0_ref,
    mix_ref, gn_ref, ss_ref, states_ref, sout_ref,
    xpad, bpad, masks, cumb_ref, cumt_ref, mask_ref, sexp, eexp, texp, wide_ref, tall_ref, g_ref,
):
    chunk, width = x_ref.shape
    step = pl.program_id(0)

    @pl.when(step == 0)
    def _():
        sout_ref[...] = s0_ref[...]
        xpad[0:8, :] = hx_ref[8:16, :].astype(jnp.float32)
        bpad[0:8, :] = hbc_ref[8:16, :].astype(jnp.float32)
        wide_ref[...] = spread(width, HEAD)
        tall_ref[...] = spread(width * 2, LANES)

    @pl.when(step > 0)
    def _():
        xpad[0:8, :] = xpad[chunk : chunk + 8, :]
        bpad[0:8, :] = bpad[chunk : chunk + 8, :]

    xpad[8 : 8 + chunk, :] = x_ref[...].astype(jnp.float32)
    bpad[8 : 8 + chunk, :] = bc_ref[...].astype(jnp.float32)
    states_ref[0] = sout_ref[...]
    raw, steps, cum, e, decay = chunk_setup(
        st_ref, meta_ref, segrow_ref, hp_ref, chunk, cumb_ref, cumt_ref, mask_ref, wide_ref, tall_ref
    )
    for m in range(3):
        masks[m] = jnp.broadcast_to(meta_ref[:, m : m + 1], (chunk, LANES))
    sexp[...] = dot(pack3(steps), wide_ref[...])
    eexp[...] = dot(pack3(e), wide_ref[...])
    texp[...] = dot(pack3(decay * steps), wide_ref[...])
    bcact = []
    for half in range(2):
        sl = slice(half * LANES, (half + 1) * LANES)
        pre, _, _ = conv_parts(bpad, sl, chunk, cbc_ref[:, sl], masks)
        bcact.append((pre * sigmoid(pre)).astype(jnp.bfloat16))
    bmat, cmat = bcact
    g_ref[...] = dot_nt(cmat, bmat)
    low_lane = lax.broadcasted_iota(jnp.int32, (chunk, LANES), 1) < HEAD
    ss_ref[...] = jnp.zeros_like(ss_ref)

    def pair(p, carry):
        start = pl.multiple_of(p * LANES, LANES)
        sl = pl.ds(start, LANES)
        cw = cw_ref[:, sl]
        pre, _, _ = conv_parts(xpad, sl, chunk, cw, masks)
        xact = pre * sigmoid(pre)
        xs = (xact * sexp[:, sl]).astype(jnp.bfloat16)
        halves = []
        for k in range(2):
            h = 2 * p + k
            cumb = cumb_ref[:, pl.ds(pl.multiple_of(h * LANES, LANES), LANES)]
            cumb = jnp.concatenate([cumb] * (chunk // LANES), axis=1)
            decays = jnp.exp(cumb - cumt_ref[pl.ds(h, 1), :] + mask_ref[...])
            halves.append(dot((g_ref[...] * decays).astype(jnp.bfloat16), xs))
        inner = jnp.where(low_lane, halves[0], halves[1])
        state = sout_ref[:, sl]
        into = eexp[:, sl]
        carried = dot(cmat, state.astype(jnp.bfloat16)) * into
        fresh = dot_tn(bmat, (xact * texp[:, sl]).astype(jnp.bfloat16))
        sout_ref[:, sl] = state * into[chunk - 1 : chunk, :] + fresh
        mixbar = (inner + carried + cw[5:6, :] * xact).astype(jnp.bfloat16)
        mix_ref[:, sl] = mixbar
        gz = gate_ref[:, sl].astype(jnp.float32)
        gated = mixbar.astype(jnp.float32) * (gz * sigmoid(gz))
        gn_ref[:, sl] = (gated * cw[6:7, :]).astype(jnp.bfloat16)
        ss_ref[...] += gated * gated
        return carry

    lax.fori_loop(0, width // LANES, pair, 0)


def common_specs(chunk, width, order):
    bc_at, st_at = 2 * width // 256, (2 * width + 256) // LANES
    return [
        pl.BlockSpec((chunk, width), lambda c: (order(c), 0)),
        pl.BlockSpec((chunk, width), lambda c: (order(c), 1)),
        pl.BlockSpec((chunk, 256), lambda c: (order(c), bc_at)),
        pl.BlockSpec((chunk, LANES), lambda c: (order(c), st_at)),
    ]


def fixed(shape):
    return pl.BlockSpec(shape, lambda c: (0,) * len(shape))


def mixer_forward(proj, halo, meta, segrow, cw, cbc, hp, state, chunk=CHUNK):
    rows = proj.shape[0]
    width = cw.shape[1]
    count = rows // chunk
    same = lambda c: c
    bc_at = 2 * width // 256
    f32 = jnp.float32
    return pl.pallas_call(
        forward_kernel,
        grid=(count,),
        in_specs=common_specs(chunk, width, same)
        + [
            pl.BlockSpec((16, width), lambda c: (0, 1)),
            pl.BlockSpec((16, 256), lambda c: (0, bc_at)),
            pl.BlockSpec((chunk, 8), lambda c: (c, 0)),
            pl.BlockSpec((1, 1, chunk), lambda c: (c, 0, 0)),
            fixed((8, width)),
            fixed((8, 256)),
            fixed((8, LANES)),
            fixed((N, width)),
        ],
        out_specs=[
            pl.BlockSpec((chunk, width), lambda c: (c, 0)),
            pl.BlockSpec((chunk, width), lambda c: (c, 0)),
            pl.BlockSpec((chunk, LANES), lambda c: (c, 0)),
            pl.BlockSpec((1, N, width), lambda c: (c, 0, 0)),
            fixed((N, width)),
        ],
        out_shape=[
            jax.ShapeDtypeStruct((rows, width), jnp.bfloat16),
            jax.ShapeDtypeStruct((rows, width), jnp.bfloat16),
            jax.ShapeDtypeStruct((rows, LANES), f32),
            jax.ShapeDtypeStruct((count, N, width), f32),
            jax.ShapeDtypeStruct((N, width), f32),
        ],
        scratch_shapes=[
            pltpu.VMEM((chunk + 8, width), f32),
            pltpu.VMEM((chunk + 8, 256), f32),
            pltpu.VMEM((3, chunk, LANES), f32),
            pltpu.VMEM((chunk, 2 * width), f32),
            pltpu.VMEM((LANES, chunk), f32),
            pltpu.VMEM((chunk, chunk), f32),
            pltpu.VMEM((chunk, width), f32),
            pltpu.VMEM((chunk, width), f32),
            pltpu.VMEM((chunk, width), f32),
            pltpu.VMEM((LANES, width), jnp.bfloat16),
            pltpu.VMEM((LANES, 2 * width), jnp.bfloat16),
            pltpu.VMEM((chunk, chunk), f32),
        ],
        compiler_params=pltpu.CompilerParams(
            vmem_limit_bytes=VMEM_BYTES, dimension_semantics=("arbitrary",)
        ),
        cost_estimate=pl.CostEstimate(
            flops=rows * width * 1200, bytes_accessed=rows * width * 12, transcendentals=rows * width * 6
        ),
        name="mix_fwd",
    )(proj, proj, proj, proj, halo, halo, meta, segrow, cw, cbc, hp, state)


def conv_back(dpre, taps, masks, here, back, dpad, tail_ref, sl, chunk, acc_ref):
    acc_ref[4:5, sl] += jnp.sum(dpre, axis=0, keepdims=True)
    acc_ref[3:4, sl] += jnp.sum(dpre * here, axis=0, keepdims=True)
    grad = taps[3:4, :] * dpre
    for m in (1, 2, 3):
        acc_ref[3 - m : 4 - m, sl] += jnp.sum(dpre * back[m - 1], axis=0, keepdims=True)
        masked = dpre * masks[m - 1]
        dpad[m - 1, 0:chunk, :] = masked
        dpad[m - 1, chunk : chunk + 8, :] = tail_ref[m - 1, :, sl]
        tail_ref[m - 1, :, sl] = masked[0:8, :]
        grad = grad + taps[3 - m : 4 - m, :] * dpad[m - 1, m : m + chunk, :]
    return grad


def backward_kernel(
    gate_ref, x_ref, bc_ref, st_ref, px_ref, pbc_ref, hx_ref, hbc_ref, meta_ref, segrow_ref, cw_ref, cbc_ref, hp_ref,
    mix_ref, u_ref, fs_ref, states_ref, ds0_ref, tx0_ref, tbc0_ref,
    gproj_ref, n2_ref, acc_ref, accbc_ref, acch_ref, ds_ref, tx_ref, tbc_ref,
    xpad, bpad, masks, cumb_ref, cumt_ref, mask_ref, sexp, eexp, dexp, wide_ref, tall_ref, g_ref,
    dg_ref, db_ref, dc_ref, dcum_ref, dsx_ref, dpad, fac_ref, sb_ref,
):
    chunk, width = x_ref.shape
    step = pl.program_id(0)
    first = step == pl.num_programs(0) - 1

    @pl.when(step == 0)
    def _():
        ds_ref[...] = ds0_ref[...]
        tx_ref[...] = tx0_ref[...]
        tbc_ref[...] = tbc0_ref[...]
        acc_ref[...] = jnp.zeros_like(acc_ref)
        accbc_ref[...] = jnp.zeros_like(accbc_ref)
        acch_ref[...] = jnp.zeros_like(acch_ref)
        wide_ref[...] = spread(width, HEAD)
        tall_ref[...] = spread(width * 2, LANES)

    @pl.when(first)
    def _():
        xpad[0:8, :] = hx_ref[8:16, :].astype(jnp.float32)
        bpad[0:8, :] = hbc_ref[8:16, :].astype(jnp.float32)

    @pl.when(jnp.logical_not(first))
    def _():
        xpad[0:8, :] = px_ref[8:16, :].astype(jnp.float32)
        bpad[0:8, :] = pbc_ref[8:16, :].astype(jnp.float32)

    xpad[8 : 8 + chunk, :] = x_ref[...].astype(jnp.float32)
    bpad[8 : 8 + chunk, :] = bc_ref[...].astype(jnp.float32)
    raw, steps, cum, e, decay = chunk_setup(
        st_ref, meta_ref, segrow_ref, hp_ref, chunk, cumb_ref, cumt_ref, mask_ref, wide_ref, tall_ref
    )
    for m in range(3):
        masks[m] = jnp.broadcast_to(meta_ref[:, m : m + 1], (chunk, LANES))
    fac_ref[...] = jnp.broadcast_to(fs_ref[:, 0:1], (chunk, LANES))
    sb_ref[...] = jnp.broadcast_to(fs_ref[:, 1:2], (chunk, LANES))
    sexp[...] = dot(pack3(steps), wide_ref[...])
    eexp[...] = dot(pack3(e), wide_ref[...])
    dexp[...] = dot(pack3(decay), wide_ref[...])
    bcact, bcpre = [], []
    for half in range(2):
        sl = slice(half * LANES, (half + 1) * LANES)
        pre, back, here = conv_parts(bpad, sl, chunk, cbc_ref[:, sl], masks)
        bcact.append((pre * sigmoid(pre)).astype(jnp.bfloat16))
    bmat, cmat = bcact
    g_ref[...] = dot_nt(cmat, bmat)
    low_lane = lax.broadcasted_iota(jnp.int32, (chunk, LANES), 1) < HEAD
    last_row = lax.broadcasted_iota(jnp.int32, (chunk, LANES), 0) == chunk - 1
    dg_ref[...] = jnp.zeros_like(dg_ref)
    db_ref[...] = jnp.zeros_like(db_ref)
    dc_ref[...] = jnp.zeros_like(dc_ref)
    dcum_ref[...] = jnp.zeros_like(dcum_ref)
    dsx_ref[...] = jnp.zeros_like(dsx_ref)

    def pair(p, carry):
        start = pl.multiple_of(p * LANES, LANES)
        sl = pl.ds(start, LANES)
        cw = cw_ref[:, sl]
        gz = gate_ref[:, sl].astype(jnp.float32)
        sg = sigmoid(gz)
        active = gz * sg
        mixval = mix_ref[:, sl].astype(jnp.float32)
        gated = mixval * active
        fac = fac_ref[...]
        up = u_ref[:, sl].astype(jnp.float32) * fac
        dgated = up * cw[6:7, :] - gated * sb_ref[...]
        gm = (dgated * active).astype(jnp.bfloat16)
        gproj_ref[:, sl] = (dgated * mixval * sg * (1.0 + gz * (1.0 - sg))).astype(jnp.bfloat16)
        n2_ref[:, sl] = (gated * fac * cw[6:7, :]).astype(jnp.bfloat16)
        acc_ref[6:7, sl] += jnp.sum(gated * up, axis=0, keepdims=True)
        dy = gm.astype(jnp.float32)
        pre, back, here = conv_parts(xpad, sl, chunk, cw, masks)
        sig = sigmoid(pre)
        xact = pre * sig
        sx = sexp[:, sl]
        xs = (xact * sx).astype(jnp.bfloat16)
        xsf = xs.astype(jnp.float32)
        ys, dxs = [], []
        for k in range(2):
            h = 2 * p + k
            cumb = cumb_ref[:, pl.ds(pl.multiple_of(h * LANES, LANES), LANES)]
            cumb = jnp.concatenate([cumb] * (chunk // LANES), axis=1)
            decays = jnp.exp(cumb - cumt_ref[pl.ds(h, 1), :] + mask_ref[...])
            weights = (g_ref[...] * decays).astype(jnp.bfloat16)
            own = low_lane if k == 0 else jnp.logical_not(low_lane)
            pulls = dot_nt(jnp.where(own, dy, 0.0).astype(jnp.bfloat16), xs)
            dg_ref[...] += pulls * decays
            ys.append(dot(weights, xs))
            dxs.append(dot_tn(weights, gm))
        inner = jnp.where(low_lane, ys[0], ys[1])
        dinner = jnp.where(low_lane, dxs[0], dxs[1])
        state = states_ref[0, :, sl]
        stateb = state.astype(jnp.bfloat16)
        dstate = ds_ref[:, sl]
        dstateb = dstate.astype(jnp.bfloat16)
        into = eexp[:, sl]
        dec = dexp[:, sl]
        carried = dot(cmat, stateb) * into
        edy = (dy * into).astype(jnp.bfloat16)
        dc_ref[...] += dot_nt(edy, stateb)
        bds = dot(bmat, dstateb) * dec
        db_ref[...] += dot_nt((xsf * dec).astype(jnp.bfloat16), dstateb)
        tails = xsf * bds
        ends = jnp.sum(tails, axis=0, keepdims=True) + into[chunk - 1 : chunk, :] * jnp.sum(
            dstate * state, axis=0, keepdims=True
        )
        rowq = dy * (inner + carried) - xsf * dinner - tails + jnp.where(last_row, ends, 0.0)
        dxsum = dinner + bds
        row = lax.broadcasted_iota(jnp.int32, (LANES, LANES), 0)
        col = lax.broadcasted_iota(jnp.int32, (LANES, LANES), 1)
        gather = (col == 2 * p + row // HEAD).astype(jnp.bfloat16)
        hi, mid, lo = split3(rowq)
        dcum_ref[...] += dot(hi, gather) + dot(mid, gather) + dot(lo, gather)
        hi, mid, lo = split3(xact * dxsum)
        dsx_ref[...] += dot(hi, gather) + dot(mid, gather)
        ds_ref[:, sl] = dstate * into[chunk - 1 : chunk, :] + dot_tn(cmat, edy)
        acc_ref[5:6, sl] += jnp.sum(dy * xact, axis=0, keepdims=True)
        dact = sx * dxsum + cw[5:6, :] * dy
        dpre = dact * (sig * (1.0 + pre * (1.0 - sig)))
        grad = conv_back(dpre, cw, masks, here, back, dpad, tx_ref, sl, chunk, acc_ref)
        gproj_ref[:, pl.ds(pl.multiple_of(width + start, LANES), LANES)] = grad.astype(jnp.bfloat16)
        return carry

    lax.fori_loop(0, width // LANES, pair, 0)
    dgb = dg_ref[...].astype(jnp.bfloat16)
    grads = (db_ref[...] + dot_tn(dgb, cmat), dc_ref[...] + dot(dgb, bmat))
    for half in range(2):
        sl = slice(half * LANES, (half + 1) * LANES)
        cw = cbc_ref[:, sl]
        pre, back, here = conv_parts(bpad, sl, chunk, cw, masks)
        sig = sigmoid(pre)
        dpre = grads[half] * (sig * (1.0 + pre * (1.0 - sig)))
        grad = conv_back(dpre, cw, masks, here, back, dpad, tbc_ref, sl, chunk, accbc_ref)
        at = 2 * width + half * LANES
        gproj_ref[:, at : at + LANES] = grad.astype(jnp.bfloat16)
    row = lax.broadcasted_iota(jnp.int32, (chunk, chunk), 0)
    col = lax.broadcasted_iota(jnp.int32, (chunk, chunk), 1)
    upper = (col >= row).astype(jnp.bfloat16)
    dlogs = exact_left(upper, dcum_ref[...])
    dsteps = dsx_ref[...] + dlogs * hp_ref[1:2, :]
    draw = dsteps * sigmoid(raw)
    gproj_ref[:, 2 * width + 256 :] = draw.astype(jnp.bfloat16)
    acch_ref[0:1, :] += jnp.sum(draw, axis=0, keepdims=True)
    acch_ref[1:2, :] += jnp.sum(dlogs * steps, axis=0, keepdims=True)


def mixer_backward(proj, halo, meta, segrow, cw, cbc, hp, mix, up, fs, states, dstate, tx, tbc, chunk=CHUNK):
    rows, cols = proj.shape
    width = cw.shape[1]
    count = rows // chunk
    back = lambda c: count - 1 - c
    bc_at = 2 * width // 256
    f32 = jnp.float32
    per = chunk // 16
    before = lambda c: jnp.maximum(back(c) * per - 1, 0)
    return pl.pallas_call(
        backward_kernel,
        grid=(count,),
        in_specs=common_specs(chunk, width, back)
        + [
            pl.BlockSpec((16, width), lambda c: (before(c), 1)),
            pl.BlockSpec((16, 256), lambda c: (before(c), bc_at)),
            pl.BlockSpec((16, width), lambda c: (0, 1)),
            pl.BlockSpec((16, 256), lambda c: (0, bc_at)),
            pl.BlockSpec((chunk, 8), lambda c: (back(c), 0)),
            pl.BlockSpec((1, 1, chunk), lambda c: (back(c), 0, 0)),
            fixed((8, width)),
            fixed((8, 256)),
            fixed((8, LANES)),
            pl.BlockSpec((chunk, width), lambda c: (back(c), 0)),
            pl.BlockSpec((chunk, width), lambda c: (back(c), 0)),
            pl.BlockSpec((chunk, 8), lambda c: (back(c), 0)),
            pl.BlockSpec((1, N, width), lambda c: (back(c), 0, 0)),
            fixed((N, width)),
            fixed((3, 8, width)),
            fixed((3, 8, 256)),
        ],
        out_specs=[
            pl.BlockSpec((chunk, cols), lambda c: (back(c), 0)),
            pl.BlockSpec((chunk, width), lambda c: (back(c), 0)),
            fixed((8, width)),
            fixed((8, 256)),
            fixed((8, LANES)),
            fixed((N, width)),
            fixed((3, 8, width)),
            fixed((3, 8, 256)),
        ],
        out_shape=[
            jax.ShapeDtypeStruct((rows, cols), jnp.bfloat16),
            jax.ShapeDtypeStruct((rows, width), jnp.bfloat16),
            jax.ShapeDtypeStruct((8, width), f32),
            jax.ShapeDtypeStruct((8, 256), f32),
            jax.ShapeDtypeStruct((8, LANES), f32),
            jax.ShapeDtypeStruct((N, width), f32),
            jax.ShapeDtypeStruct((3, 8, width), f32),
            jax.ShapeDtypeStruct((3, 8, 256), f32),
        ],
        scratch_shapes=[
            pltpu.VMEM((chunk + 8, width), f32),
            pltpu.VMEM((chunk + 8, 256), f32),
            pltpu.VMEM((3, chunk, LANES), f32),
            pltpu.VMEM((chunk, 2 * width), f32),
            pltpu.VMEM((LANES, chunk), f32),
            pltpu.VMEM((chunk, chunk), f32),
            pltpu.VMEM((chunk, width), f32),
            pltpu.VMEM((chunk, width), f32),
            pltpu.VMEM((chunk, width), f32),
            pltpu.VMEM((LANES, width), jnp.bfloat16),
            pltpu.VMEM((LANES, 2 * width), jnp.bfloat16),
            pltpu.VMEM((chunk, chunk), f32),
            pltpu.VMEM((chunk, chunk), f32),
            pltpu.VMEM((chunk, N), f32),
            pltpu.VMEM((chunk, N), f32),
            pltpu.VMEM((chunk, LANES), f32),
            pltpu.VMEM((chunk, LANES), f32),
            pltpu.VMEM((3, chunk + 8, LANES), f32),
            pltpu.VMEM((chunk, LANES), f32),
            pltpu.VMEM((chunk, LANES), f32),
        ],
        compiler_params=pltpu.CompilerParams(
            vmem_limit_bytes=VMEM_BYTES, dimension_semantics=("arbitrary",)
        ),
        cost_estimate=pl.CostEstimate(
            flops=rows * width * 4000, bytes_accessed=rows * width * 24, transcendentals=rows * width * 8
        ),
        name="mix_bwd",
    )(
        proj, proj, proj, proj, proj, proj, halo, halo, meta, segrow, cw, cbc, hp,
        mix, up, fs, states, dstate, tx, tbc,
    )


def token_facts(seg, chunk=CHUNK):
    total = seg.shape[0]
    place = jnp.arange(total, dtype=jnp.int32)
    cols = []
    for m in (1, 2, 3):
        before = jnp.concatenate([jnp.full((m,), -1, jnp.int32), seg[:-m]])
        cols.append(before == seg)
    ends = seg.reshape(-1, chunk)[:, -1]
    starts = jnp.concatenate([jnp.full((1,), -1, jnp.int32), ends[:-1]])
    cols.append(jnp.repeat(starts, chunk) == seg)
    cols.append(jnp.repeat(ends, chunk) == seg)
    meta = jnp.stack([c.astype(jnp.float32) for c in cols] + [seg.astype(jnp.float32)], axis=1)
    meta = jnp.pad(meta, ((0, 0), (0, 2)))
    return meta, seg.astype(jnp.float32).reshape(-1, 1, chunk)


def team_sizes():
    return lax.axis_size("x"), 2 * lax.axis_size("x")


def in_order(first, mine, theirs):
    return jnp.stack([jnp.where(first, mine, theirs), jnp.where(first, theirs, mine)])


def team_gather(own):
    across = lax.axis_size("x")
    if across == 2:
        row = in_order(lax.axis_index("x") == 0, own, lax.ppermute(own, "x", SWAP))
    else:
        row = lax.all_gather(own, "x", axis=0)
    both = in_order(lax.axis_index("core") == 0, row, lax.ppermute(row, "core", SWAP))
    return both.reshape((2 * across,) + own.shape)


def team_reduce(parts, kind):
    across = lax.axis_size("x")
    core = lax.axis_index("core")
    halves = parts.reshape((2, across) + parts.shape[1:])
    keep = lax.dynamic_index_in_dim(halves, core, 0, False)
    got = lax.ppermute(lax.dynamic_index_in_dim(halves, 1 - core, 0, False), "core", SWAP)
    if across == 2:
        place = lax.axis_index("x")

        def added(at):
            return lax.dynamic_index_in_dim(keep, at, 0, False).astype(jnp.float32) + (
                lax.dynamic_index_in_dim(got, at, 0, False).astype(jnp.float32)
            )

        far = lax.ppermute(added(1 - place).astype(kind), "x", SWAP)
        return added(place) + far.astype(jnp.float32)
    sums = (keep.astype(jnp.float32) + got.astype(jnp.float32)).astype(kind)
    return lax.psum_scatter(sums, "x", scatter_dimension=0, tiled=False).astype(jnp.float32)


def deal_moves():
    moves = []
    for r in range(2):
        pairs = []
        for core in range(2):
            for z in range(DEPTH):
                pairs.append((core * DEPTH + z, (z // 2) * DEPTH + 2 * core + ((z % 2) ^ r)))
        moves.append(pairs)
    return moves


def to_team(rows):
    low = lax.axis_index("z") % 2
    got = []
    for r, pairs in enumerate(deal_moves()):
        block = lax.dynamic_index_in_dim(rows, low ^ r, 0, False)
        got.append(lax.ppermute(block, ("core", "z"), pairs))
    return in_order(low == 0, got[0], got[1]).reshape(-1, rows.shape[2])


def from_team(rows):
    low = lax.axis_index("z") % 2
    blocks = rows.reshape(2, -1, rows.shape[1])
    got = []
    for r, pairs in enumerate(deal_moves()):
        block = lax.dynamic_index_in_dim(blocks, low ^ r, 0, False)
        got.append(lax.ppermute(block, ("core", "z"), [(b, a) for a, b in pairs]))
    return in_order(low == 0, got[0], got[1])


def inverse_of(perm):
    count = perm.shape[0]
    places = jnp.arange(count, dtype=jnp.int32)
    return jnp.sum(jnp.where(places[:, None] == perm[None, :], places[None, :], 0), axis=1)


def segments_of(sizes, total):
    ends = jnp.cumsum(sizes)
    places = jnp.arange(total, dtype=jnp.int32)
    return jnp.sum((places[:, None] >= ends[None, :]).astype(jnp.int32), axis=1)


def natural_rows(gathered):
    total, cols = gathered.shape
    view = gathered.reshape(lax.axis_size("y"), DEPTH, 2, -1, cols)
    return view.transpose(0, 2, 1, 3, 4).reshape(total, cols)


def plane_rows(natural):
    total, cols = natural.shape
    view = natural.reshape(lax.axis_size("y"), 2, DEPTH, -1, cols)
    return view.transpose(0, 2, 1, 3, 4).reshape(total, cols)


def to_heads(pieces):
    sent = lax.all_to_all(pieces, ("core", "x"), split_axis=1, concat_axis=0, tiled=True)
    sent = sent.reshape(-1, pieces.shape[2])
    return natural_rows(lax.all_gather(sent, ("y", "z"), axis=0, tiled=True))


def from_heads(grads):
    cols = grads.shape[1]
    team = 2 * lax.axis_size("x")
    summed = lax.psum_scatter(plane_rows(grads), ("y", "z"), scatter_dimension=0, tiled=True)
    back = lax.all_to_all(
        summed.reshape(team, -1, cols), ("core", "x"), split_axis=0, concat_axis=0, tiled=True
    )
    return back.transpose(1, 0, 2)


def in_columns(w_in, team):
    rows = w_in.shape[0]
    bc = w_in[:, 2 * DI : 2 * DI + 2 * N]
    step = w_in[:, 2 * DI + 2 * N :].reshape(rows, team, -1)
    return jnp.concatenate(
        [
            w_in[:, :DI].reshape(rows, team, -1),
            w_in[:, DI : 2 * DI].reshape(rows, team, -1),
            jnp.broadcast_to(bc[:, None, :], (rows, team, 2 * N)),
            step,
            jnp.zeros((rows, team, LANES - step.shape[2]), w_in.dtype),
        ],
        axis=2,
    )


def row_scale(rows):
    return lax.rsqrt(jnp.mean(rows * rows, axis=1, keepdims=True) + EPS)


def per_device(
    hidden,
    lengths,
    token_order,
    norm_gain,
    in_weight,
    conv_weight,
    conv_bias,
    dt_bias,
    log_decay,
    skip_gain,
    gate_gain,
    out_weight,
    cotangent,
):
    bf16, f32 = jnp.bfloat16, jnp.float32
    layers = in_weight.shape[0]
    across, team = team_sizes()
    core, z, x = (lax.axis_index(name) for name in ("core", "z", "x"))
    member = core * across + x
    width = DI // team
    heads = width // HEAD
    rows_here = hidden.shape[1]
    tokens = token_order.shape[2]
    part_rows = tokens // PARTS
    own_rows = part_rows // team

    def of_pair(ints):
        other = lax.ppermute(ints, "core", SWAP)
        return lax.dynamic_index_in_dim(jnp.where(z // 2 == core, ints, other), z % 2, 0, False)[0]

    order, sizes = of_pair(token_order), of_pair(lengths)
    inverse = inverse_of(order)
    block, within = inverse // rows_here, inverse % rows_here
    from_z, from_x = block // across, block % across
    place = ((from_z // 2 * across + from_x) * 2 + from_z % 2) * rows_here + within
    own_block = (2 * core + jnp.arange(2, dtype=jnp.int32)) * across + x
    own_dealt = (own_block[:, None] * rows_here + jnp.arange(rows_here, dtype=jnp.int32)).reshape(-1)
    meta, segrow = token_facts(segments_of(sizes, tokens))

    w_cols = [to_heads(in_columns(in_weight[layer], team)) for layer in range(layers)]
    w_out = [
        to_heads(out_weight[layer].T.reshape(-1, team, width)) for layer in range(layers)
    ]
    flat = jnp.concatenate(
        [conv_weight.reshape(layers, -1), conv_bias, norm_gain, gate_gain], axis=1
    )
    wide = conv_bias.shape[1]
    full = lax.all_gather(flat, ("y", "core", "z", "x"), axis=0).transpose(1, 0, 2)
    cuts = [CONV * wide, (CONV + 1) * wide, (CONV + 1) * wide + norm_gain.shape[1]]
    taps, shift, ngain, ggain = jnp.split(full.astype(f32), cuts, axis=2)
    taps = taps.reshape(layers, -1, CONV, wide).transpose(0, 2, 1, 3).reshape(layers, CONV, -1)
    shift, ngain, ggain = (v.reshape(layers, -1) for v in (shift, ngain, ggain))
    per_head = lax.all_gather(
        jnp.stack([dt_bias, log_decay, skip_gain]), ("z", "x"), axis=2, tiled=True
    )
    own_heads = lax.dynamic_slice_in_dim(per_head, member * heads, heads, 2)

    def mine(values):
        return lax.dynamic_slice_in_dim(values, member * width, width, values.ndim - 1)

    tables = []
    for layer in range(layers):
        cw = jnp.concatenate(
            [
                mine(taps[layer, :, :DI]),
                mine(shift[layer, None, :DI]),
                jnp.repeat(own_heads[2, layer], HEAD)[None],
                mine(ggain[layer, None]),
                jnp.zeros((1, width), f32),
            ]
        )
        cbc = jnp.concatenate(
            [taps[layer, :, DI:], shift[layer, None, DI:], jnp.zeros((3, 2 * N), f32)]
        )
        hp = jnp.stack([own_heads[0, layer], -jnp.exp(own_heads[1, layer])])
        tables.append((cw, cbc, jnp.pad(hp, ((0, 6), (0, LANES - heads)))))

    def packed(rows):
        gathered = team_gather(to_team(rows)).reshape(tokens, -1)
        return gathered[place]

    def part(values, i):
        return values[i * part_rows : (i + 1) * part_rows]

    def own_of(values):
        return lax.dynamic_slice_in_dim(values, member * own_rows, own_rows, 0)

    def facts(i):
        count = part_rows // CHUNK
        return part(meta, i), segrow[i * count : (i + 1) * count]

    everything = packed(hidden)
    states = [own_of(part(everything, i)).astype(f32) for i in range(PARTS)]
    record = []
    no_halo = jnp.zeros((16, 2 * width + 2 * N + LANES), bf16)
    for layer in range(layers):
        kept = []
        state = jnp.zeros((N, width), f32)
        halo = no_halo
        for i in range(PARTS):
            rows = states[i]
            if layer == 0:
                every = part(everything, i).astype(f32)
                normed = (every * row_scale(every) * ngain[layer]).astype(bf16)
            else:
                normed = (rows * row_scale(rows) * ngain[layer]).astype(bf16)
                normed = team_gather(normed).reshape(part_rows, -1)
            proj = jnp.dot(normed, w_cols[layer], preferred_element_type=f32).astype(bf16)
            mix, gated, squares, starts, state = mixer_forward(
                proj, halo, *facts(i), *tables[layer], state
            )
            partial = dot_nt(gated, w_out[layer]).astype(bf16)
            branch = team_reduce(partial.reshape(team, own_rows, -1), bf16)
            total = team_reduce(jnp.sum(squares, axis=1).reshape(team, own_rows), f32)
            factor = lax.rsqrt(total / DI + EPS)
            states[i] = rows + branch * factor[:, None]
            kept.append((rows, normed, proj, halo, mix, starts, branch.astype(bf16), factor))
            halo = proj[part_rows - 16 :]
        record.append(kept)

    def dealt(parts):
        whole = [team_gather(p.astype(bf16)).reshape(part_rows, -1) for p in parts]
        whole = jnp.concatenate(whole) if PARTS > 1 else whole[0]
        return from_team(whole[order[own_dealt]])

    block_out = dealt(states)
    gout_whole = packed(cotangent)
    grads_rows = [own_of(part(gout_whole, i)).astype(f32) for i in range(PARTS)]
    results = [None] * layers
    small = [None] * layers
    for layer in reversed(range(layers)):
        dstate = jnp.zeros((N, width), f32)
        tail_x = jnp.zeros((3, 8, width), f32)
        tail_bc = jnp.zeros((3, 8, 2 * N), f32)
        gathered, sums = [None] * PARTS, None
        for i in reversed(range(PARTS)):
            rows, normed, proj, halo, mix, starts, branch, factor = record[layer][i]
            gout = grads_rows[i].astype(bf16)
            inner = jnp.sum(gout.astype(f32) * branch.astype(f32), axis=1)
            scales = jnp.stack([factor, factor * factor * factor * inner / DI])
            scales = team_gather(scales).transpose(0, 2, 1).reshape(part_rows, 2)
            if layer == layers - 1:
                gout_all = part(gout_whole, i)
            else:
                gout_all = team_gather(gout).reshape(part_rows, -1)
            up = jnp.dot(gout_all, w_out[layer], preferred_element_type=f32).astype(bf16)
            gproj, normed2, acc, acc_bc, acc_h, dstate, tail_x, tail_bc = mixer_backward(
                proj,
                halo,
                *facts(i),
                *tables[layer],
                mix,
                up,
                jnp.pad(scales, ((0, 0), (0, 6))),
                starts,
                dstate,
                tail_x,
                tail_bc,
            )
            partial = dot_nt(gproj, w_cols[layer]).astype(bf16)
            gnormed = team_reduce(partial.reshape(team, own_rows, -1), bf16)
            scale = row_scale(rows)
            pulled = gnormed * ngain[layer]
            back = jnp.mean(pulled * rows, axis=1, keepdims=True)
            grads_rows[i] = grads_rows[i] + scale * pulled - rows * (scale * scale * scale * back)
            gathered[i] = (normed, gproj, gout_all, normed2)
            found = (acc, acc_bc, acc_h)
            sums = found if sums is None else tuple(a + b for a, b in zip(sums, found))
        if PARTS > 1:
            whole = [jnp.concatenate([g[k] for g in gathered]) for k in range(4)]
        else:
            whole = gathered[0]
        grad_out = from_heads(dot_tn(whole[2], whole[3]).astype(bf16))
        split = from_heads(dot_tn(whole[0], whole[1]).astype(bf16)).astype(f32)
        count = split.shape[0]
        bc_at = 2 * width
        step_at = bc_at + 2 * N
        grad_in = jnp.concatenate(
            [
                split[:, :, :width].reshape(count, DI),
                split[:, :, width:bc_at].reshape(count, DI),
                jnp.sum(split[:, :, bc_at:step_at], axis=1),
                split[:, :, step_at : step_at + heads].reshape(count, team * heads),
            ],
            axis=1,
        )
        grad_norm = jnp.sum(grad_in * in_weight[layer].astype(f32), axis=1) / (
            norm_gain[layer].astype(f32)
        )
        results[layer] = (grad_norm, grad_in, grad_out.astype(f32).reshape(count, DI).T)
        acc, acc_bc, acc_h = sums
        taps_full = jnp.zeros((CONV + 1, DI + 2 * N), f32)
        taps_full = lax.dynamic_update_slice(taps_full, acc[: CONV + 1], (0, member * width))
        taps_full = lax.dynamic_update_slice(taps_full, acc_bc[: CONV + 1], (0, DI))
        gate_full = lax.dynamic_update_slice(jnp.zeros((DI,), f32), acc[6], (member * width,))
        spread_out = jnp.concatenate(
            [
                taps_full.reshape(CONV + 1, -1, wide).transpose(1, 0, 2).reshape(-1, (CONV + 1) * wide),
                gate_full.reshape(-1, gate_gain.shape[1]),
            ],
            axis=1,
        )
        head_sums = jnp.stack(
            [
                acc_h[0, :heads],
                acc_h[1, :heads] * tables[layer][2][1, :heads],
                jnp.sum(acc[5].reshape(heads, HEAD), axis=1),
            ]
        )
        head_full = lax.dynamic_update_slice(
            jnp.zeros((3, team * heads), f32), head_sums, (0, member * heads)
        )
        small[layer] = (spread_out, head_full)
    grad_hidden = dealt(grads_rows).astype(f32)
    every_axis = ("y", "core", "z", "x")
    spread_sum = lax.psum_scatter(
        jnp.stack([s[0] for s in small], axis=1), every_axis, scatter_dimension=0, tiled=False
    )
    head_sum = lax.psum(jnp.stack([s[1] for s in small]), every_axis)
    here = dt_bias.shape[1]
    head_own = lax.dynamic_slice_in_dim(head_sum, (z * across + x) * here, here, 2)
    grad_taps = spread_sum[:, : CONV * wide].reshape(layers, CONV, wide)
    return (
        block_out,
        grad_hidden,
        jnp.stack([r[0] for r in results]),
        jnp.stack([r[1] for r in results]),
        grad_taps,
        spread_sum[:, CONV * wide : (CONV + 1) * wide],
        head_own[:, 0],
        head_own[:, 1],
        head_own[:, 2],
        spread_sum[:, (CONV + 1) * wide :],
        jnp.stack([r[2] for r in results]),
    )


def solution(mesh):
    grid = mesh.devices.reshape(mesh.shape["dp"] // 2, 2, DEPTH, mesh.shape["seq"] // DEPTH)
    fine = Mesh(grid, ("y", "core", "z", "x"))
    dp, seq = ("y", "core"), ("z", "x")
    both = dp + seq
    return jax.shard_map(
        per_device,
        mesh=fine,
        in_specs=(
            P(None, both, None),
            P(None, dp, None),
            P(None, dp, None),
            P(None, both),
            P(None, both, None),
            P(None, None, both),
            P(None, both),
            P(None, seq),
            P(None, seq),
            P(None, seq),
            P(None, both),
            P(None, None, both),
            P(None, both, None),
        ),
        out_specs=(
            P(None, both, None),
            P(None, both, None),
            P(None, both),
            P(None, both, None),
            P(None, None, both),
            P(None, both),
            P(None, seq),
            P(None, seq),
            P(None, seq),
            P(None, both),
            P(None, None, both),
        ),
        check_vma=False,
    )
```

time: 6390 us -> 1930 us (0.30)
  waiting for transfers between devices: 2860 us -> 556 us
  matrix products: 1160 us -> 242 us
  local copies, waits for them, and re-layouts: 994 us -> 216 us
  other arithmetic: 541 us -> 187 us
  blocking collectives: 656 us -> 334 us
  Pallas kernels: 0 us -> 279 us
  loops' own time: 93.4 us -> 0 us
    reduce_scatter x16 -> x4, waiting for transfers between devices: 2140 us -> 166 us  [from_heads(): lax.psum_scatter(plane_rows(grads), ('y', 'z'), scatter_dimension=0, tile...]
    dot_general x644 -> x12, matrix products: 1160 us -> 242 us  [the longest x4 82.5 us: dot_tn(): lax.dot_general(a, b, (((0,), (0,)), ((), ())), preferred_element_type=jn...]
    all_gather x16 -> x4, waiting for transfers between devices: 501 us -> 0.03 us  [to_heads(): return natural_rows(lax.all_gather(sent, ('y', 'z'), axis=0, tiled=True))]
    ppermute x0 -> x38, waiting for transfers between devices: none -> 378 us  [the longest x8 182 us: team_gather(): row = in_order(lax.axis_index('x') == 0, own, lax.ppermute(own, 'x', SWAP))]
    pallas_call x0 -> x4, Pallas kernels: none -> 279 us  [the longest x2 190 us: mixer_backward(): pl.pallas_call(backward_kernel, grid=(count,), in_specs=common_specs(chun...]
    gather x52 -> x5, local copies, waits for them, and re-layouts: 330 us -> 63.5 us  [the longest x2 41.6 us: packed(): return gathered[place]]
    mul x362 -> x2, other arithmetic: 222 us -> 0.02 us  [the longest x1 0.01 us: per_device(): scale * scale * scale * back]
    unnamed x36 -> x10, waiting for transfers between devices: 178 us -> 0.81 us
  transfers between devices with their start and end apart: 39 -> 53, of which waited for: 22 -> 22; matrix products, arithmetic and copies ran while one was open for 25% -> 28% of each run, Pallas kernels for 0% -> 10%
where the time goes in v1:
time: 1930 us; the launch traced here: 1920 us
  waiting for transfers between devices  556 us (29%)
  blocking collectives  334 us (17%)
  Pallas kernels  279 us (14%)
  matrix products  242 us (13%)
  local copies, waits for them, and re-layouts  216 us (11%)
  other arithmetic  187 us (10%)
  starting transfers between devices  89.6 us (5%)
    pallas_call x2, Pallas kernels, mixer_backward(): pl.pallas_call(backward_kernel, grid=(count,), in_specs=common_specs(chun...  190 us
    ppermute x8, waiting for transfers between devices, team_gather(): row = in_order(lax.axis_index('x') == 0, own, lax.ppermute(own, 'x', SWAP))  182 us
    reduce_scatter x4, waiting for transfers between devices, from_heads(): lax.psum_scatter(plane_rows(grads), ('y', 'z'), scatter_dimension=0, tile...  166 us
    ppermute x6, waiting for transfers between devices, team_reduce(): far = lax.ppermute(added(1 - place).astype(kind), 'x', SWAP)  136 us
    all_gather x1, blocking collectives, per_device(): lax.all_gather(flat, ('y', 'core', 'z', 'x'), axis=0).transpose(1, 0, 2)  129 us
    another operation x39, other arithmetic, in_order(): jnp.stack([jnp.where(first, mine, theirs), jnp.where(first, theirs, mine)])  113 us
    psum x1, blocking collectives, per_device(): head_sum = lax.psum(jnp.stack([s[1] for s in small]), every_axis)  93.3 us
    pallas_call x2, Pallas kernels, mixer_forward(): pl.pallas_call(forward_kernel, grid=(count,), in_specs=common_specs(chunk...  89.3 us
  transfers between devices with their start and end apart: 53, of which 22 were waited for; matrix products, arithmetic and copies ran while one was open for 28% of the time, Pallas kernels for 10%

profile of v1, /device:TPU:0, one launch (start us, length us, event | category | flops | bytes accessed | tf_op | source)
XLA Modules:
  0.0 1920.5 jit_solution(1967527524615230467)
XLA Ops:
  9.4 13.0 all_to_all.80
  35.2 19.7 %all_to_all.81 = bf16[64,4,2432]{2,0,1:T(8,128)(2,1)} all-to-all(bf16[64,4,2432]{2,0,1:T(8,128)(2,1)S(1)} %concatenate.55), channel_id=1, replica_groups=mesh['y'=2,'core'=2,'z'=4,'x'=2] {'core','x'}, dimensions={1} | all-to-all | bytes 2490368 | tf_op jit(solution)/shard_map/all_to_all | solution.py:601
  58.2 9.5 collective-permute-start
  85.4 129.4 %all-gather.1 = bf16[32,2,872]{2,1,0:T(2,128)(2,1)S(1)} all-gather(bf16[1,2,872]{2,1,0:T(2,128)(2,1)S(1)} %maximum_bitcast_fusion.2), channel_id=2, replica_groups=mesh['y'=2,'core'=2,'z'=4,'x'=2] {'y','core','z','x'}, dimensions={0}, use_global_device_ids=true | all-gather | bytes 115104 | tf_op jit(solution)/shard_map/all_gather | solution.py:684
  226.1 78.9 %all_gather.24 = f32[3,2,64]{0,1,2:T(2,128)S(1)} all-gather(f32[3,2,8]{0,1,2:T(2,128)S(1)} %copy.208), channel_id=1, replica_groups=mesh['y'=2,'core'=2,'z'=4,'x'=2] {'z','x'}, dimensions={2}, use_global_device_ids=true | all-gather | bytes 1728 | tf_op jit(solution)/shard_map/all_gather | solution.py:689
  320.1 5.5 select_bitcast_fusion.11
  325.6 7.6 pad_maximum_fusion.1
  333.1 20.8 %gather_fusion = bf16[2048,2048]{1,0:T(8,128)(2,1)} fusion(bf16[2048,2048]{1,0:T(8,128)(2,1)} %bitcast.433, s32[2048]{0:T(1024)S(1)} %broadcast_clamp_fusion), kind=kCustom, calls=%fused_computation | custom fusion | bytes 16785408 | tf_op jit(solution)/shard_map/gather | solution.py:716
  353.9 5.5 fusion
  364.2 8.7 copy.204
  372.9 29.3 %convolution_convert_fusion.3.gate_ref.x_ref.bc_ref.st_ref.px_ref.pbc_ref = bf16[2048,2432]{1,0:T(8,128)(2,1)} fusion(bf16[2048,2432]{1,0:T(8,128)(2,1)} %bitcast.468, bf16[2048,2048]{1,0:T(8,128)(2,1)} %gather_fusion, f32[2048]{0:T(1024)S(1)} %mul.283, f32[2048]{0:T(1024)S(1)} %add_rsqrt_fusion), kind=kOutput, calls=%fused_computation.15 | convolution fusion | flops 20422852608 | bytes 28327936 | tf_op jit(solution)/shard_map/dot_general | solution.py:744
  402.3 45.3 %mix_fwd.2 = (bf16[2048,1024]{1,0:T(8,128)(2,1)}, bf16[2048,1024]{1,0:T(8,128)(2,1)}, f32[2048,128]{1,0:T(8,128)}, f32[8,128,1024]{2,1,0:T(8,128)}, f32[128,1024]{1,0:T(8,128)}) custom-call(bf16[2048,2432]{1,0:T(8,128)(2,1)} %convolution_convert_fusion.3.gate_ref.x_ref.bc_ref.st_ref.px_ref.pbc_ref, ...), custom_call_target="tpu_custom_call" | custom-call | flops 2516582400 | bytes 25165824 | tf_op jit(solution)/shard_map/mix_fwd/pallas_call | solution.py:189
  447.6 10.7 convolution_convert_fusion.7
  463.4 7.1 collective-permute-done.6
  480.0 43.1 %collective-permute-done.9 = f32[512]{0:T(512)S(1)} collective-permute-done((f32[512]{0:T(512)S(1)}, f32[512]{0:T(512)S(1)}, u32[]{:S(2)}, u32[]{:S(2)}) %collective-permute-start.9) | collective-permute-done | bytes 2080 | tf_op jit(solution)/shard_map/ppermute | solution.py:540
  523.1 5.1 multiply_reduce_fusion.4
  529.0 46.8 %collective-permute-done.10 = bf16[512,2048]{1,0:T(8,128)(2,1)S(1)} collective-permute-done((bf16[512,2048]{1,0:T(8,128)(2,1)S(1)}, bf16[512,2048]{1,0:T(8,128)(2,1)S(1)}, u32[]{:S(2)}, u32[]{:S(2)}) %collective-permute-start.10) | collective-permute-done | bytes 2097184 | tf_op jit(solution)/shard_map/ppermute | solution.py:519
  581.8 9.6 collective-permute-start.20
  593.8 34.4 %collective-permute-done.21 = bf16[256,2048]{1,0:T(8,128)(2,1)} collective-permute-done((bf16[256,2048]{1,0:T(8,128)(2,1)}, bf16[256,2048]{1,0:T(8,128)(2,1)}, u32[]{:S(2)}, u32[]{:S(2)}) %collective-permute-start.21) | collective-permute-done | bytes 1048608 | tf_op jit(solution)/shard_map/ppermute | solution.py:562
  631.8 4.8 copy.218
  636.6 8.4 copy.216
  645.1 5.4 select_bitcast_fusion.9
  650.5 7.5 pad_maximum_fusion.2
  658.0 27.9 %convolution_convert_fusion.2.gate_ref.x_ref.bc_ref.st_ref.px_ref.pbc_ref = bf16[2048,2432]{1,0:T(8,128)(2,1)} fusion(bf16[2048,2048]{1,0:T(8,128)(2,1)} %bitcast.478, bf16[2048,2432]{1,0:T(8,128)(2,1)} %bitcast.472), kind=kOutput, calls=%fused_computation.14 | convolution fusion | flops 20406075392 | bytes 28311552 | tf_op jit(solution)/shard_map/dot_general | solution.py:744
  686.0 43.9 %mix_fwd.3 = (bf16[2048,1024]{1,0:T(8,128)(2,1)}, bf16[2048,1024]{1,0:T(8,128)(2,1)}, f32[2048,128]{1,0:T(8,128)}, f32[8,128,1024]{2,1,0:T(8,128)}, f32[128,1024]{1,0:T(8,128)}) custom-call(bf16[2048,2432]{1,0:T(8,128)(2,1)} %convolution_convert_fusion.2.gate_ref.x_ref.bc_ref.st_ref.px_ref.pbc_ref, ...), custom_call_target="tpu_custom_call" | custom-call | flops 2516582400 | bytes 25165824 | tf_op jit(solution)/shard_map/mix_fwd/pallas_call | solution.py:189
  729.9 10.9 convolution_convert_fusion.6
  759.7 7.5 pad_maximum_fusion.4
  767.2 20.8 %gather_fusion.3 = bf16[2048,2048]{1,0:T(8,128)(2,1)} fusion(bf16[2048,2048]{1,0:T(8,128)(2,1)} %bitcast.432, s32[2048]{0:T(1024)S(1)} %copy-done.46), kind=kCustom, calls=%fused_computation.3 | custom fusion | bytes 16785408 | tf_op jit(solution)/shard_map/gather | solution.py:716
  792.5 7.1 collective-permute-done.13
  807.6 12.4 convolution_convert_fusion.9.u_ref
  823.6 95.1 %mix_bwd.2 = (bf16[2048,2432]{1,0:T(8,128)(2,1)}, bf16[2048,1024]{1,0:T(8,128)(2,1)}, f32[8,1024]{1,0:T(8,128)S(1)}, f32[8,256]{1,0:T(8,128)S(1)}, f32[8,128]{1,...) custom-call(bf16[2048,2432]{1,0:T(8,128)(2,1)} %convolution_convert_fusion.2.gate_ref.x_ref.bc_ref., ...), custom_call_target="tpu_custom_call" | custom-call | flops 8388608000 | bytes 50331648 | tf_op jit(solution)/shard_map/mix_bwd/pallas_call | solution.py:415
  918.7 27.3 %convolution_convert_fusion.5 = bf16[2048,2048]{1,0:T(8,128)(2,1)S(1)} fusion(bf16[2048,2432]{1,0:T(8,128)(2,1)} %get-tuple-element.35, bf16[2048,2432]{1,0:T(8,128)(2,1)} %bitcast.473), kind=kOutput, calls=%fused_computation.24 | convolution fusion | flops 20405288960 | bytes 28311552 | tf_op jit(solution)/shard_map/dot_general | solution.py:32
  952.1 7.0 collective-permute-done.26
  964.6 46.4 %collective-permute-done.27 = bf16[512,2048]{1,0:T(8,128)(2,1)S(1)} collective-permute-done((bf16[512,2048]{1,0:T(8,128)(2,1)S(1)}, bf16[512,2048]{1,0:T(8,128)(2,1)S(1)}, u32[]{:S(2)}, u32[]{:S(2)}) %collective-permute-start.27) | collective-permute-done | bytes 2097184 | tf_op jit(solution)/shard_map/ppermute | solution.py:540
  1014.8 9.1 multiply_reduce_fusion.2
  1025.4 45.8 %collective-permute-done.28 = bf16[512,2048]{1,0:T(8,128)(2,1)S(1)} collective-permute-done((bf16[512,2048]{1,0:T(8,128)(2,1)}, bf16[512,2048]{1,0:T(8,128)(2,1)S(1)}, u32[]{:S(2)}, u32[]{:S(2)}) %collective-permute-start.28) | collective-permute-done | bytes 2097184 | tf_op jit(solution)/shard_map/ppermute | solution.py:519
  1077.6 9.7 convolution_convert_fusion.10
  1099.1 5.7 select_bitcast_fusion.3
  1104.8 7.5 pad_maximum_fusion.5
  1112.2 14.0 convolution_convert_fusion.8.u_ref
  1126.3 94.7 %mix_bwd.3 = (bf16[2048,2432]{1,0:T(8,128)(2,1)}, bf16[2048,1024]{1,0:T(8,128)(2,1)}, f32[8,1024]{1,0:T(8,128)S(1)}, f32[8,256]{1,0:T(8,128)S(1)}, f32[8,128]{1,...) custom-call(bf16[2048,2432]{1,0:T(8,128)(2,1)} %convolution_convert_fusion.3.gate_ref.x_ref.bc_ref., ...), custom_call_target="tpu_custom_call" | custom-call | flops 8388608000 | bytes 50331648 | tf_op jit(solution)/shard_map/mix_bwd/pallas_call | solution.py:415
  1223.7 28.6 %convolution_convert_fusion = bf16[2048,2432]{1,0:T(8,128)(2,1)} fusion(bf16[2048,2048]{1,0:T(8,128)(2,1)} %bitcast.479, bf16[2048,2432]{1,0:T(8,128)(2,1)} %get-tuple-element.35), kind=kOutput, calls=%fused_computation.12 | convolution fusion | flops 20406075392 | bytes 28311552 | tf_op jit(solution)/shard_map/dot_general | solution.py:36
  1252.2 8.6 copy.226
  1260.9 12.7 convolution_convert_fusion.11
  1276.9 31.5 %convolution_convert_fusion.1 = bf16[2048,2432]{1,0:T(8,128)(2,1)} fusion(bf16[2048,2432]{1,0:T(8,128)(2,1)} %get-tuple-element.38, bf16[2048,2048]{1,0:T(8,128)(2,1)} %gather_fusion, f32[2048]{0:T(1024)S(1)} %copy-done.44, f32[2048]{0:T(1024)S(1)} %copy-done.56), kind=kOutput, calls=%fused_computation.13 | convolution fusion | flops 20422852608 | bytes 28327936 | tf_op jit(solution)/shard_map/dot_general | solution.py:36
  1308.4 8.5 copy.221
  1316.9 27.5 %convolution_convert_fusion.4 = bf16[2048,2048]{1,0:T(8,128)(2,1)S(1)} fusion(bf16[2048,2432]{1,0:T(8,128)(2,1)} %get-tuple-element.38, bf16[2048,2432]{1,0:T(8,128)(2,1)} %bitcast.469), kind=kOutput, calls=%fused_computation.23 | convolution fusion | flops 20405288960 | bytes 28311552 | tf_op jit(solution)/shard_map/dot_general | solution.py:32
  1354.6 39.8 %collective-permute-done.16 = bf16[512,2048]{1,0:T(8,128)(2,1)S(1)} collective-permute-done((bf16[512,2048]{1,0:T(8,128)(2,1)S(1)}, bf16[512,2048]{1,0:T(8,128)(2,1)S(1)}, u32[]{:S(2)}, u32[]{:S(2)}) %collective-permute-start.16) | collective-permute-done | bytes 2097184 | tf_op jit(solution)/shard_map/ppermute | solution.py:519
  1398.9 39.8 %collective-permute-done.33 = bf16[512,2048]{1,0:T(8,128)(2,1)S(1)} collective-permute-done((bf16[512,2048]{1,0:T(8,128)(2,1)S(1)}, bf16[512,2048]{1,0:T(8,128)(2,1)S(1)}, u32[]{:S(2)}, u32[]{:S(2)}) %collective-permute-start.33) | collective-permute-done | bytes 2097184 | tf_op jit(solution)/shard_map/ppermute | solution.py:540
  1446.5 45.6 %collective-permute-done.34 = bf16[512,2048]{1,0:T(8,128)(2,1)S(1)} collective-permute-done((bf16[512,2048]{1,0:T(8,128)(2,1)S(1)}, bf16[512,2048]{1,0:T(8,128)(2,1)S(1)}, u32[]{:S(2)}, u32[]{:S(2)}) %collective-permute-start.34) | collective-permute-done | bytes 2097184 | tf_op jit(solution)/shard_map/ppermute | solution.py:519
  1502.0 5.8 select_bitcast_fusion.7
  1507.8 7.7 pad_maximum_fusion.3
  1515.5 9.7 gather_fusion.2
  1528.4 9.4 collective-permute-start.18
  1542.7 93.3 %psum.7 = f32[2,3,64]{2,0,1:T(2,128)S(1)} all-reduce(f32[2,3,64]{2,0,1:T(2,128)S(1)} %pad_maximum_fusion.26), channel_id=1, replica_groups=mesh['y'=2,'core'=2,'z'=4,'x'=2] {'y','core','z','x'}, use_global_device_ids=true, to_apply=%region_21.22 | all-reduce | flops 384 | bytes 3072 | tf_op jit(solution)/shard_map/psum | solution.py:855
  1646.9 5.5 select_bitcast_fusion.1
  1652.4 7.7 pad_maximum_fusion.6
  1660.1 9.1 gather_fusion.4
  1670.6 9.4 collective-permute-start.36
  1696.6 165.7 %reduce-scatter.5.cloned.1.call-done = bf16[256,2432]{1,0:T(8,128)(2,1)} async-done(((bf16[2048,2432]{1,0:T(8,128)(2,1)}), bf16[256,2432]{1,0:T(8,128)(2,1)}) %reduce-scatter.5.cloned.1.call-update) | async-done | bytes 1245200 | tf_op jit(solution)/shard_map/reduce_scatter | solution.py:609
  1871.6 11.1 all-to-all-done.4
  1890.1 9.3 fusion.21
  1899.4 5.4 pad_maximum_fusion
  1904.8 8.1 copy.240
  (491 shorter events, 255.8 us)
Async XLA Ops:
  7.2 352.3 %all-gather.9.cloned.1.call-start = ((), (), s32[]{:S(2)}) async-start(), calls=%async_computation.13 | async-start | bytes 4718592 | tf_op jit(solution)/shard_map/all_gather | solution.py:603
  22.3 341.9 %all-gather.7.cloned.1.call-start = ((), (), s32[]{:S(2)}) async-start(), calls=%async_computation.12 | async-start | bytes 11206656 | tf_op jit(solution)/shard_map/all_gather | solution.py:603
  58.2 161.9 %collective-permute-start = (bf16[256,2048]{1,0:T(8,128)(2,1)}, bf16[256,2048]{1,0:T(8,128)(2,1)}, u32[]{:S(2)}, u32[]{:S(2)}) collective-permute-start(bf16[256,2048]{1,0:T(8,128)(2,1)} %get-tuple-element.172), channel_id=1, source_target_pairs={{0,0},{2,2},{4,8},{6,10},{8,4},{10,6},{12,12},{14,14},{1,1},{3,3},... | collective-permute-start | bytes 3145736 | tf_op jit(solution)/shard_map/ppermute | solution.py:562
  67.6 152.4 %collective-permute-start.1 = (bf16[256,2048]{1,0:T(8,128)(2,1)}, bf16[256,2048]{1,0:T(8,128)(2,1)}, u32[]{:S(2)}, u32[]{:S(2)}) collective-permute-start(bf16[256,2048]{1,0:T(8,128)(2,1)} %get-tuple-element.173), channel_id=1, source_target_pairs={{0,2},{2,0},{4,10},{6,8},{8,6},{10,4},{12,14},{14,12},{1,3},{3,1},... | collective-permute-start | bytes 3145736 | tf_op jit(solution)/shard_map/ppermute | solution.py:562
  69.7 248.0 %collective-permute-start.4 = (s32[2,1,2048]{2,1,0:T(1,128)S(1)}, s32[2,1,2048]{2,1,0:T(1,128)S(1)}, u32[]{:S(2)}, u32[]{:S(2)}) collective-permute-start(s32[2,1,2048]{2,1,0:T(1,128)S(1)} %copy-done.63), channel_id=1, source_target_pairs={{0,8},{8,0},{1,9},{9,1},{2,10},{10,2},{3,11},{11,3},{4,12},{12,4},... | collective-permute-start | bytes 49160 | tf_op jit(solution)/shard_map/ppermute | solution.py:664
  69.7 243.2 %collective-permute-start.5 = (s32[2,1,3]{2,1,0:T(1,128)S(1)}, s32[2,1,3]{2,1,0:T(1,128)S(1)}, u32[]{:S(2)}, u32[]{:S(2)}) collective-permute-start(s32[2,1,3]{2,1,0:T(1,128)S(1)} %copy-done.72), channel_id=1, source_target_pairs={{0,8},{8,0},{1,9},{9,1},{2,10},{10,2},{3,11},{11,3},{4,12},{12,4},... | collective-permute-start | bytes 80 | tf_op jit(solution)/shard_map/ppermute | solution.py:664
  71.0 143.9 %all-to-all-start.3 = ((bf16[64,4,1024]{2,0,1:T(8,128)(2,1)}), bf16[64,4,1024]{2,0,1:T(8,128)(2,1)}, u32[]{:S(2)}, u32[]{:S(2)}) async-start(bf16[64,4,1024]{2,0,1:T(8,128)(2,1)} %bitcast.422), calls=%async_computation.3 | async-start | bytes 1048576 | tf_op jit(solution)/shard_map/all_to_all | solution.py:601
  214.9 104.8 %all-to-all-start.2 = ((bf16[64,4,2432]{2,0,1:T(8,128)(2,1)}), bf16[64,4,2432]{2,0,1:T(8,128)(2,1)}, u32[]{:S(2)}, u32[]{:S(2)}) async-start(bf16[64,4,2432]{2,0,1:T(8,128)(2,1)} %concatenate.63), calls=%async_computation.2 | async-start | bytes 2490368 | tf_op jit(solution)/shard_map/all_to_all | solution.py:601
  219.3 412.6 %all-gather.13.cloned.1.call-start = ((), (), s32[]{:S(2)}) async-start(), calls=%async_computation.15 | async-start | bytes 4718592 | tf_op jit(solution)/shard_map/all_gather | solution.py:603
  220.0 416.7 %all-gather.11.cloned.1.call-start = ((), (), s32[]{:S(2)}) async-start(), calls=%async_computation.14 | async-start | bytes 11206656 | tf_op jit(solution)/shard_map/all_gather | solution.py:603
  222.0 85.4 %copy-start.30 = (bf16[2,256,2048]{2,1,0:T(8,128)(2,1)}, bf16[2,256,2048]{2,1,0:T(8,128)(2,1)S(1)}, u32[]{:S(2)}) copy-start(bf16[2,256,2048]{2,1,0:T(8,128)(2,1)S(1)} %pad_maximum_fusion.15) | copy-start | bytes 6291460
  222.0 85.4 %collective-permute-start.2 = (bf16[512,2048]{1,0:T(8,128)(2,1)S(1)}, bf16[512,2048]{1,0:T(8,128)(2,1)}, u32[]{:S(2)}, u32[]{:S(2)}) collective-permute-start(bf16[512,2048]{1,0:T(8,128)(2,1)S(1)} %bitcast.482), channel_id=1, source_target_pairs={{0,1},{1,0},{2,3},{3,2},{4,5},{5,4},{6,7},{7,6},{8,9},{9,8},{10,11... | collective-permute-start | bytes 6291464 | tf_op jit(solution)/shard_map/ppermute | solution.py:519
  225.2 147.7 %copy-start.43 = (f32[2048]{0:T(1024)}, f32[2048]{0:T(1024)S(1)}, u32[]{:S(2)}) copy-start(f32[2048]{0:T(1024)S(1)} %mul.283) | copy-start | bytes 24580
  312.6 7.5 collective-permute-start.3
  312.7 89.5 %copy-start = (f32[8,1024]{1,0:T(8,128)}, f32[8,1024]{1,0:T(8,128)S(1)}, u32[]{:S(2)}) copy-start(f32[8,1024]{1,0:T(8,128)S(1)} %concatenate.61.cw_ref) | copy-start | bytes 98308
  312.7 89.5 %copy-start.4 = (f32[8,128]{1,0:T(8,128)}, f32[8,128]{1,0:T(8,128)S(1)}, u32[]{:S(2)}) copy-start(f32[8,128]{1,0:T(8,128)S(1)} %select_maximum_fusion.1.hp_ref) | copy-start | bytes 12292
  312.8 89.4 %copy-start.2 = (f32[8,256]{1,0:T(8,128)}, f32[8,256]{1,0:T(8,128)S(1)}, u32[]{:S(2)}) copy-start(f32[8,256]{1,0:T(8,128)S(1)} %get-tuple-element.223.cbc_ref) | copy-start | bytes 24580
  319.7 1178.7 %reduce-scatter.11.cloned.1.call-start = ((), (), s32[]{:S(2)}) async-start(), calls=%async_computation.19 | async-start | bytes 4718592 | tf_op jit(solution)/shard_map/reduce_scatter | solution.py:609
  462.9 7.5 collective-permute-start.6
  474.9 48.2 %collective-permute-start.7 = (bf16[512,2048]{1,0:T(8,128)(2,1)}, bf16[512,2048]{1,0:T(8,128)(2,1)S(1)}, u32[]{:S(2)}, u32[]{:S(2)}) collective-permute-start(bf16[512,2048]{1,0:T(8,128)(2,1)} %fusion.17), channel_id=1, source_target_pairs={{0,1},{1,0},{2,3},{3,2},{4,5},{5,4},{6,7},{7,6},{8,9},{9,8},{10,11... | collective-permute-start | bytes 6291464 | tf_op jit(solution)/shard_map/ppermute | solution.py:540
  476.5 1.3 collective-permute-start.8
  477.8 45.3 %collective-permute-start.9 = (f32[512]{0:T(512)S(1)}, f32[512]{0:T(512)S(1)}, u32[]{:S(2)}, u32[]{:S(2)}) collective-permute-start(f32[512]{0:T(512)S(1)} %add.475), channel_id=1, source_target_pairs={{0,1},{1,0},{2,3},{3,2},{4,5},{5,4},{6,7},{7,6},{8,9},{9,8},{10,11... | collective-permute-start | bytes 6152 | tf_op jit(solution)/shard_map/ppermute | solution.py:540
  480.0 95.9 %copy-start.41 = (f32[2048]{0:T(1024)}, f32[2048]{0:T(1024)S(1)}, u32[]{:S(2)}) copy-start(f32[2048]{0:T(1024)S(1)} %mul.293) | copy-start | bytes 24580
  528.7 47.2 %collective-permute-start.10 = (bf16[512,2048]{1,0:T(8,128)(2,1)S(1)}, bf16[512,2048]{1,0:T(8,128)(2,1)S(1)}, u32[]{:S(2)}, u32[]{:S(2)}) collective-permute-start(bf16[512,2048]{1,0:T(8,128)(2,1)S(1)} %multiply_convert_fusion), channel_id=1, source_target_pairs={{0,1},{1,0},{2,3},{3,2},{4,5},{5,4},{6,7},{7,6},{8,9},{9,8},{10,11... | collective-permute-start | bytes 6291464 | tf_op jit(solution)/shard_map/ppermute | solution.py:519
  580.0 65.1 %collective-permute-start.11 = (bf16[2,512,2048]{2,1,0:T(8,128)(2,1)}, bf16[2,512,2048]{2,1,0:T(8,128)(2,1)}, u32[]{:S(2)}, u32[]{:S(2)}) collective-permute-start(bf16[2,512,2048]{2,1,0:T(8,128)(2,1)} %pad_maximum_fusion.10), channel_id=1, source_target_pairs={{0,8},{8,0},{1,9},{9,1},{2,10},{10,2},{3,11},{11,3},{4,12},{12,4},... | collective-permute-start | bytes 12582920 | tf_op jit(solution)/shard_map/ppermute | solution.py:522
  581.8 12.0 collective-permute-start.20
  591.4 36.8 %collective-permute-start.21 = (bf16[256,2048]{1,0:T(8,128)(2,1)}, bf16[256,2048]{1,0:T(8,128)(2,1)}, u32[]{:S(2)}, u32[]{:S(2)}) collective-permute-start(bf16[256,2048]{1,0:T(8,128)(2,1)} %get-tuple-element.169), channel_id=1, source_target_pairs={{0,2},{2,0},{4,10},{6,8},{8,6},{10,4},{12,14},{14,12},{1,3},{3,1},... | collective-permute-start | bytes 3145736 | tf_op jit(solution)/shard_map/ppermute | solution.py:562
  631.3 110.2 %collective-permute-start.22 = (bf16[512,2048]{1,0:T(8,128)(2,1)}, bf16[512,2048]{1,0:T(8,128)(2,1)}, u32[]{:S(2)}, u32[]{:S(2)}) collective-permute-start(bf16[512,2048]{1,0:T(8,128)(2,1)} %bitcast.112), channel_id=1, source_target_pairs={{0,1},{1,0},{2,3},{3,2},{4,5},{5,4},{6,7},{7,6},{8,9},{9,8},{10,11... | collective-permute-start | bytes 6291464 | tf_op jit(solution)/shard_map/ppermute | solution.py:519
  741.4 7.3 collective-permute-start.12
  748.7 7.4 collective-permute-start.23
  751.3 48.3 %collective-permute-start.13 = (bf16[512,2048]{1,0:T(8,128)(2,1)}, bf16[512,2048]{1,0:T(8,128)(2,1)S(1)}, u32[]{:S(2)}, u32[]{:S(2)}) collective-permute-start(bf16[512,2048]{1,0:T(8,128)(2,1)} %fusion.15), channel_id=1, source_target_pairs={{0,1},{1,0},{2,3},{3,2},{4,5},{5,4},{6,7},{7,6},{8,9},{9,8},{10,11... | collective-permute-start | bytes 6291464 | tf_op jit(solution)/shard_map/ppermute | solution.py:540
  789.6 1.2 collective-permute-start.14
  790.9 12.9 collective-permute-start.15
  803.8 3.7 collective-permute-start.24
  807.5 12.5 collective-permute-start.25
  949.2 61.8 %copy-start.42 = (f32[2048]{0:T(1024)S(1)}, f32[2048]{0:T(1024)}, u32[]{:S(2)}) copy-start(f32[2048]{0:T(1024)} %copy-done.41) | copy-start | bytes 24580
  949.2 65.6 %slice-start.2 = ((s8[8388608]{0:T(1024)(128)(4,1)}), s8[4194304]{0:T(1024)(128)(4,1)S(1)}, s32[]{:S(2)}) async-start(s8[8388608]{0:T(1024)(128)(4,1)} %bitcast.448), calls=%async_computation.23 | async-start | bytes 8388608
  951.6 59.4 %copy-start.9 = (f32[512,2048]{1,0:T(8,128)S(1)}, f32[512,2048]{1,0:T(8,128)}, u32[]{:S(2)}) copy-start(f32[512,2048]{1,0:T(8,128)} %copy-done.8) | copy-start | bytes 12582916
  951.6 63.1 %slice-start.3 = ((s8[8388608]{0:T(1024)(128)(4,1)}), s8[4194304]{0:T(1024)(128)(4,1)S(1)}, s32[]{:S(2)}) async-start(s8[8388608]{0:T(1024)(128)(4,1)} %bitcast.448), calls=%async_computation.24 | async-start | bytes 8388608
  951.7 7.5 collective-permute-start.26
  963.0 48.0 %collective-permute-start.27 = (bf16[512,2048]{1,0:T(8,128)(2,1)S(1)}, bf16[512,2048]{1,0:T(8,128)(2,1)S(1)}, u32[]{:S(2)}, u32[]{:S(2)}) collective-permute-start(bf16[512,2048]{1,0:T(8,128)(2,1)S(1)} %fusion.12), channel_id=1, source_target_pairs={{0,1},{1,0},{2,3},{3,2},{4,5},{5,4},{6,7},{7,6},{8,9},{9,8},{10,11... | collective-permute-start | bytes 6291464 | tf_op jit(solution)/shard_map/ppermute | solution.py:540
  1023.9 47.3 %collective-permute-start.28 = (bf16[512,2048]{1,0:T(8,128)(2,1)}, bf16[512,2048]{1,0:T(8,128)(2,1)S(1)}, u32[]{:S(2)}, u32[]{:S(2)}) collective-permute-start(bf16[512,2048]{1,0:T(8,128)(2,1)} %get-tuple-element.113), channel_id=1, source_target_pairs={{0,1},{1,0},{2,3},{3,2},{4,5},{5,4},{6,7},{7,6},{8,9},{9,8},{10,11... | collective-permute-start | bytes 6291464 | tf_op jit(solution)/shard_map/ppermute | solution.py:519
  1076.3 22.8 %collective-permute-start.29 = (bf16[2,512,2048]{2,1,0:T(8,128)(2,1)}, bf16[2,512,2048]{2,1,0:T(8,128)(2,1)}, u32[]{:S(2)}, u32[]{:S(2)}) collective-permute-start(bf16[2,512,2048]{2,1,0:T(8,128)(2,1)} %pad_maximum_fusion.13), channel_id=1, source_target_pairs={{0,8},{8,0},{1,9},{9,1},{2,10},{10,2},{3,11},{11,3},{4,12},{12,4},... | collective-permute-start | bytes 12582920 | tf_op jit(solution)/shard_map/ppermute | solution.py:522
  1089.8 546.9 %all-reduce.10.cloned.1.call-start = ((), (), s32[]{:S(2)}) async-start(), calls=%async_computation.20 | async-start | bytes 458752
  1090.5 3.7 collective-permute-start.30
  1094.2 1.2 collective-permute-start.31
  1223.6 419.0 %reduce-scatter.7.cloned.1.call-start = ((), (), s32[]{:S(2)}) async-start(), calls=%async_computation.17 | async-start | bytes 11206656 | tf_op jit(solution)/shard_map/reduce_scatter | solution.py:609
  1260.9 421.6 %reduce-scatter.9.cloned.1.call-start = ((), (), s32[]{:S(2)}) async-start(), calls=%async_computation.18 | async-start | bytes 4718592 | tf_op jit(solution)/shard_map/reduce_scatter | solution.py:609
  1276.2 586.2 %reduce-scatter.5.cloned.1.call-start = ((), (), s32[]{:S(2)}) async-start(), calls=%async_computation.16 | async-start | bytes 11206656 | tf_op jit(solution)/shard_map/reduce_scatter | solution.py:609
  1345.0 7.2 collective-permute-start.32
  1346.0 48.5 %collective-permute-start.16 = (bf16[512,2048]{1,0:T(8,128)(2,1)S(1)}, bf16[512,2048]{1,0:T(8,128)(2,1)S(1)}, u32[]{:S(2)}, u32[]{:S(2)}) collective-permute-start(bf16[512,2048]{1,0:T(8,128)(2,1)S(1)} %copy-done.33), channel_id=1, source_target_pairs={{0,1},{1,0},{2,3},{3,2},{4,5},{5,4},{6,7},{7,6},{8,9},{9,8},{10,11... | collective-permute-start | bytes 6291464 | tf_op jit(solution)/shard_map/ppermute | solution.py:519
  1353.1 85.7 %collective-permute-start.33 = (bf16[512,2048]{1,0:T(8,128)(2,1)S(1)}, bf16[512,2048]{1,0:T(8,128)(2,1)S(1)}, u32[]{:S(2)}, u32[]{:S(2)}) collective-permute-start(bf16[512,2048]{1,0:T(8,128)(2,1)S(1)} %fusion.9), channel_id=1, source_target_pairs={{0,1},{1,0},{2,3},{3,2},{4,5},{5,4},{6,7},{7,6},{8,9},{9,8},{10,11... | collective-permute-start | bytes 6291464 | tf_op jit(solution)/shard_map/ppermute | solution.py:540
  1398.9 103.0 %collective-permute-start.17 = (bf16[2,512,2048]{2,1,0:T(8,128)(2,1)}, bf16[2,512,2048]{2,1,0:T(8,128)(2,1)}, u32[]{:S(2)}, u32[]{:S(2)}) collective-permute-start(bf16[2,512,2048]{2,1,0:T(8,128)(2,1)} %pad_maximum_fusion.11), channel_id=1, source_target_pairs={{0,8},{8,0},{1,9},{9,1},{2,10},{10,2},{3,11},{11,3},{4,12},{12,4},... | collective-permute-start | bytes 12582920 | tf_op jit(solution)/shard_map/ppermute | solution.py:522
  1445.0 47.2 %collective-permute-start.34 = (bf16[512,2048]{1,0:T(8,128)(2,1)S(1)}, bf16[512,2048]{1,0:T(8,128)(2,1)S(1)}, u32[]{:S(2)}, u32[]{:S(2)}) collective-permute-start(bf16[512,2048]{1,0:T(8,128)(2,1)S(1)} %fusion.8), channel_id=1, source_target_pairs={{0,1},{1,0},{2,3},{3,2},{4,5},{5,4},{6,7},{7,6},{8,9},{9,8},{10,11... | collective-permute-start | bytes 6291464 | tf_op jit(solution)/shard_map/ppermute | solution.py:519
  1495.2 151.7 %collective-permute-start.35 = (bf16[2,512,2048]{2,1,0:T(8,128)(2,1)}, bf16[2,512,2048]{2,1,0:T(8,128)(2,1)}, u32[]{:S(2)}, u32[]{:S(2)}) collective-permute-start(bf16[2,512,2048]{2,1,0:T(8,128)(2,1)} %pad_maximum_fusion.14), channel_id=1, source_target_pairs={{0,8},{8,0},{1,9},{9,1},{2,10},{10,2},{3,11},{11,3},{4,12},{12,4},... | collective-permute-start | bytes 12582920 | tf_op jit(solution)/shard_map/ppermute | solution.py:522
  1498.5 42.5 %all-to-all-start.7 = ((bf16[4,64,1024]{2,1,0:T(8,128)(2,1)}), bf16[4,64,1024]{2,1,0:T(8,128)(2,1)S(1)}, u32[]{:S(2)}, u32[]{:S(2)}) async-start(bf16[4,64,1024]{2,1,0:T(8,128)(2,1)} %bitcast.519), calls=%async_computation.11 | async-start | bytes 1048576 | tf_op jit(solution)/shard_map/all_to_all | solution.py:610
  1528.4 111.0 %collective-permute-start.18 = (bf16[256,2048]{1,0:T(8,128)(2,1)}, bf16[256,2048]{1,0:T(8,128)(2,1)}, u32[]{:S(2)}, u32[]{:S(2)}) collective-permute-start(bf16[256,2048]{1,0:T(8,128)(2,1)} %get-tuple-element.164), channel_id=1, source_target_pairs={{0,0},{2,2},{8,4},{10,6},{4,8},{6,10},{12,12},{14,14},{1,1},{3,3},... | collective-permute-start | bytes 3145736 | tf_op jit(solution)/shard_map/ppermute | solution.py:572
  1537.8 101.5 %collective-permute-start.19 = (bf16[256,2048]{1,0:T(8,128)(2,1)}, bf16[256,2048]{1,0:T(8,128)(2,1)}, u32[]{:S(2)}, u32[]{:S(2)}) collective-permute-start(bf16[256,2048]{1,0:T(8,128)(2,1)} %get-tuple-element.165), channel_id=1, source_target_pairs={{2,0},{0,2},{10,4},{8,6},{6,8},{4,10},{14,12},{12,14},{3,1},{1,3},... | collective-permute-start | bytes 3145736 | tf_op jit(solution)/shard_map/ppermute | solution.py:572
  1642.6 37.8 %all-to-all-start.5 = ((bf16[4,64,2432]{2,1,0:T(8,128)(2,1)}), bf16[4,64,2432]{2,1,0:T(8,128)(2,1)}, u32[]{:S(2)}, u32[]{:S(2)}) async-start(bf16[4,64,2432]{2,1,0:T(8,128)(2,1)} %bitcast.510), calls=%async_computation.7 | async-start | bytes 2490368 | tf_op jit(solution)/shard_map/all_to_all | solution.py:610
  1670.6 197.0 %collective-permute-start.36 = (bf16[256,2048]{1,0:T(8,128)(2,1)}, bf16[256,2048]{1,0:T(8,128)(2,1)}, u32[]{:S(2)}, u32[]{:S(2)}) collective-permute-start(bf16[256,2048]{1,0:T(8,128)(2,1)} %get-tuple-element.160), channel_id=1, source_target_pairs={{0,0},{2,2},{8,4},{10,6},{4,8},{6,10},{12,12},{14,14},{1,1},{3,3},... | collective-permute-start | bytes 3145736 | tf_op jit(solution)/shard_map/ppermute | solution.py:572
  1680.0 187.6 %collective-permute-start.37 = (bf16[256,2048]{1,0:T(8,128)(2,1)}, bf16[256,2048]{1,0:T(8,128)(2,1)}, u32[]{:S(2)}, u32[]{:S(2)}) collective-permute-start(bf16[256,2048]{1,0:T(8,128)(2,1)} %get-tuple-element.161), channel_id=1, source_target_pairs={{2,0},{0,2},{10,4},{8,6},{6,8},{4,10},{14,12},{12,14},{3,1},{1,3},... | collective-permute-start | bytes 3145736 | tf_op jit(solution)/shard_map/ppermute | solution.py:572
  1682.5 13.0 all-to-all-start.6
  1693.0 173.2 %copy-start.39 = (bf16[4,8,8,1024]{3,2,0,1:T(8,128)(2,1)S(1)}, bf16[4,8,8,1024]{3,2,0,1:T(8,128)(2,1)}, u32[]{:S(2)}) copy-start(bf16[4,8,8,1024]{3,2,0,1:T(8,128)(2,1)} %copy.246) | copy-start | bytes 1572868
  1862.3 20.3 %all-to-all-start.4 = ((bf16[4,64,2432]{2,1,0:T(8,128)(2,1)}), bf16[4,64,2432]{2,1,0:T(8,128)(2,1)S(1)}, u32[]{:S(2)}, u32[]{:S(2)}) async-start(bf16[4,64,2432]{2,1,0:T(8,128)(2,1)} %bitcast.509), calls=%async_computation.5 | async-start | bytes 2490368 | tf_op jit(solution)/shard_map/all_to_all | solution.py:610
  (68 other events, 1115.8 us)
Sparse Core Ops, SparseCore 0:
  22.5 92.7 all-gather.8
  117.4 152.9 all-gather.6
  272.5 72.1 all-gather.12
  346.6 142.7 all-gather.10
  1089.9 89.7 reduce-scatter.10
  1223.7 128.5 all-reduce.9
  1356.5 169.3 reduce-scatter.6
  1529.9 119.1 reduce-scatter.8
  1652.7 209.5 reduce-scatter.4

commit v2 on v1

--- a/solution.py
+++ b/solution.py
@@ -10,7 +10,7 @@
 N = 128
 CONV = 4
 EPS = 1e-05
-PARTS = 1
+PARTS = 2
 DEPTH = 4
 SWAP = ((0, 1), (1, 0))
 CHUNK = 256
@@ -93,7 +93,7 @@
 
 
 def forward_kernel(
-    gate_ref, x_ref, bc_ref, st_ref, hx_ref, hbc_ref, meta_ref, segrow_ref, cw_ref, cbc_ref, hp_ref, s0_ref,
+    perm_ref, gate_ref, x_ref, bc_ref, st_ref, hx_ref, hbc_ref, meta_ref, segrow_ref, cw_ref, cbc_ref, hp_ref, s0_ref,
     mix_ref, gn_ref, ss_ref, states_ref, sout_ref,
     xpad, bpad, masks, cumb_ref, cumt_ref, mask_ref, sexp, eexp, texp, wide_ref, tall_ref, g_ref,
 ):
@@ -168,51 +168,51 @@
 def common_specs(chunk, width, order):
     bc_at, st_at = 2 * width // 256, (2 * width + 256) // LANES
     return [
-        pl.BlockSpec((chunk, width), lambda c: (order(c), 0)),
-        pl.BlockSpec((chunk, width), lambda c: (order(c), 1)),
-        pl.BlockSpec((chunk, 256), lambda c: (order(c), bc_at)),
-        pl.BlockSpec((chunk, LANES), lambda c: (order(c), st_at)),
+        pl.BlockSpec((chunk, width), lambda c, perm: (perm[order(c)], 0)),
+        pl.BlockSpec((chunk, width), lambda c, perm: (perm[order(c)], 1)),
+        pl.BlockSpec((chunk, 256), lambda c, perm: (perm[order(c)], bc_at)),
+        pl.BlockSpec((chunk, LANES), lambda c, perm: (perm[order(c)], st_at)),
     ]
 
 
 def fixed(shape):
-    return pl.BlockSpec(shape, lambda c: (0,) * len(shape))
-
-
-def mixer_forward(proj, halo, meta, segrow, cw, cbc, hp, state, chunk=CHUNK):
+    return pl.BlockSpec(shape, lambda c, perm: (0,) * len(shape))
+
+
+def last_rows(count, chunk):
+    return lambda perm: (perm[count - 1] + 1) * (chunk // 16) - 1
+
+
+def mixer_forward(perm, proj, before, meta, segrow, cw, cbc, hp, state, chunk=CHUNK):
     rows = proj.shape[0]
     width = cw.shape[1]
     count = rows // chunk
     same = lambda c: c
     bc_at = 2 * width // 256
+    ending = last_rows(count, chunk)
     f32 = jnp.float32
     return pl.pallas_call(
         forward_kernel,
+        grid_spec=pltpu.PrefetchScalarGridSpec(
+        num_scalar_prefetch=1,
         grid=(count,),
         in_specs=common_specs(chunk, width, same)
         + [
-            pl.BlockSpec((16, width), lambda c: (0, 1)),
-            pl.BlockSpec((16, 256), lambda c: (0, bc_at)),
-            pl.BlockSpec((chunk, 8), lambda c: (c, 0)),
-            pl.BlockSpec((1, 1, chunk), lambda c: (c, 0, 0)),
+            pl.BlockSpec((16, width), lambda c, perm: (ending(perm), 1)),
+            pl.BlockSpec((16, 256), lambda c, perm: (ending(perm), bc_at)),
+            pl.BlockSpec((chunk, 8), lambda c, perm: (c, 0)),
+            pl.BlockSpec((1, 1, chunk), lambda c, perm: (c, 0, 0)),
             fixed((8, width)),
             fixed((8, 256)),
             fixed((8, LANES)),
             fixed((N, width)),
         ],
         out_specs=[
-            pl.BlockSpec((chunk, width), lambda c: (c, 0)),
-            pl.BlockSpec((chunk, width), lambda c: (c, 0)),
-            pl.BlockSpec((chunk, LANES), lambda c: (c, 0)),
-            pl.BlockSpec((1, N, width), lambda c: (c, 0, 0)),
+            pl.BlockSpec((chunk, width), lambda c, perm: (perm[c], 0)),
+            pl.BlockSpec((chunk, width), lambda c, perm: (perm[c], 0)),
+            pl.BlockSpec((chunk, LANES), lambda c, perm: (perm[c], 0)),
+            pl.BlockSpec((1, N, width), lambda c, perm: (c, 0, 0)),
             fixed((N, width)),
-        ],
-        out_shape=[
-            jax.ShapeDtypeStruct((rows, width), jnp.bfloat16),
-            jax.ShapeDtypeStruct((rows, width), jnp.bfloat16),
-            jax.ShapeDtypeStruct((rows, LANES), f32),
-            jax.ShapeDtypeStruct((count, N, width), f32),
-            jax.ShapeDtypeStruct((N, width), f32),
         ],
         scratch_shapes=[
             pltpu.VMEM((chunk + 8, width), f32),
@@ -228,14 +228,22 @@
             pltpu.VMEM((LANES, 2 * width), jnp.bfloat16),
             pltpu.VMEM((chunk, chunk), f32),
         ],
+        ),
+        out_shape=[
+            jax.ShapeDtypeStruct((rows, width), jnp.bfloat16),
+            jax.ShapeDtypeStruct((rows, width), jnp.bfloat16),
+            jax.ShapeDtypeStruct((rows, LANES), f32),
+            jax.ShapeDtypeStruct((count, N, width), f32),
+            jax.ShapeDtypeStruct((N, width), f32),
+        ],
         compiler_params=pltpu.CompilerParams(
             vmem_limit_bytes=VMEM_BYTES, dimension_semantics=("arbitrary",)
         ),
         cost_estimate=pl.CostEstimate(
-            flops=rows * width * 1200, bytes_accessed=rows * width * 12, transcendentals=rows * width * 6
+            flops=rows * width * 28000, bytes_accessed=rows * width * 12, transcendentals=rows * width * 6
         ),
         name="mix_fwd",
-    )(proj, proj, proj, proj, halo, halo, meta, segrow, cw, cbc, hp, state)
+    )(perm, proj, proj, proj, proj, before, before, meta, segrow, cw, cbc, hp, state)
 
 
 def conv_back(dpre, taps, masks, here, back, dpad, tail_ref, sl, chunk, acc_ref):
@@ -253,9 +261,9 @@
 
 
 def backward_kernel(
-    gate_ref, x_ref, bc_ref, st_ref, px_ref, pbc_ref, hx_ref, hbc_ref, meta_ref, segrow_ref, cw_ref, cbc_ref, hp_ref,
+    perm_ref, gate_ref, x_ref, bc_ref, st_ref, px_ref, pbc_ref, hx_ref, hbc_ref, meta_ref, segrow_ref, cw_ref, cbc_ref, hp_ref,
     mix_ref, u_ref, fs_ref, states_ref, ds0_ref, tx0_ref, tbc0_ref,
-    gproj_ref, n2_ref, acc_ref, accbc_ref, acch_ref, ds_ref, tx_ref, tbc_ref,
+    gproj_ref, acc_ref, accbc_ref, acch_ref, ds_ref, tx_ref, tbc_ref,
     xpad, bpad, masks, cumb_ref, cumt_ref, mask_ref, sexp, eexp, dexp, wide_ref, tall_ref, g_ref,
     dg_ref, db_ref, dc_ref, dcum_ref, dsx_ref, dpad, fac_ref, sb_ref,
 ):
@@ -325,7 +333,6 @@
         dgated = up * cw[6:7, :] - gated * sb_ref[...]
         gm = (dgated * active).astype(jnp.bfloat16)
         gproj_ref[:, sl] = (dgated * mixval * sg * (1.0 + gz * (1.0 - sg))).astype(jnp.bfloat16)
-        n2_ref[:, sl] = (gated * fac * cw[6:7, :]).astype(jnp.bfloat16)
         acc_ref[6:7, sl] += jnp.sum(gated * up, axis=0, keepdims=True)
         dy = gm.astype(jnp.float32)
         pre, back, here = conv_parts(xpad, sl, chunk, cw, masks)
@@ -403,7 +410,7 @@
     acch_ref[1:2, :] += jnp.sum(dlogs * steps, axis=0, keepdims=True)
 
 
-def mixer_backward(proj, halo, meta, segrow, cw, cbc, hp, mix, up, fs, states, dstate, tx, tbc, chunk=CHUNK):
+def mixer_backward(perm, proj, prior, meta, segrow, cw, cbc, hp, mix, up, fs, states, dstate, tx, tbc, chunk=CHUNK):
     rows, cols = proj.shape
     width = cw.shape[1]
     count = rows // chunk
@@ -411,48 +418,43 @@
     bc_at = 2 * width // 256
     f32 = jnp.float32
     per = chunk // 16
-    before = lambda c: jnp.maximum(back(c) * per - 1, 0)
+    ending = last_rows(count, chunk)
+
+    def before(c, perm):
+        return (perm[jnp.maximum(back(c) - 1, 0)] + 1) * per - 1
+
     return pl.pallas_call(
         backward_kernel,
+        grid_spec=pltpu.PrefetchScalarGridSpec(
+        num_scalar_prefetch=1,
         grid=(count,),
         in_specs=common_specs(chunk, width, back)
         + [
-            pl.BlockSpec((16, width), lambda c: (before(c), 1)),
-            pl.BlockSpec((16, 256), lambda c: (before(c), bc_at)),
-            pl.BlockSpec((16, width), lambda c: (0, 1)),
-            pl.BlockSpec((16, 256), lambda c: (0, bc_at)),
-            pl.BlockSpec((chunk, 8), lambda c: (back(c), 0)),
-            pl.BlockSpec((1, 1, chunk), lambda c: (back(c), 0, 0)),
+            pl.BlockSpec((16, width), lambda c, perm: (before(c, perm), 1)),
+            pl.BlockSpec((16, 256), lambda c, perm: (before(c, perm), bc_at)),
+            pl.BlockSpec((16, width), lambda c, perm: (ending(perm), 1)),
+            pl.BlockSpec((16, 256), lambda c, perm: (ending(perm), bc_at)),
+            pl.BlockSpec((chunk, 8), lambda c, perm: (back(c), 0)),
+            pl.BlockSpec((1, 1, chunk), lambda c, perm: (back(c), 0, 0)),
             fixed((8, width)),
             fixed((8, 256)),
             fixed((8, LANES)),
-            pl.BlockSpec((chunk, width), lambda c: (back(c), 0)),
-            pl.BlockSpec((chunk, width), lambda c: (back(c), 0)),
-            pl.BlockSpec((chunk, 8), lambda c: (back(c), 0)),
-            pl.BlockSpec((1, N, width), lambda c: (back(c), 0, 0)),
+            pl.BlockSpec((chunk, width), lambda c, perm: (perm[back(c)], 0)),
+            pl.BlockSpec((chunk, width), lambda c, perm: (perm[back(c)], 0)),
+            pl.BlockSpec((chunk, 8), lambda c, perm: (perm[back(c)], 0)),
+            pl.BlockSpec((1, N, width), lambda c, perm: (back(c), 0, 0)),
             fixed((N, width)),
             fixed((3, 8, width)),
             fixed((3, 8, 256)),
         ],
         out_specs=[
-            pl.BlockSpec((chunk, cols), lambda c: (back(c), 0)),
-            pl.BlockSpec((chunk, width), lambda c: (back(c), 0)),
+            pl.BlockSpec((chunk, cols), lambda c, perm: (perm[back(c)], 0)),
             fixed((8, width)),
             fixed((8, 256)),
             fixed((8, LANES)),
             fixed((N, width)),
             fixed((3, 8, width)),
             fixed((3, 8, 256)),
-        ],
-        out_shape=[
-            jax.ShapeDtypeStruct((rows, cols), jnp.bfloat16),
-            jax.ShapeDtypeStruct((rows, width), jnp.bfloat16),
-            jax.ShapeDtypeStruct((8, width), f32),
-            jax.ShapeDtypeStruct((8, 256), f32),
-            jax.ShapeDtypeStruct((8, LANES), f32),
-            jax.ShapeDtypeStruct((N, width), f32),
-            jax.ShapeDtypeStruct((3, 8, width), f32),
-            jax.ShapeDtypeStruct((3, 8, 256), f32),
         ],
         scratch_shapes=[
             pltpu.VMEM((chunk + 8, width), f32),
@@ -476,15 +478,25 @@
             pltpu.VMEM((chunk, LANES), f32),
             pltpu.VMEM((chunk, LANES), f32),
         ],
+        ),
+        out_shape=[
+            jax.ShapeDtypeStruct((rows, cols), jnp.bfloat16),
+            jax.ShapeDtypeStruct((8, width), f32),
+            jax.ShapeDtypeStruct((8, 256), f32),
+            jax.ShapeDtypeStruct((8, LANES), f32),
+            jax.ShapeDtypeStruct((N, width), f32),
+            jax.ShapeDtypeStruct((3, 8, width), f32),
+            jax.ShapeDtypeStruct((3, 8, 256), f32),
+        ],
         compiler_params=pltpu.CompilerParams(
             vmem_limit_bytes=VMEM_BYTES, dimension_semantics=("arbitrary",)
         ),
         cost_estimate=pl.CostEstimate(
-            flops=rows * width * 4000, bytes_accessed=rows * width * 24, transcendentals=rows * width * 8
+            flops=rows * width * 56000, bytes_accessed=rows * width * 24, transcendentals=rows * width * 8
         ),
         name="mix_bwd",
     )(
-        proj, proj, proj, proj, proj, proj, halo, halo, meta, segrow, cw, cbc, hp,
+        perm, proj, proj, proj, proj, proj, proj, prior, prior, meta, segrow, cw, cbc, hp,
         mix, up, fs, states, dstate, tx, tbc,
     )
 
@@ -505,42 +517,88 @@
     return meta, seg.astype(jnp.float32).reshape(-1, 1, chunk)
 
 
-def team_sizes():
-    return lax.axis_size("x"), 2 * lax.axis_size("x")
-
-
-def in_order(first, mine, theirs):
-    return jnp.stack([jnp.where(first, mine, theirs), jnp.where(first, theirs, mine)])
-
-
-def team_gather(own):
-    across = lax.axis_size("x")
-    if across == 2:
-        row = in_order(lax.axis_index("x") == 0, own, lax.ppermute(own, "x", SWAP))
-    else:
-        row = lax.all_gather(own, "x", axis=0)
-    both = in_order(lax.axis_index("core") == 0, row, lax.ppermute(row, "core", SWAP))
-    return both.reshape((2 * across,) + own.shape)
-
-
-def team_reduce(parts, kind):
-    across = lax.axis_size("x")
+def swap(value, axis):
+    return lax.ppermute(value, axis, SWAP)
+
+
+def paired():
+    return lax.axis_size("x") == 2
+
+
+def member_index():
+    return lax.axis_index("core") * lax.axis_size("x") + lax.axis_index("x")
+
+
+def slot_of(members):
+    return members ^ member_index() if paired() else members
+
+
+def team_gather(own, *first):
+    if paired():
+        came = swap(own, "x")
+        row = after(jnp.concatenate([own, came]), *first)
+        return jnp.concatenate([row, swap(row, "core")]), came
+    row = lax.all_gather(own, "x", axis=0, tiled=True)
+    other = swap(row, "core")
+    first = lax.axis_index("core") == 0
+    return jnp.concatenate([jnp.where(first, row, other), jnp.where(first, other, row)]), row
+
+
+def team_reduce(blocks, rows, kind, first=()):
+    half = lax.axis_size("x") * rows
+    if paired():
+        got = swap(blocks[half:], "core")
+        near = blocks[rows:half].astype(jnp.float32) + got[rows:].astype(jnp.float32)
+        near = after(near.astype(kind), *first)
+        far = swap(near, "x")
+        total = blocks[:rows].astype(jnp.float32) + got[:rows].astype(jnp.float32)
+        return total + far.astype(jnp.float32), near, far
     core = lax.axis_index("core")
-    halves = parts.reshape((2, across) + parts.shape[1:])
+    halves = blocks.reshape((2, half) + blocks.shape[1:])
+    got = swap(lax.dynamic_index_in_dim(halves, 1 - core, 0, False), "core")
     keep = lax.dynamic_index_in_dim(halves, core, 0, False)
-    got = lax.ppermute(lax.dynamic_index_in_dim(halves, 1 - core, 0, False), "core", SWAP)
-    if across == 2:
-        place = lax.axis_index("x")
-
-        def added(at):
-            return lax.dynamic_index_in_dim(keep, at, 0, False).astype(jnp.float32) + (
-                lax.dynamic_index_in_dim(got, at, 0, False).astype(jnp.float32)
-            )
-
-        far = lax.ppermute(added(1 - place).astype(kind), "x", SWAP)
-        return added(place) + far.astype(jnp.float32)
     sums = (keep.astype(jnp.float32) + got.astype(jnp.float32)).astype(kind)
-    return lax.psum_scatter(sums, "x", scatter_dimension=0, tiled=False).astype(jnp.float32)
+    total = lax.psum_scatter(sums, "x", scatter_dimension=0, tiled=True)
+    return total.astype(jnp.float32), sums, total
+
+
+def plane_cycle():
+    across = lax.axis_size("y")
+    walk = [0]
+    for y in range(across):
+        line = range(1, DEPTH) if y % 2 == 0 else range(DEPTH - 1, 0, -1)
+        walk += [y * DEPTH + z for z in line]
+    return walk + [y * DEPTH for y in range(across - 1, 0, -1)]
+
+
+def plane_steps():
+    walk = plane_cycle()
+    count = len(walk)
+    places = [walk.index(i) for i in range(count)]
+    here = jnp.asarray(places, jnp.int32)[lax.axis_index("y") * DEPTH + lax.axis_index("z")]
+    forwards = [(walk[i], walk[(i + 1) % count]) for i in range(count)]
+    return jnp.asarray(walk, jnp.int32), here, forwards, [(b, a) for a, b in forwards]
+
+
+def ring_gather(block, beside=()):
+    walk, here, forwards, backwards = plane_steps()
+    count = walk.shape[0]
+    rows = block.shape[0]
+
+    def put(whole, value, place):
+        return lax.dynamic_update_slice_in_dim(whole, value, walk[place % count] * rows, 0)
+
+    whole = put(jnp.zeros((count * rows, block.shape[1]), block.dtype), block, here)
+    ahead = behind = block
+    for step in range(1, count // 2 + 1):
+        ahead = lax.ppermute(ahead, ("y", "z"), forwards)
+        whole = put(whole, ahead, here + count - step)
+        if step < count - count // 2:
+            behind = lax.ppermute(behind, ("y", "z"), backwards)
+            whole = put(whole, behind, here + step)
+        if step <= len(beside):
+            ahead = after(ahead, beside[step - 1])
+    return whole
 
 
 def deal_moves():
@@ -554,23 +612,66 @@
     return moves
 
 
-def to_team(rows):
+def column_blocks(across, rows):
+    wide = lax.axis_size("x") * rows
+    for y in range(across):
+        for core in range(2):
+            for z in range(DEPTH):
+                yield ((y * DEPTH + z) * 2 + core) * wide, ((y * 2 + core) * DEPTH + z) * wide, wide
+
+
+def to_team(rows, weight_rows):
+    blocks = list(column_blocks(lax.axis_size("y"), weight_rows))
     low = lax.axis_index("z") % 2
-    got = []
-    for r, pairs in enumerate(deal_moves()):
-        block = lax.dynamic_index_in_dim(rows, low ^ r, 0, False)
-        got.append(lax.ppermute(block, ("core", "z"), pairs))
-    return in_order(low == 0, got[0], got[1]).reshape(-1, rows.shape[2])
+
+    def body(low_ref, rows_ref, *out_refs):
+        for to, at, wide in blocks:
+            for r in range(2):
+                out_refs[r][:, to : to + wide] = rows_ref[low_ref[0] ^ r, :, at : at + wide]
+
+    shape = jax.ShapeDtypeStruct(rows.shape[1:], rows.dtype)
+    sent = pl.pallas_call(
+        body,
+        grid_spec=pltpu.PrefetchScalarGridSpec(
+            num_scalar_prefetch=1,
+            grid=(1,),
+            in_specs=[pl.BlockSpec(rows.shape, lambda c, low: (0, 0, 0))],
+            out_specs=[pl.BlockSpec(rows.shape[1:], lambda c, low: (0, 0))] * 2,
+        ),
+        out_shape=[shape, shape],
+        compiler_params=pltpu.CompilerParams(vmem_limit_bytes=VMEM_BYTES),
+        name="to_plane",
+    )(low.reshape(1), rows)
+    return [lax.ppermute(v, ("core", "z"), pairs) for v, pairs in zip(sent, deal_moves())]
 
 
 def from_team(rows):
+    moves = zip(rows, deal_moves())
+    return [lax.ppermute(v, ("core", "z"), [(b, a) for a, b in pairs]) for v, pairs in moves]
+
+
+def dealt(got, weight_rows, kind):
+    blocks = list(column_blocks(lax.axis_size("y"), weight_rows))
     low = lax.axis_index("z") % 2
-    blocks = rows.reshape(2, -1, rows.shape[1])
-    got = []
-    for r, pairs in enumerate(deal_moves()):
-        block = lax.dynamic_index_in_dim(blocks, low ^ r, 0, False)
-        got.append(lax.ppermute(block, ("core", "z"), [(b, a) for a, b in pairs]))
-    return in_order(low == 0, got[0], got[1])
+    shape = got[0].shape
+
+    def body(low_ref, first_ref, second_ref, out_ref):
+        for at, to, wide in blocks:
+            for r, ref in enumerate((first_ref, second_ref)):
+                out_ref[low_ref[0] ^ r, :, to : to + wide] = ref[:, at : at + wide].astype(kind)
+
+    return pl.pallas_call(
+        body,
+        grid_spec=pltpu.PrefetchScalarGridSpec(
+            num_scalar_prefetch=1,
+            grid=(1,),
+            in_specs=[pl.BlockSpec(shape, lambda c, low: (0, 0))] * 2,
+            out_specs=pl.BlockSpec((2,) + shape, lambda c, low: (0, 0, 0)),
+        ),
+        out_shape=jax.ShapeDtypeStruct((2,) + shape, kind),
+        compiler_params=pltpu.CompilerParams(vmem_limit_bytes=VMEM_BYTES),
+        name="to_natural",
+    )(low.reshape(1), *got)
 
 
 def inverse_of(perm):
@@ -585,48 +686,139 @@
     return jnp.sum((places[:, None] >= ends[None, :]).astype(jnp.int32), axis=1)
 
 
-def natural_rows(gathered):
-    total, cols = gathered.shape
-    view = gathered.reshape(lax.axis_size("y"), DEPTH, 2, -1, cols)
-    return view.transpose(0, 2, 1, 3, 4).reshape(total, cols)
-
-
-def plane_rows(natural):
-    total, cols = natural.shape
-    view = natural.reshape(lax.axis_size("y"), 2, DEPTH, -1, cols)
-    return view.transpose(0, 2, 1, 3, 4).reshape(total, cols)
-
-
-def to_heads(pieces):
+def reorder(values, axis, inner, outer):
+    shape = values.shape
+    count = lax.axis_size("y")
+    view = values.reshape(shape[:axis] + (count, inner, outer, -1) + shape[axis + 1 :])
+    order = list(range(view.ndim))
+    order[axis + 1], order[axis + 2] = axis + 2, axis + 1
+    return view.transpose(order).reshape(shape)
+
+
+def to_plane(values, axis):
+    return reorder(values, axis, 2, DEPTH)
+
+
+def to_members(pieces):
     sent = lax.all_to_all(pieces, ("core", "x"), split_axis=1, concat_axis=0, tiled=True)
-    sent = sent.reshape(-1, pieces.shape[2])
-    return natural_rows(lax.all_gather(sent, ("y", "z"), axis=0, tiled=True))
-
-
-def from_heads(grads):
-    cols = grads.shape[1]
+    return sent.reshape(-1, pieces.shape[2])
+
+
+def plane_gather(block):
+    return lax.all_gather(block, ("y", "z"), axis=0, tiled=True)
+
+
+def from_plane(summed):
     team = 2 * lax.axis_size("x")
-    summed = lax.psum_scatter(plane_rows(grads), ("y", "z"), scatter_dimension=0, tiled=True)
-    back = lax.all_to_all(
-        summed.reshape(team, -1, cols), ("core", "x"), split_axis=0, concat_axis=0, tiled=True
-    )
-    return back.transpose(1, 0, 2)
-
-
-def in_columns(w_in, team):
+    blocks = summed.reshape(team, -1, summed.shape[1])
+    return lax.all_to_all(blocks, ("core", "x"), split_axis=0, concat_axis=0, tiled=True)
+
+
+def after(value, *others):
+    return lax.optimization_barrier((value,) + others)[0]
+
+
+def in_kernel(layers, team, width, split_refs, weight_ref, grad_ref, norm_ref, tile_ref):
+    for layer in range(layers):
+        total = jnp.zeros(norm_ref.shape[1:], jnp.float32)
+        pieces = []
+        for q in range(team):
+            pieces.append((q * width, split_refs[layer][q, :, :width].astype(jnp.float32)))
+            pieces.append((DI + q * width, split_refs[layer][q, :, width : 2 * width].astype(jnp.float32)))
+        states = split_refs[layer][0, :, 2 * width : 2 * width + 2 * N].astype(jnp.float32)
+        for q in range(1, team):
+            states = states + split_refs[layer][q, :, 2 * width : 2 * width + 2 * N].astype(jnp.float32)
+        pieces.append((2 * DI, states))
+        for at, value in pieces:
+            count = value.shape[1]
+            grad_ref[layer, :, at : at + count] = value
+            product = value * weight_ref[layer, :, at : at + count].astype(jnp.float32)
+            for tile in range(count // LANES):
+                total = total + product[:, tile * LANES : (tile + 1) * LANES]
+        tiles = split_refs[layer][:, :, 2 * width + 2 * N :].astype(jnp.float32)
+        tile_ref[layer] = tiles
+        count = (weight_ref.shape[2] - 2 * DI - 2 * N) // team
+        steps = jnp.zeros(norm_ref.shape[1:], jnp.float32)
+        lane = lax.broadcasted_iota(jnp.int32, steps.shape, 1)
+        for q in range(team):
+            moved = pltpu.roll(tiles[q], q * count, 1) if q else tiles[q]
+            steps = jnp.where((lane >= q * count) & (lane < (q + 1) * count), moved, steps)
+        grad_ref[layer, :, 2 * DI + 2 * N :] = steps[:, : team * count]
+        product = steps[:, : team * count] * weight_ref[layer, :, 2 * DI + 2 * N :].astype(jnp.float32)
+        norm_ref[layer] = jnp.broadcast_to(
+            jnp.sum(total, axis=1, keepdims=True) + jnp.sum(product, axis=1, keepdims=True), total.shape
+        )
+
+
+def assemble_in(splits, in_weight):
+    layers, rows, cols = in_weight.shape
+    team, width = splits[0].shape[0], DI // splits[0].shape[0]
+
+    def body(*refs):
+        in_kernel(layers, team, width, refs[:layers], *refs[layers:])
+
+    return pl.pallas_call(
+        body,
+        out_shape=[
+            jax.ShapeDtypeStruct((layers, rows, cols), jnp.float32),
+            jax.ShapeDtypeStruct((layers, rows, LANES), jnp.float32),
+            jax.ShapeDtypeStruct((layers, team, rows, LANES), jnp.float32),
+        ],
+        compiler_params=pltpu.CompilerParams(vmem_limit_bytes=VMEM_BYTES),
+        name="grad_in",
+    )(*splits, in_weight)
+
+
+def assemble_out(outs):
+    layers = len(outs)
+    team, rows, width = outs[0].shape
+
+    def body(*refs):
+        for layer in range(layers):
+            for q in range(team):
+                refs[layers][layer, :, q * width : (q + 1) * width] = refs[layer][q].astype(jnp.float32)
+
+    return pl.pallas_call(
+        body,
+        out_shape=jax.ShapeDtypeStruct((layers, rows, DI), jnp.float32),
+        compiler_params=pltpu.CompilerParams(vmem_limit_bytes=VMEM_BYTES),
+        name="grad_out",
+    )(*outs)
+
+
+def in_columns(w_in, team, extra):
     rows = w_in.shape[0]
     bc = w_in[:, 2 * DI : 2 * DI + 2 * N]
     step = w_in[:, 2 * DI + 2 * N :].reshape(rows, team, -1)
+    shared = jnp.concatenate(
+        [extra, jnp.zeros((rows, LANES - step.shape[2] - extra.shape[1]), w_in.dtype)], axis=1
+    )
     return jnp.concatenate(
         [
             w_in[:, :DI].reshape(rows, team, -1),
             w_in[:, DI : 2 * DI].reshape(rows, team, -1),
             jnp.broadcast_to(bc[:, None, :], (rows, team, 2 * N)),
             step,
-            jnp.zeros((rows, team, LANES - step.shape[2]), w_in.dtype),
+            jnp.broadcast_to(shared[:, None, :], (rows, team, shared.shape[1])),
         ],
         axis=2,
     )
+
+
+def rounded(values):
+    return lax.reduce_precision(values, 8, 7)
+
+
+def in_parts(values):
+    hi = rounded(values)
+    mid = rounded(values - hi)
+    return jnp.stack([hi, mid, rounded(values - hi - mid)]).astype(jnp.bfloat16)
+
+
+def as_rows(flat, rows):
+    count = -(-flat.shape[-1] // rows)
+    flat = jnp.pad(flat, [(0, 0)] * (flat.ndim - 1) + [(0, count * rows - flat.shape[-1])])
+    return jnp.swapaxes(flat.reshape(flat.shape[:-1] + (count, rows)), -1, -2)
 
 
 def row_scale(rows):
@@ -650,192 +842,189 @@
 ):
     bf16, f32 = jnp.bfloat16, jnp.float32
     layers = in_weight.shape[0]
-    across, team = team_sizes()
+    across = lax.axis_size("x")
+    team = 2 * across
     core, z, x = (lax.axis_index(name) for name in ("core", "z", "x"))
-    member = core * across + x
+    member = member_index()
     width = DI // team
     heads = width // HEAD
     rows_here = hidden.shape[1]
     tokens = token_order.shape[2]
     part_rows = tokens // PARTS
     own_rows = part_rows // team
+    weight_rows = in_weight.shape[1]
+    wide = conv_bias.shape[1]
+    gate_wide = gate_gain.shape[1]
+    head_wide = dt_bias.shape[1]
+    bc_at = 2 * width
+    step_at = bc_at + 2 * N
+    extra_at = step_at + heads
+    numbers = jnp.arange(tokens, dtype=jnp.int32)
 
     def of_pair(ints):
-        other = lax.ppermute(ints, "core", SWAP)
-        return lax.dynamic_index_in_dim(jnp.where(z // 2 == core, ints, other), z % 2, 0, False)[0]
+        return lax.dynamic_index_in_dim(
+            jnp.where(z // 2 == core, ints, swap(ints, "core")), z % 2, 0, False
+        )[0]
 
     order, sizes = of_pair(token_order), of_pair(lengths)
     inverse = inverse_of(order)
+    mine = z % 2
     block, within = inverse // rows_here, inverse % rows_here
     from_z, from_x = block // across, block % across
-    place = ((from_z // 2 * across + from_x) * 2 + from_z % 2) * rows_here + within
-    own_block = (2 * core + jnp.arange(2, dtype=jnp.int32)) * across + x
-    own_dealt = (own_block[:, None] * rows_here + jnp.arange(rows_here, dtype=jnp.int32)).reshape(-1)
+    place = (slot_of(from_z // 2 * across + from_x) * 2 + (from_z % 2 ^ mine)) * rows_here + within
+    if paired():
+        view = place.reshape(PARTS, 2, 2, own_rows)
+        view = jnp.where(core == 1, view[:, ::-1], view)
+        place = jnp.where(x == 1, view[:, :, ::-1], view).reshape(-1)
+    target = jnp.concatenate(
+        [
+            lax.dynamic_slice_in_dim(order, ((2 * core + (r ^ mine)) * across + x) * rows_here, rows_here)
+            for r in range(2)
+        ]
+    )
+    inside = target % part_rows
+    own_place = (
+        target // part_rows * part_rows + slot_of(inside // own_rows) * own_rows + inside % own_rows
+    )
     meta, segrow = token_facts(segments_of(sizes, tokens))
-
-    w_cols = [to_heads(in_columns(in_weight[layer], team)) for layer in range(layers)]
-    w_out = [
-        to_heads(out_weight[layer].T.reshape(-1, team, width)) for layer in range(layers)
-    ]
-    flat = jnp.concatenate(
-        [conv_weight.reshape(layers, -1), conv_bias, norm_gain, gate_gain], axis=1
-    )
-    wide = conv_bias.shape[1]
-    full = lax.all_gather(flat, ("y", "core", "z", "x"), axis=0).transpose(1, 0, 2)
-    cuts = [CONV * wide, (CONV + 1) * wide, (CONV + 1) * wide + norm_gain.shape[1]]
-    taps, shift, ngain, ggain = jnp.split(full.astype(f32), cuts, axis=2)
-    taps = taps.reshape(layers, -1, CONV, wide).transpose(0, 2, 1, 3).reshape(layers, CONV, -1)
-    shift, ngain, ggain = (v.reshape(layers, -1) for v in (shift, ngain, ggain))
-    per_head = lax.all_gather(
-        jnp.stack([dt_bias, log_decay, skip_gain]), ("z", "x"), axis=2, tiled=True
-    )
-    own_heads = lax.dynamic_slice_in_dim(per_head, member * heads, heads, 2)
-
-    def mine(values):
+    chunks = numbers[: part_rows // CHUNK]
+    if paired():
+        per = own_rows // CHUNK
+        perm = slot_of(chunks // per) * per + chunks % per
+    else:
+        perm = chunks
+
+    small = []
+    for layer in range(layers):
+        per_head = jnp.stack([dt_bias[layer], log_decay[layer], skip_gain[layer]])
+        flat = [conv_weight[layer], conv_bias[layer], gate_gain[layer], in_parts(per_head)]
+        flat = as_rows(jnp.concatenate([v.reshape(-1) for v in flat]), weight_rows)
+        small.append(jnp.concatenate([norm_gain[layer][:, None], flat], axis=1))
+    extras = small[0].shape[1]
+    def part(values, i):
+        return values[i * part_rows : (i + 1) * part_rows]
+
+    places = [part(place, i) for i in range(PARTS)]
+    arrived = to_team(hidden, weight_rows)
+    sent_in = to_members(in_columns(in_weight[0], team, small[0]))
+    pieces = [out_weight[layer].T.reshape(-1, team, width) for layer in range(layers)]
+    pieces += [in_columns(in_weight[layer], team, small[layer]) for layer in range(1, layers)]
+    blocks = to_members(after(jnp.concatenate(pieces, axis=2), sent_in))
+    gathered, came = team_gather(jnp.concatenate(arrived))
+    w_cols = [ring_gather(sent_in, (blocks, came, gathered))]
+    everything = [gathered[at] for at in places]
+    w_out = [plane_gather(blocks[:, :width])]
+    arrived_out = to_team(after(cotangent, everything[0]), weight_rows)
+    gout_gathered, came_out = team_gather(jnp.concatenate(arrived_out))
+    cols = sent_in.shape[1]
+    for layer in range(1, layers):
+        start = layers * width + (layer - 1) * cols
+        w_cols.append(plane_gather(after(blocks[:, start : start + cols], gathered)))
+        block = blocks[:, layer * width : (layer + 1) * width]
+        w_out.append(plane_gather(after(block, everything[0])))
+
+    def own_columns(values):
         return lax.dynamic_slice_in_dim(values, member * width, width, values.ndim - 1)
 
-    tables = []
-    for layer in range(layers):
+    def tables_of(tile):
+        spare = tile.astype(f32).T[heads : heads + extras]
+        gain = spare[0]
+        flat = spare[1:].reshape(extras - 1, -1, weight_rows).transpose(1, 0, 2)
+        flat = flat.reshape(-1, DEPTH, 2, across, weight_rows * (extras - 1))
+        heads_flat = flat[0, :, 0, :, (CONV + 1) * wide + gate_wide :][:, :, : 9 * head_wide]
+        per_head = jnp.sum(heads_flat.astype(f32).reshape(-1, 3, 3, head_wide), axis=1)
+        per_head = per_head.transpose(1, 0, 2).reshape(3, -1)
+        own_heads = lax.dynamic_slice_in_dim(per_head, member * heads, heads, 1)
+        flat = flat.transpose(0, 2, 1, 3, 4).reshape(-1, weight_rows * (extras - 1)).astype(f32)
+        taps = flat[:, : CONV * wide].reshape(-1, CONV, wide).transpose(1, 0, 2).reshape(CONV, -1)
+        shift = flat[:, CONV * wide : (CONV + 1) * wide].reshape(1, -1)
+        ggain = flat[:, (CONV + 1) * wide : (CONV + 1) * wide + gate_wide].reshape(1, -1)
         cw = jnp.concatenate(
             [
-                mine(taps[layer, :, :DI]),
-                mine(shift[layer, None, :DI]),
-                jnp.repeat(own_heads[2, layer], HEAD)[None],
-                mine(ggain[layer, None]),
+                own_columns(taps[:, :DI]),
+                own_columns(shift[:, :DI]),
+                jnp.repeat(own_heads[2], HEAD)[None],
+                own_columns(ggain),
                 jnp.zeros((1, width), f32),
             ]
         )
-        cbc = jnp.concatenate(
-            [taps[layer, :, DI:], shift[layer, None, DI:], jnp.zeros((3, 2 * N), f32)]
-        )
-        hp = jnp.stack([own_heads[0, layer], -jnp.exp(own_heads[1, layer])])
-        tables.append((cw, cbc, jnp.pad(hp, ((0, 6), (0, LANES - heads)))))
-
-    def packed(rows):
-        gathered = team_gather(to_team(rows)).reshape(tokens, -1)
-        return gathered[place]
-
-    def part(values, i):
-        return values[i * part_rows : (i + 1) * part_rows]
-
-    def own_of(values):
-        return lax.dynamic_slice_in_dim(values, member * own_rows, own_rows, 0)
+        cbc = jnp.concatenate([taps[:, DI:], shift[:, DI:], jnp.zeros((3, 2 * N), f32)])
+        hp = jnp.stack([own_heads[0], -jnp.exp(own_heads[1])])
+        return gain, (cw, cbc, jnp.pad(hp, ((0, 6), (0, LANES - heads))))
 
     def facts(i):
         count = part_rows // CHUNK
         return part(meta, i), segrow[i * count : (i + 1) * count]
 
-    everything = packed(hidden)
-    states = [own_of(part(everything, i)).astype(f32) for i in range(PARTS)]
+    def own_first(values):
+        start = 0 if paired() else member * own_rows
+        return lax.dynamic_slice_in_dim(values, start, own_rows, 0)
+
+    states = [own_first(everything[i]).astype(f32) for i in range(PARTS)]
     record = []
-    no_halo = jnp.zeros((16, 2 * width + 2 * N + LANES), bf16)
+    last = []
+
+    def turn(value, *needed):
+        return after(value, *last, *needed)
+
+    def done(value):
+        last[:] = [value]
+        return value
+
+    ready, needed = tuple(arrived_out), ()
+    tables, gains, own_normed, gathered_rows = [], [], [None] * PARTS, [None] * PARTS
+
+    def normed_rows(rows, gain, *before):
+        rows = after(rows, *before)
+        return (rows * row_scale(rows) * gain).astype(bf16)
+
     for layer in range(layers):
+        gain, table = tables_of(turn(w_cols[layer][:, step_at:]))
+        gains.append(gain)
+        tables.append(table)
         kept = []
         state = jnp.zeros((N, width), f32)
-        halo = no_halo
+        before = None
         for i in range(PARTS):
             rows = states[i]
             if layer == 0:
-                every = part(everything, i).astype(f32)
-                normed = (every * row_scale(every) * ngain[layer]).astype(bf16)
+                normed = normed_rows(everything[i].astype(f32), gain)
             else:
-                normed = (rows * row_scale(rows) * ngain[layer]).astype(bf16)
-                normed = team_gather(normed).reshape(part_rows, -1)
-            proj = jnp.dot(normed, w_cols[layer], preferred_element_type=f32).astype(bf16)
+                normed = gathered_rows[i]
+            proj = jnp.dot(turn(normed), w_cols[layer], preferred_element_type=f32).astype(bf16)
+            done(proj)
+            before = proj if before is None else before
             mix, gated, squares, starts, state = mixer_forward(
-                proj, halo, *facts(i), *tables[layer], state
+                perm, turn(proj, *ready), before, *facts(i), *table, state
             )
-            partial = dot_nt(gated, w_out[layer]).astype(bf16)
-            branch = team_reduce(partial.reshape(team, own_rows, -1), bf16)
-            total = team_reduce(jnp.sum(squares, axis=1).reshape(team, own_rows), f32)
+            done(gated)
+            partial = done(dot_nt(turn(gated, *needed), w_out[layer]).astype(bf16))
+            total, sent_total, far_total = team_reduce(jnp.sum(squares, axis=1), own_rows, f32)
+            branch, sent, far = team_reduce(partial, own_rows, bf16, (far_total,))
             factor = lax.rsqrt(total / DI + EPS)
             states[i] = rows + branch * factor[:, None]
-            kept.append((rows, normed, proj, halo, mix, starts, branch.astype(bf16), factor))
-            halo = proj[part_rows - 16 :]
+            ready, needed = (sent,), (far,)
+            if layer + 1 < layers:
+                later = tables_of(w_cols[layer + 1][:, step_at:])[0]
+                own_normed[i] = normed_rows(states[i], later, *own_normed[:i])
+                gathered_rows[i], _ = team_gather(own_normed[i])
+                needed = (own_normed[i],)
+            if layer == 0 and i == 0:
+                ready += (came_out,)
+            if layer == 0 and i == PARTS - 1:
+                rows_at = turn(gout_gathered)
+                gout_parts = [rows_at[at] for at in places]
+                ready += tuple(gout_parts)
+            kept.append((rows, normed, proj, before, mix, starts, branch.astype(bf16), factor, gated))
+            before = proj
         record.append(kept)
 
-    def dealt(parts):
-        whole = [team_gather(p.astype(bf16)).reshape(part_rows, -1) for p in parts]
-        whole = jnp.concatenate(whole) if PARTS > 1 else whole[0]
-        return from_team(whole[order[own_dealt]])
-
-    block_out = dealt(states)
-    gout_whole = packed(cotangent)
-    grads_rows = [own_of(part(gout_whole, i)).astype(f32) for i in range(PARTS)]
-    results = [None] * layers
-    small = [None] * layers
-    for layer in reversed(range(layers)):
-        dstate = jnp.zeros((N, width), f32)
-        tail_x = jnp.zeros((3, 8, width), f32)
-        tail_bc = jnp.zeros((3, 8, 2 * N), f32)
-        gathered, sums = [None] * PARTS, None
-        for i in reversed(range(PARTS)):
-            rows, normed, proj, halo, mix, starts, branch, factor = record[layer][i]
-            gout = grads_rows[i].astype(bf16)
-            inner = jnp.sum(gout.astype(f32) * branch.astype(f32), axis=1)
-            scales = jnp.stack([factor, factor * factor * factor * inner / DI])
-            scales = team_gather(scales).transpose(0, 2, 1).reshape(part_rows, 2)
-            if layer == layers - 1:
-                gout_all = part(gout_whole, i)
-            else:
-                gout_all = team_gather(gout).reshape(part_rows, -1)
-            up = jnp.dot(gout_all, w_out[layer], preferred_element_type=f32).astype(bf16)
-            gproj, normed2, acc, acc_bc, acc_h, dstate, tail_x, tail_bc = mixer_backward(
-                proj,
-                halo,
-                *facts(i),
-                *tables[layer],
-                mix,
-                up,
-                jnp.pad(scales, ((0, 0), (0, 6))),
-                starts,
-                dstate,
-                tail_x,
-                tail_bc,
-            )
-            partial = dot_nt(gproj, w_cols[layer]).astype(bf16)
-            gnormed = team_reduce(partial.reshape(team, own_rows, -1), bf16)
-            scale = row_scale(rows)
-            pulled = gnormed * ngain[layer]
-            back = jnp.mean(pulled * rows, axis=1, keepdims=True)
-            grads_rows[i] = grads_rows[i] + scale * pulled - rows * (scale * scale * scale * back)
-            gathered[i] = (normed, gproj, gout_all, normed2)
-            found = (acc, acc_bc, acc_h)
-            sums = found if sums is None else tuple(a + b for a, b in zip(sums, found))
-        if PARTS > 1:
-            whole = [jnp.concatenate([g[k] for g in gathered]) for k in range(4)]
-        else:
-            whole = gathered[0]
-        grad_out = from_heads(dot_tn(whole[2], whole[3]).astype(bf16))
-        split = from_heads(dot_tn(whole[0], whole[1]).astype(bf16)).astype(f32)
-        count = split.shape[0]
-        bc_at = 2 * width
-        step_at = bc_at + 2 * N
-        grad_in = jnp.concatenate(
-            [
-                split[:, :, :width].reshape(count, DI),
-                split[:, :, width:bc_at].reshape(count, DI),
-                jnp.sum(split[:, :, bc_at:step_at], axis=1),
-                split[:, :, step_at : step_at + heads].reshape(count, team * heads),
-            ],
-            axis=1,
-        )
-        grad_norm = jnp.sum(grad_in * in_weight[layer].astype(f32), axis=1) / (
-            norm_gain[layer].astype(f32)
-        )
-        results[layer] = (grad_norm, grad_in, grad_out.astype(f32).reshape(count, DI).T)
+    def with_small(sum_in, sums, layer):
         acc, acc_bc, acc_h = sums
         taps_full = jnp.zeros((CONV + 1, DI + 2 * N), f32)
         taps_full = lax.dynamic_update_slice(taps_full, acc[: CONV + 1], (0, member * width))
         taps_full = lax.dynamic_update_slice(taps_full, acc_bc[: CONV + 1], (0, DI))
         gate_full = lax.dynamic_update_slice(jnp.zeros((DI,), f32), acc[6], (member * width,))
-        spread_out = jnp.concatenate(
-            [
-                taps_full.reshape(CONV + 1, -1, wide).transpose(1, 0, 2).reshape(-1, (CONV + 1) * wide),
-                gate_full.reshape(-1, gate_gain.shape[1]),
-            ],
-            axis=1,
-        )
         head_sums = jnp.stack(
             [
                 acc_h[0, :heads],
@@ -846,28 +1035,166 @@
         head_full = lax.dynamic_update_slice(
             jnp.zeros((3, team * heads), f32), head_sums, (0, member * heads)
         )
-        small[layer] = (spread_out, head_full)
-    grad_hidden = dealt(grads_rows).astype(f32)
-    every_axis = ("y", "core", "z", "x")
-    spread_sum = lax.psum_scatter(
-        jnp.stack([s[0] for s in small], axis=1), every_axis, scatter_dimension=0, tiled=False
-    )
-    head_sum = lax.psum(jnp.stack([s[1] for s in small]), every_axis)
-    here = dt_bias.shape[1]
-    head_own = lax.dynamic_slice_in_dim(head_sum, (z * across + x) * here, here, 2)
-    grad_taps = spread_sum[:, : CONV * wide].reshape(layers, CONV, wide)
+        head_full = head_full.reshape(3, -1, head_wide).transpose(1, 0, 2).reshape(-1, 3 * head_wide)
+        owners = 2 * lax.axis_size("y")
+        flat = jnp.concatenate(
+            [
+                taps_full.reshape(CONV + 1, -1, wide).transpose(1, 0, 2).reshape(-1, (CONV + 1) * wide),
+                gate_full.reshape(-1, gate_wide),
+                jnp.tile(head_full, (owners, 1)),
+            ],
+            axis=1,
+        )
+        flat = as_rows(to_plane(flat, 0), weight_rows)
+        spare = flat.shape[-1]
+        flat = flat.reshape(-1, spare).astype(bf16)
+        tile = jnp.concatenate(
+            [
+                sum_in[:, step_at:extra_at],
+                flat,
+                jnp.zeros((flat.shape[0], LANES - heads - spare), bf16),
+            ],
+            axis=1,
+        )
+        return lax.dynamic_update_slice(sum_in, tile, (0, step_at))
+
+    def picked(parts):
+        return jnp.concatenate(parts)[own_place].reshape(2, rows_here, -1)
+
+    grads_rows = [own_first(gout_parts[i]).astype(f32) for i in range(PARTS)]
+
+    def gather_rows(values):
+        return team_gather(values[None])[0].reshape(part_rows)
+
+    factors = [[gather_rows(record[layer][i][7]) for i in range(PARTS)] for layer in range(layers)]
+
+    def scales_of(layer, i):
+        branch, factor = record[layer][i][6:8]
+        inner = jnp.sum(grads_rows[i].astype(bf16).astype(f32) * branch.astype(f32), axis=1)
+        pulls = gather_rows(factor * factor * factor * inner / DI)
+        return jnp.pad(jnp.stack([factors[layer][i], pulls], axis=1), ((0, 0), (0, 6)))
+
+    def pull_in(layer, i, gout, scales, *needed):
+        up = done(jnp.dot(turn(gout), w_out[layer], preferred_element_type=f32).astype(bf16))
+        rows, normed, proj, before, mix, starts = record[layer][i][:6]
+        found = mixer_backward(
+            perm, proj, before, *facts(i), *tables[layer], mix, turn(up, *needed), scales, starts, *carry[0]
+        )
+        done(found[0])
+        carry[0] = found[4:]
+        carry[1] = found[1:4] if carry[1] is None else tuple(a + b for a, b in zip(carry[1], found[1:4]))
+        return found[0]
+
+    def send_back(layer, gproj, *needed):
+        partial = done(dot_nt(turn(gproj, *needed), w_cols[layer]).astype(bf16))
+        return team_reduce(partial, own_rows, bf16)
+
+    def add_in(layer, i, gproj, total, *needed):
+        term = dot_tn(record[layer][i][1], turn(gproj, *needed))
+        return done((term if total is None else term + total.astype(f32)).astype(bf16))
+
+    def add_out(layer, i, gout, total, *needed):
+        scaled = record[layer][i][8].astype(f32) * factors[layer][i][:, None]
+        term = dot_tn(turn(gout, *needed), scaled.astype(bf16))
+        return done((term if total is None else term + total.astype(f32)).astype(bf16))
+
+    def step_back(layer, i, gnormed):
+        rows = record[layer][i][0]
+        scale = row_scale(rows)
+        pulled = gnormed * gains[layer]
+        back = jnp.mean(pulled * rows, axis=1, keepdims=True)
+        return grads_rows[i] + scale * pulled - rows * (scale * scale * scale * back)
+
+    def plane_sum(values):
+        return lax.psum_scatter(values, ("y", "z"), scatter_dimension=0, tiled=True)
+
+    carry = [None, None]
+    splits, outs = [None] * layers, [None] * layers
+    gouts = list(gout_parts)
+    top = layers - 1
+    sum_out = None
+    for i in reversed(range(PARTS)):
+        sum_out = add_out(top, i, gouts[i], sum_out)
+    sum_out_done = plane_sum(sum_out)
+    outs[top] = from_plane(sum_out_done)
+    scales = [scales_of(top, i) for i in range(PARTS)]
+    sent, pending = (), None
+    out_parts = [None] * PARTS
+
+    def catch_up(pending, *started):
+        layer, i, gnormed = pending
+        grads_rows[i] = step_back(layer, i, after(gnormed, *started))
+        own = grads_rows[i].astype(bf16)
+        if layer > 0:
+            next_gouts[i] = team_gather(own)
+            next_scales[i] = scales_of(layer - 1, i)
+        else:
+            last_rows_of[i] = team_gather(own)
+        return (own,)
+
+    last_rows_of = [None] * PARTS
+    next_gouts, next_scales = gouts, scales
+    for layer in reversed(range(layers)):
+        carry[:] = [
+            (jnp.zeros((N, width), f32), jnp.zeros((3, 8, width), f32), jnp.zeros((3, 8, 2 * N), f32)),
+            None,
+        ]
+        sum_in, sum_out, kept = None, None, [None] * PARTS
+        if layer == top:
+            next_gouts, next_scales = [None] * PARTS, [None] * PARTS
+        for i in reversed(range(PARTS)):
+            if layer < top:
+                gouts[i], scales[i] = next_gouts[i][0], next_scales[i]
+            gproj = pull_in(layer, i, gouts[i], scales[i], *sent)
+            kept[i] = gproj
+            needed = catch_up(pending, gproj) if pending is not None else ()
+            if layer == top:
+                out_parts[i], came = team_gather(after(states[i].astype(bf16), gproj))
+                if i + 1 < PARTS:
+                    needed += (out_parts[i + 1],)
+            if layer == 0 and i == 0:
+                sum_in = add_in(layer, i, gproj, sum_in, *needed, *splits[1:], *outs[1:])
+                sum_in = done(with_small(sum_in, carry[1], layer))
+                splits[layer] = plane_sum(sum_in)
+            gnormed, near, far = send_back(layer, gproj, *needed)
+            sent, pending = (near,), (layer, i, gnormed)
+            if layer == 0 and i > 0:
+                sum_out = add_out(layer, i, gouts[i], sum_out)
+                sum_in = add_in(layer, i, gproj, sum_in, next_gouts[i - 1][1])
+                sum_out = add_out(layer, i - 1, next_gouts[i - 1][0], sum_out)
+                summed_out = plane_sum(sum_out)
+        if layer > 0:
+            for i in reversed(range(PARTS)):
+                wait = (next_gouts[i + 1][1], sum_out_done) if i + 1 < PARTS else ()
+                sum_in = add_in(layer, i, kept[i], sum_in, *wait)
+            sum_in = done(with_small(sum_in, carry[1], layer))
+            splits[layer] = from_plane(plane_sum(sum_in))
+        else:
+            outs[layer] = from_plane(summed_out)
+    block_out = from_team(picked([after(p, *last) for p in out_parts]))
+    catch_up(pending)
+    rows = picked([p[0] for p in last_rows_of])
+    block_out = dealt(block_out, weight_rows, bf16)
+    grad_hidden = dealt(from_team(rows), weight_rows, f32)
+    splits[0] = from_plane(after(splits[0], block_out, grad_hidden))
+    grad_out = assemble_out(outs).transpose(0, 2, 1)
+    grad_in, products, tiles = assemble_in(splits, in_weight)
+    spare = extras - 1
+    sums = jnp.sum(tiles, axis=1).transpose(0, 2, 1)[:, heads : heads + spare].reshape(layers, -1)
+    shift_at, gate_at, head_at = CONV * wide, (CONV + 1) * wide, (CONV + 1) * wide + gate_wide
+    grad_heads = sums[:, head_at : head_at + 3 * head_wide].reshape(layers, 3, head_wide)
     return (
         block_out,
         grad_hidden,
-        jnp.stack([r[0] for r in results]),
-        jnp.stack([r[1] for r in results]),
-        grad_taps,
-        spread_sum[:, CONV * wide : (CONV + 1) * wide],
-        head_own[:, 0],
-        head_own[:, 1],
-        head_own[:, 2],
-        spread_sum[:, (CONV + 1) * wide :],
-        jnp.stack([r[2] for r in results]),
+        products[:, :, 0] / norm_gain.astype(f32),
+        grad_in,
+        sums[:, :shift_at].reshape(layers, CONV, wide),
+        sums[:, shift_at:gate_at],
+        grad_heads[:, 0],
+        grad_heads[:, 1],
+        grad_heads[:, 2],
+        sums[:, gate_at:head_at],
+        grad_out,
     )
 
 

time: 1930 us -> 1600 us (0.83)
  blocking collectives: 334 us -> 0 us
  waiting for transfers between devices: 556 us -> 378 us
  starting transfers between devices: 89.6 us -> 200 us
  matrix products: 242 us -> 282 us
  Pallas kernels: 279 us -> 316 us
    all_gather x2 -> x0, blocking collectives: 208 us -> none  [the longest x1 129 us: per_device(): lax.all_gather(flat, ('y', 'core', 'z', 'x'), axis=0).transpose(1, 0, 2)]
    another operation x56 -> x13, other arithmetic: 130 us -> 0.31 us  [the longest x39 113 us: in_order(): jnp.stack([jnp.where(first, mine, theirs), jnp.where(first, theirs, mine)])]
    reduce_scatter x4, waiting for transfers between devices: 166 us -> 39.8 us  [plane_sum(): return lax.psum_scatter(values, ('y', 'z'), scatter_dimension=0, tiled=True)]
    psum x1 -> x0, blocking collectives: 93.3 us -> none  [per_device(): head_sum = lax.psum(jnp.stack([s[1] for s in small]), every_axis)]
    concatenate x1 -> x35, other arithmetic: 0.07 us -> 83.1 us  [the longest x8 36.8 us: team_gather(): return (jnp.concatenate([row, swap(row, 'core')]), came)]
    ppermute x38 -> x77, waiting for transfers between devices: 378 us -> 313 us  [the longest x62 226 us: swap(): return lax.ppermute(value, axis, SWAP)]
    ppermute x38 -> x77, starting transfers between devices: 64.9 us -> 129 us  [the longest x62 65.1 us: swap(): return lax.ppermute(value, axis, SWAP)]
    reshape x22 -> x26, local copies, waits for them, and re-layouts: 55.7 us -> 7.98 us  [the longest x1 2.4 us: to_members(): return sent.reshape(-1, pieces.shape[2])]
  transfers between devices with their start and end apart: 53 -> 90, of which waited for: 22 -> 35; matrix products, arithmetic and copies ran while one was open for 28% -> 35% of each run, Pallas kernels for 10% -> 17%
where the time goes in v2:
time: 1600 us; the launch traced here: 1590 us
  waiting for transfers between devices  378 us (24%)
  Pallas kernels  316 us (20%)
  matrix products  282 us (18%)
  local copies, waits for them, and re-layouts  208 us (13%)
  starting transfers between devices  200 us (12%)
  other arithmetic  172 us (11%)
  between operations  29 us (2%)
    ppermute x62, waiting for transfers between devices, swap(): return lax.ppermute(value, axis, SWAP)  226 us
    pallas_call x4, Pallas kernels, mixer_backward(): pl.pallas_call(backward_kernel, grid_spec=pltpu.PrefetchScalarGridSpec(nu...  198 us
    pallas_call x4, Pallas kernels, mixer_forward(): pl.pallas_call(forward_kernel, grid_spec=pltpu.PrefetchScalarGridSpec(num...  97.7 us
    dot_general x8, matrix products, dot_tn(): lax.dot_general(a, b, (((0,), (0,)), ((), ())), preferred_element_type=jn...  95.6 us
    dot_general x8, matrix products, dot_nt(): lax.dot_general(a, b, (((1,), (1,)), ((), ())), preferred_element_type=jn...  89.3 us
    ppermute x62, starting transfers between devices, swap(): return lax.ppermute(value, axis, SWAP)  65.1 us
    all_to_all x4, starting transfers between devices, from_plane(): lax.all_to_all(blocks, ('core', 'x'), split_axis=0, concat_axis=0, tiled=...  62.2 us
    dot_general x4, matrix products, per_device(): jnp.dot(turn(normed), w_cols[layer], preferred_element_type=f32)  60 us
  transfers between devices with their start and end apart: 90, of which 35 were waited for; matrix products, arithmetic and copies ran while one was open for 35% of the time, Pallas kernels for 17%

profile of v2, /device:TPU:0, one launch (start us, length us, event | category | flops | bytes accessed | tf_op | source)
XLA Modules:
  0.0 1585.4 jit_solution(17208553527725723351)
XLA Ops:
  74.8 9.7 collective-permute-done.1
  98.8 25.5 %collective-permute-done.2 = bf16[512,2048]{1,0:T(8,128)(2,1)} collective-permute-done((bf16[512,2048]{1,0:T(8,128)(2,1)}, bf16[512,2048]{1,0:T(8,128)(2,1)}, u32[]{:S(2)}, u32[]{:S(2)}) %collective-permute-start.2) | collective-permute-done | bytes 2097184 | tf_op jit(solution)/shard_map/ppermute | solution.py:521
  128.0 12.3 collective-permute-start.3
  142.5 42.1 %collective-permute-start.7 = (bf16[256,2432]{1,0:T(8,128)(2,1)}, bf16[256,2432]{1,0:T(8,128)(2,1)}, u32[]{:S(2)}, u32[]{:S(2)}) collective-permute-start(bf16[256,2432]{1,0:T(8,128)(2,1)} %collective-permute-done.5), channel_id=1, source_target_pairs={{0,2},{2,4},{4,6},{6,22},{22,20},{20,18},{18,16},{16,0},{1,3},{3,5... | collective-permute-start | bytes 3735560 | tf_op jit(solution)/shard_map/ppermute | solution.py:594
  196.2 25.5 %collective-permute-done.8 = bf16[256,2432]{1,0:T(8,128)(2,1)} collective-permute-done((bf16[256,2432]{1,0:T(8,128)(2,1)}, bf16[256,2432]{1,0:T(8,128)(2,1)}, u32[]{:S(2)}, u32[]{:S(2)}) %collective-permute-start.8) | collective-permute-done | bytes 1245216 | tf_op jit(solution)/shard_map/ppermute | solution.py:597
  240.0 10.9 collective-permute-done.10
  256.8 8.5 pad_maximum_fusion
  267.1 13.3 gather_fusion
  280.4 13.3 gather_fusion.1
  293.7 6.6 convert_element_type.450
  321.0 8.7 multiply_convert_fusion.1
  329.7 16.7 %convolution_convert_fusion.5.gate_ref.x_ref.bc_ref.st_ref.hx_ref.hbc_ref.px_ref.pbc_ref = bf16[1024,2432]{1,0:T(8,128)(2,1)} fusion(bf16[1024,2048]{1,0:T(8,128)(2,1)S(1)} %get-tuple-element.261, bf16[2048,2432]{0,1:T(8,128)(2,1)} %constant_dynamic-update-slice_fusion), kind=kOutput, calls=%fused_computation.25 | convolution fusion | flops 10203037696 | bytes 19136512 | tf_op jit(solution)/shard_map/dot_general | solution.py:994
  355.4 24.3 %mix_fwd.4 = (bf16[1024,1024]{1,0:T(8,128)(2,1)}, bf16[1024,1024]{1,0:T(8,128)(2,1)}, f32[1024,128]{1,0:T(8,128)S(1)}, f32[4,128,1024]{2,1,0:T(8,128)}, f32[128,1024]{1,0:T(8,128)S(1)}) custom-call(s32[4]{0:T(128)S(1)} %add_xor_fusion.perm_ref, bf16[1024,2432]{1,0:T(8,128)(2,1)} %convolution_convert_fusion.5.gate_ref.x_ref.bc_ref.st_ref.hx_ref.hbc_ref.px_ref.pbc_ref, ...), custom_call_target="tpu_custom_call" | custom-call | flops 29360128000 | bytes 12582912 | tf_op jit(solution)/shard_map/mix_fwd/pallas_call | solution.py:194
  379.9 16.9 %collective-permute-start.16 = (f32[512]{0:T(512)S(1)}, f32[512]{0:T(512)S(1)}, u32[]{:S(2)}, u32[]{:S(2)}) collective-permute-start(f32[512]{0:T(512)S(1)} %slice.578), channel_id=1, source_target_pairs={{0,8},{8,0},{1,9},{9,1},{2,10},{10,2},{3,11},{11,3},{4,12},{12,4},... | collective-permute-start | bytes 6152 | tf_op jit(solution)/shard_map/ppermute | solution.py:521
  402.9 7.4 convolution_convert_fusion.15
  414.0 15.2 convolution_convert_fusion.4.gate_ref.x_ref.bc_ref.st_ref.px_ref.pbc_ref
  429.2 19.8 %collective-permute-done.21 = bf16[512,2048]{1,0:T(8,128)(2,1)} collective-permute-done((bf16[512,2048]{1,0:T(8,128)(2,1)}, bf16[512,2048]{1,0:T(8,128)(2,1)}, u32[]{:S(2)}, u32[]{:S(2)}) %collective-permute-start.21) | collective-permute-done | bytes 2097184 | tf_op jit(solution)/shard_map/ppermute | solution.py:521
  455.0 24.6 %mix_fwd.5 = (bf16[1024,1024]{1,0:T(8,128)(2,1)}, bf16[1024,1024]{1,0:T(8,128)(2,1)}, f32[1024,128]{1,0:T(8,128)S(1)}, f32[4,128,1024]{2,1,0:T(8,128)}, f32[128,1024]{1,0:T(8,128)}) custom-call(s32[4]{0:T(128)S(1)} %add_xor_fusion.perm_ref, bf16[1024,2432]{1,0:T(8,128)(2,1)} %convolution_convert_fusion.4.gate_ref.x_ref.bc_ref.st_ref.px_ref.pbc_ref, ...), custom_call_target="tpu_custom_call" | custom-call | flops 29360128000 | bytes 12582912 | tf_op jit(solution)/shard_map/mix_fwd/pallas_call | solution.py:194
  499.0 14.3 collective-permute-done.24
  513.3 8.3 pad_maximum_fusion.1
  535.5 13.5 gather_fusion.3
  549.0 13.3 gather_fusion.2
  571.4 12.8 convolution_convert_fusion.3.gate_ref.x_ref.bc_ref.st_ref.hx_ref.hbc_ref.px_ref.pbc_ref
  584.2 24.3 %mix_fwd.6 = (bf16[1024,1024]{1,0:T(8,128)(2,1)}, bf16[1024,1024]{1,0:T(8,128)(2,1)}, f32[1024,128]{1,0:T(8,128)S(1)}, f32[4,128,1024]{2,1,0:T(8,128)}, f32[128,1024]{1,0:T(8,128)S(1)}) custom-call(s32[4]{0:T(128)S(1)} %add_xor_fusion.perm_ref, bf16[1024,2432]{1,0:T(8,128)(2,1)} %convolution_convert_fusion.3.gate_ref.x_ref.bc_ref.st_ref.hx_ref.hbc_ref.px_ref.pbc_ref, ...), custom_call_target="tpu_custom_call" | custom-call | flops 29360128000 | bytes 12582912 | tf_op jit(solution)/shard_map/mix_fwd/pallas_call | solution.py:194
  608.5 7.5 convolution_convert_fusion.13
  632.5 15.3 convolution_convert_fusion.2.gate_ref.x_ref.bc_ref.st_ref.px_ref.pbc_ref
  647.8 24.6 %mix_fwd.7 = (bf16[1024,1024]{1,0:T(8,128)(2,1)}, bf16[1024,1024]{1,0:T(8,128)(2,1)}, f32[1024,128]{1,0:T(8,128)S(1)}, f32[4,128,1024]{2,1,0:T(8,128)}, f32[128,1024]{1,0:T(8,128)}) custom-call(s32[4]{0:T(128)S(1)} %add_xor_fusion.perm_ref, bf16[1024,2432]{1,0:T(8,128)(2,1)} %convolution_convert_fusion.2.gate_ref.x_ref.bc_ref.st_ref.px_ref.pbc_ref, ...), custom_call_target="tpu_custom_call" | custom-call | flops 29360128000 | bytes 12582912 | tf_op jit(solution)/shard_map/mix_fwd/pallas_call | solution.py:194
  672.4 6.8 convolution_convert_fusion.12
  695.1 19.7 %collective-permute-done.37 = f32[1,256]{1,0:T(1,128)S(1)} collective-permute-done((f32[1,256]{1,0:T(1,128)S(1)}, f32[1,256]{1,0:T(1,128)S(1)}, u32[]{:S(2)}, u32[]{:S(2)}) %collective-permute-start.37) | collective-permute-done | bytes 1056 | tf_op jit(solution)/shard_map/ppermute | solution.py:521
  724.5 7.7 convolution_convert_fusion.11
  732.3 6.8 add_convert_fusion.3
  739.0 9.3 convolution_convert_fusion.19.u_ref
  748.4 49.3 %mix_bwd.4 = (bf16[1024,2432]{1,0:T(8,128)(2,1)}, f32[8,1024]{1,0:T(8,128)S(1)}, f32[8,256]{1,0:T(8,128)S(1)}, f32[8,128]{1,0:T(8,128)S(1)}, f32[128,1024]{1,0:T...) custom-call(s32[4]{0:T(128)S(1)} %add_xor_fusion.perm_ref, ...), custom_call_target="tpu_custom_call" | custom-call | flops 58720256000 | bytes 25165824 | tf_op jit(solution)/shard_map/mix_bwd/pallas_call | solution.py:426
  797.7 15.5 convolution_convert_fusion.9
  822.0 9.4 convolution_convert_fusion.18.u_ref
  832.9 49.6 %mix_bwd.5 = (bf16[1024,2432]{1,0:T(8,128)(2,1)}, f32[8,1024]{1,0:T(8,128)S(1)}, f32[8,256]{1,0:T(8,128)S(1)}, f32[8,128]{1,0:T(8,128)S(1)}, f32[128,1024]{1,0:T...) custom-call(s32[4]{0:T(128)S(1)} %add_xor_fusion.perm_ref, ...), custom_call_target="tpu_custom_call" | custom-call | flops 58720256000 | bytes 25165824 | tf_op jit(solution)/shard_map/mix_bwd/pallas_call | solution.py:426
  890.8 24.0 %collective-permute-done.49 = bf16[256,2048]{1,0:T(8,128)(2,1)} collective-permute-done((bf16[256,2048]{1,0:T(8,128)(2,1)S(1)}, bf16[256,2048]{1,0:T(8,128)(2,1)}, u32[]{:S(2)}, u32[]{:S(2)}) %collective-permute-start.49) | collective-permute-done | bytes 1048608 | tf_op jit(solution)/shard_map/ppermute | solution.py:521
  926.3 16.6 %convolution_convert_fusion.8 = bf16[1024,2048]{1,0:T(8,128)(2,1)} fusion(bf16[1024,2432]{1,0:T(8,128)(2,1)} %get-tuple-element.171, bf16[2048,2432]{1,0:T(8,128)(2,1)} %all-gather.6.cloned.1.call-done), kind=kOutput, calls=%fused_computation.40 | convolution fusion | flops 10202644480 | bytes 19136512 | tf_op jit(solution)/shard_map/dot_general | solution.py:32
  943.0 15.7 convolution_convert_fusion.1
  958.6 39.8 %reduce-scatter.5.cloned.1.call-done = bf16[256,1024]{1,0:T(8,128)(2,1)} async-done(((bf16[2048,1024]{1,0:T(8,128)(2,1)}), bf16[256,1024]{1,0:T(8,128)(2,1)}) %reduce-scatter.5.cloned.1.call-update) | async-done | bytes 524304 | tf_op jit(solution)/shard_map/reduce_scatter | solution.py:1109
  998.4 18.0 %add_convert_fusion.1 = bf16[2048,2432]{1,0:T(8,128)(2,1)} fusion(bf16[2048,2432]{1,0:T(8,128)(2,1)} %convolution_convert_fusion.1, bf16[1024,2432]{1,0:T(8,128)(2,1)} %get-tuple-element.171, bf16[512,2048]{1,0:T(8,128)(2,1)} %collective-permute-done.20, bf16[512,2048]{1,0:T(8,128)(2,1)S(1)} %copy-done.34), kind=kOutput, calls=%fused_computation.7 | convolution fusion | flops 10223878144 | bytes 29097984 | tf_op jit(solution)/shard_map/dot_general | solution.py:36
  1045.2 9.5 convolution_convert_fusion.17.u_ref
  1058.7 50.0 %mix_bwd.6 = (bf16[1024,2432]{1,0:T(8,128)(2,1)}, f32[8,1024]{1,0:T(8,128)S(1)}, f32[8,256]{1,0:T(8,128)S(1)}, f32[8,128]{1,0:T(8,128)S(1)}, f32[128,1024]{1,0:T...) custom-call(s32[4]{0:T(128)S(1)} %add_xor_fusion.perm_ref, ...), custom_call_target="tpu_custom_call" | custom-call | flops 58720256000 | bytes 25165824 | tf_op jit(solution)/shard_map/mix_bwd/pallas_call | solution.py:426
  1117.9 14.0 convolution_convert_fusion.7
  1133.5 7.4 collective-permute-done.64
  1150.2 15.9 %convolution_convert_fusion = bf16[2048,2432]{1,0:T(8,128)(2,1)} fusion(bf16[1024,2048]{1,0:T(8,128)(2,1)S(1)} %copy-done.53, bf16[1024,2432]{1,0:T(8,128)(2,1)} %get-tuple-element.185), kind=kOutput, calls=%fused_computation.10 | convolution fusion | flops 10205528064 | bytes 19136512 | tf_op jit(solution)/shard_map/dot_general | solution.py:36
  1173.4 6.6 add_convert_fusion.2
  1180.0 9.3 convolution_convert_fusion.16.u_ref
  1189.4 49.6 %mix_bwd.7 = (bf16[1024,2432]{1,0:T(8,128)(2,1)}, f32[8,1024]{1,0:T(8,128)S(1)}, f32[8,256]{1,0:T(8,128)S(1)}, f32[8,128]{1,0:T(8,128)S(1)}, f32[128,1024]{1,0:T...) custom-call(s32[4]{0:T(128)S(1)} %add_xor_fusion.perm_ref, ...), custom_call_target="tpu_custom_call" | custom-call | flops 58720256000 | bytes 25165824 | tf_op jit(solution)/shard_map/mix_bwd/pallas_call | solution.py:426
  1257.0 11.0 all-to-all-done.2.refs_1_
  1267.9 18.6 %add_convert_fusion = bf16[2048,2432]{1,0:T(8,128)(2,1)} fusion(bf16[2048,2432]{1,0:T(8,128)(2,1)} %convolution_convert_fusion, bf16[1024,2048]{1,0:T(8,128)(2,1)} %copy-done.51, bf16[1024,2432]{1,0:T(8,128)(2,1)} %get-tuple-element.202), kind=kOutput, calls=%fused_computation.6 | convolution fusion | flops 10215489536 | bytes 29097984 | tf_op jit(solution)/shard_map/dot_general | solution.py:36
  1288.8 15.1 convolution_convert_fusion.6
  1309.3 24.8 %collective-permute-done.70 = bf16[256,2048]{1,0:T(8,128)(2,1)S(1)} collective-permute-done((bf16[256,2048]{1,0:T(8,128)(2,1)S(1)}, bf16[256,2048]{1,0:T(8,128)(2,1)S(1)}, u32[]{:S(2)}, u32[]{:S(2)}) %collective-permute-start.70) | collective-permute-done | bytes 1048608 | tf_op jit(solution)/shard_map/ppermute | solution.py:521
  1340.8 24.1 %collective-permute-done.46 = bf16[256,2048]{1,0:T(8,128)(2,1)S(1)} collective-permute-done((bf16[256,2048]{1,0:T(8,128)(2,1)S(1)}, bf16[256,2048]{1,0:T(8,128)(2,1)S(1)}, u32[]{:S(2)}, u32[]{:S(2)}) %collective-permute-start.46) | collective-permute-done | bytes 1048608 | tf_op jit(solution)/shard_map/ppermute | solution.py:521
  1365.7 21.7 %collective-permute-done.73 = bf16[256,2048]{1,0:T(8,128)(2,1)S(1)} collective-permute-done((bf16[256,2048]{1,0:T(8,128)(2,1)}, bf16[256,2048]{1,0:T(8,128)(2,1)S(1)}, u32[]{:S(2)}, u32[]{:S(2)}) %collective-permute-start.73) | collective-permute-done | bytes 1048608 | tf_op jit(solution)/shard_map/ppermute | solution.py:521
  1390.3 17.9 %collective-permute-done.71 = bf16[256,2048]{1,0:T(8,128)(2,1)S(1)} collective-permute-done((bf16[256,2048]{1,0:T(8,128)(2,1)S(1)}, bf16[256,2048]{1,0:T(8,128)(2,1)S(1)}, u32[]{:S(2)}, u32[]{:S(2)}) %collective-permute-start.71) | collective-permute-done | bytes 1048608 | tf_op jit(solution)/shard_map/ppermute | solution.py:521
  1415.2 8.6 pad_maximum_fusion.2
  1423.7 8.9 gather_fusion.4
  1437.6 7.1 pad_maximum_fusion.3
  1444.8 8.9 gather_fusion.5
  1462.7 13.7 collective-permute-done.68.second_ref
  1479.7 21.1 %collective-permute-done.76.second_ref = bf16[256,2048]{1,0:T(8,128)(2,1)} collective-permute-done((bf16[256,2048]{1,0:T(8,128)(2,1)}, bf16[256,2048]{1,0:T(8,128)(2,1)}, u32[]{:S(2)}, u32[]{:S(2)}) %collective-permute-start.76) | collective-permute-done | bytes 1048608 | tf_op jit(solution)/shard_map/ppermute | solution.py:650
  1504.6 48.3 %all-to-all-start.4 = ((bf16[4,64,2432]{2,1,0:T(8,128)(2,1)}), bf16[4,64,2432]{2,1,0:T(8,128)(2,1)S(1)}, u32[]{:S(2)}, u32[]{:S(2)}) async-start(bf16[4,64,2432]{2,1,0:T(8,128)(2,1)} %bitcast.277), calls=%async_computation.7 | async-start | bytes 2490368 | tf_op jit(solution)/shard_map/all_to_all | solution.py:714
  1555.4 14.5 all-to-all-done.4.refs_0_
  (782 shorter events, 406.7 us)
Async XLA Ops:
  18.8 28.3 %all-to-all-start = ((bf16[64,4,2432]{2,0,1:T(8,128)(2,1)}), bf16[64,4,2432]{2,0,1:T(8,128)(2,1)S(1)}, u32[]{:S(2)}, u32[]{:S(2)}) async-start(bf16[64,4,2432]{2,0,1:T(8,128)(2,1)} %concatenate.282), calls=%async_computation | async-start | bytes 2490368 | tf_op jit(solution)/shard_map/all_to_all | solution.py:703
  48.8 40.6 %all-to-all-start.1 = ((bf16[64,4,4480]{2,0,1:T(8,128)(2,1)}), bf16[64,4,4480]{2,0,1:T(8,128)(2,1)S(1)}, u32[]{:S(2)}, u32[]{:S(2)}) async-start(bf16[64,4,4480]{2,0,1:T(8,128)(2,1)} %copy.192), calls=%async_computation.1 | async-start | bytes 4587520 | tf_op jit(solution)/shard_map/all_to_all | solution.py:703
  52.6 350.3 %all-gather.4.cloned.1.call-start = ((), (), s32[]{:S(2)}) async-start(), calls=%async_computation.10 | async-start | bytes 4718592 | tf_op jit(solution)/shard_map/all_gather | solution.py:708
  52.7 21.2 %collective-permute-start.14 = (s32[2,1,3]{2,1,0:T(1,128)S(1)}, s32[2,1,3]{2,1,0:T(1,128)S(1)}, u32[]{:S(2)}, u32[]{:S(2)}) collective-permute-start(s32[2,1,3]{2,1,0:T(1,128)S(1)} %copy-done.99), channel_id=1, source_target_pairs={{0,8},{8,0},{1,9},{9,1},{2,10},{10,2},{3,11},{11,3},{4,12},{12,4},... | collective-permute-start | bytes 80 | tf_op jit(solution)/shard_map/ppermute | solution.py:521
  53.2 40.3 %collective-permute-start.4 = (s32[2,1,2048]{2,1,0:T(1,128)}, s32[2,1,2048]{2,1,0:T(1,128)S(1)}, u32[]{:S(2)}, u32[]{:S(2)}) collective-permute-start(s32[2,1,2048]{2,1,0:T(1,128)} %param.17), channel_id=1, source_target_pairs={{0,8},{8,0},{1,9},{9,1},{2,10},{10,2},{3,11},{11,3},{4,12},{12,4},... | collective-permute-start | bytes 49160 | tf_op jit(solution)/shard_map/ppermute | solution.py:521
  56.2 18.5 %collective-permute-start = (bf16[256,2048]{1,0:T(8,128)(2,1)S(1)}, bf16[256,2048]{1,0:T(8,128)(2,1)}, u32[]{:S(2)}, u32[]{:S(2)}) collective-permute-start(bf16[256,2048]{1,0:T(8,128)(2,1)S(1)} %get-tuple-element.110), channel_id=1, source_target_pairs={{0,0},{2,2},{4,8},{6,10},{8,4},{10,6},{12,12},{14,14},{1,1},{3,3},... | collective-permute-start | bytes 3145736 | tf_op jit(solution)/shard_map/ppermute | solution.py:645
  57.9 26.6 %collective-permute-start.1 = (bf16[256,2048]{1,0:T(8,128)(2,1)}, bf16[256,2048]{1,0:T(8,128)(2,1)}, u32[]{:S(2)}, u32[]{:S(2)}) collective-permute-start(bf16[256,2048]{1,0:T(8,128)(2,1)} %get-tuple-element.111), channel_id=1, source_target_pairs={{0,2},{2,0},{4,10},{6,8},{8,6},{10,4},{12,14},{14,12},{1,3},{3,1},... | collective-permute-start | bytes 3145736 | tf_op jit(solution)/shard_map/ppermute | solution.py:645
  87.6 36.7 %collective-permute-start.2 = (bf16[512,2048]{1,0:T(8,128)(2,1)}, bf16[512,2048]{1,0:T(8,128)(2,1)}, u32[]{:S(2)}, u32[]{:S(2)}) collective-permute-start(bf16[512,2048]{1,0:T(8,128)(2,1)} %pad_maximum_fusion.12), channel_id=1, source_target_pairs={{0,1},{1,0},{2,3},{3,2},{4,5},{5,4},{6,7},{7,6},{8,9},{9,8},{10,11... | collective-permute-start | bytes 6291464 | tf_op jit(solution)/shard_map/ppermute | solution.py:521
  90.6 392.9 %all-gather.6.cloned.1.call-start = ((), (), s32[]{:S(2)}) async-start(), calls=%async_computation.11 | async-start | bytes 11206656 | tf_op jit(solution)/shard_map/all_gather | solution.py:708
  94.9 45.6 %collective-permute-start.6 = (bf16[256,2432]{1,0:T(8,128)(2,1)}, bf16[256,2432]{1,0:T(8,128)(2,1)}, u32[]{:S(2)}, u32[]{:S(2)}) collective-permute-start(bf16[256,2432]{1,0:T(8,128)(2,1)} %bitcast.265), channel_id=1, source_target_pairs={{2,0},{4,2},{6,4},{22,6},{20,22},{18,20},{16,18},{0,16},{3,1},{5,3... | collective-permute-start | bytes 3735560 | tf_op jit(solution)/shard_map/ppermute | solution.py:597
  97.0 45.5 %collective-permute-start.5 = (bf16[256,2432]{1,0:T(8,128)(2,1)}, bf16[256,2432]{1,0:T(8,128)(2,1)}, u32[]{:S(2)}, u32[]{:S(2)}) collective-permute-start(bf16[256,2432]{1,0:T(8,128)(2,1)} %bitcast.266), channel_id=1, source_target_pairs={{0,2},{2,4},{4,6},{6,22},{22,20},{20,18},{18,16},{16,0},{1,3},{3,5... | collective-permute-start | bytes 3735560 | tf_op jit(solution)/shard_map/ppermute | solution.py:594
  128.0 128.8 %collective-permute-start.3 = (bf16[1024,2048]{1,0:T(8,128)(2,1)}, bf16[1024,2048]{1,0:T(8,128)(2,1)}, u32[]{:S(2)}, u32[]{:S(2)}) collective-permute-start(bf16[1024,2048]{1,0:T(8,128)(2,1)} %pad_maximum_fusion.4), channel_id=1, source_target_pairs={{0,8},{8,0},{1,9},{9,1},{2,10},{10,2},{3,11},{11,3},{4,12},{12,4},... | collective-permute-start | bytes 12582920 | tf_op jit(solution)/shard_map/ppermute | solution.py:521
  140.5 81.2 %collective-permute-start.8 = (bf16[256,2432]{1,0:T(8,128)(2,1)}, bf16[256,2432]{1,0:T(8,128)(2,1)}, u32[]{:S(2)}, u32[]{:S(2)}) collective-permute-start(bf16[256,2432]{1,0:T(8,128)(2,1)} %collective-permute-done.6), channel_id=1, source_target_pairs={{2,0},{4,2},{6,4},{22,6},{20,22},{18,20},{16,18},{0,16},{3,1},{5,3... | collective-permute-start | bytes 3735560 | tf_op jit(solution)/shard_map/ppermute | solution.py:597
  142.5 79.2 %collective-permute-start.7 = (bf16[256,2432]{1,0:T(8,128)(2,1)}, bf16[256,2432]{1,0:T(8,128)(2,1)}, u32[]{:S(2)}, u32[]{:S(2)}) collective-permute-start(bf16[256,2432]{1,0:T(8,128)(2,1)} %collective-permute-done.5), channel_id=1, source_target_pairs={{0,2},{2,4},{4,6},{6,22},{22,20},{20,18},{18,16},{16,0},{1,3},{3,5... | collective-permute-start | bytes 3735560 | tf_op jit(solution)/shard_map/ppermute | solution.py:594
  221.7 29.2 %collective-permute-start.10 = (bf16[256,2432]{1,0:T(8,128)(2,1)}, bf16[256,2432]{1,0:T(8,128)(2,1)}, u32[]{:S(2)}, u32[]{:S(2)}) collective-permute-start(bf16[256,2432]{1,0:T(8,128)(2,1)} %collective-permute-done.8), channel_id=1, source_target_pairs={{2,0},{4,2},{6,4},{22,6},{20,22},{18,20},{16,18},{0,16},{3,1},{5,3... | collective-permute-start | bytes 3735560 | tf_op jit(solution)/shard_map/ppermute | solution.py:597
  221.7 30.9 %collective-permute-start.9 = (bf16[256,2432]{1,0:T(8,128)(2,1)}, bf16[256,2432]{1,0:T(8,128)(2,1)}, u32[]{:S(2)}, u32[]{:S(2)}) collective-permute-start(bf16[256,2432]{1,0:T(8,128)(2,1)} %collective-permute-done.7), channel_id=1, source_target_pairs={{0,2},{2,4},{4,6},{6,22},{22,20},{20,18},{18,16},{16,0},{1,3},{3,5... | collective-permute-start | bytes 3735560 | tf_op jit(solution)/shard_map/ppermute | solution.py:594
  265.4 51.3 %collective-permute-start.11 = (bf16[256,2432]{1,0:T(8,128)(2,1)}, bf16[256,2432]{1,0:T(8,128)(2,1)}, u32[]{:S(2)}, u32[]{:S(2)}) collective-permute-start(bf16[256,2432]{1,0:T(8,128)(2,1)} %collective-permute-done.9), channel_id=1, source_target_pairs={{0,2},{2,4},{4,6},{6,22},{22,20},{20,18},{18,16},{16,0},{1,3},{3,5... | collective-permute-start | bytes 3735560 | tf_op jit(solution)/shard_map/ppermute | solution.py:594
  303.2 45.5 %collective-permute-start.12 = (bf16[256,2048]{1,0:T(8,128)(2,1)S(1)}, bf16[256,2048]{1,0:T(8,128)(2,1)}, u32[]{:S(2)}, u32[]{:S(2)}) collective-permute-start(bf16[256,2048]{1,0:T(8,128)(2,1)S(1)} %get-tuple-element.117), channel_id=1, source_target_pairs={{0,0},{2,2},{4,8},{6,10},{8,4},{10,6},{12,12},{14,14},{1,1},{3,3},... | collective-permute-start | bytes 3145736 | tf_op jit(solution)/shard_map/ppermute | solution.py:645
  304.8 49.5 %collective-permute-start.13 = (bf16[256,2048]{1,0:T(8,128)(2,1)}, bf16[256,2048]{1,0:T(8,128)(2,1)}, u32[]{:S(2)}, u32[]{:S(2)}) collective-permute-start(bf16[256,2048]{1,0:T(8,128)(2,1)} %get-tuple-element.118), channel_id=1, source_target_pairs={{0,2},{2,0},{4,10},{6,8},{8,6},{10,4},{12,14},{14,12},{1,3},{3,1},... | collective-permute-start | bytes 3145736 | tf_op jit(solution)/shard_map/ppermute | solution.py:645
  310.1 298.4 %all-gather.8.cloned.1.call-start = ((), (), s32[]{:S(2)}) async-start(), calls=%async_computation.12 | async-start | bytes 4718592 | tf_op jit(solution)/shard_map/all_gather | solution.py:708
  379.9 17.7 %collective-permute-start.16 = (f32[512]{0:T(512)S(1)}, f32[512]{0:T(512)S(1)}, u32[]{:S(2)}, u32[]{:S(2)}) collective-permute-start(f32[512]{0:T(512)S(1)} %slice.578), channel_id=1, source_target_pairs={{0,8},{8,0},{1,9},{9,1},{2,10},{10,2},{3,11},{11,3},{4,12},{12,4},... | collective-permute-start | bytes 6152 | tf_op jit(solution)/shard_map/ppermute | solution.py:521
  400.8 48.2 %collective-permute-start.21 = (bf16[512,2048]{1,0:T(8,128)(2,1)}, bf16[512,2048]{1,0:T(8,128)(2,1)}, u32[]{:S(2)}, u32[]{:S(2)}) collective-permute-start(bf16[512,2048]{1,0:T(8,128)(2,1)} %pad_maximum_fusion.14), channel_id=1, source_target_pairs={{0,1},{1,0},{2,3},{3,2},{4,5},{5,4},{6,7},{7,6},{8,9},{9,8},{10,11... | collective-permute-start | bytes 6291464 | tf_op jit(solution)/shard_map/ppermute | solution.py:521
  410.6 42.3 %collective-permute-start.15 = (bf16[512,2048]{1,0:T(8,128)(2,1)S(1)}, bf16[512,2048]{1,0:T(8,128)(2,1)S(1)}, u32[]{:S(2)}, u32[]{:S(2)}) collective-permute-start(bf16[512,2048]{1,0:T(8,128)(2,1)S(1)} %slice.719), channel_id=1, source_target_pairs={{0,8},{8,0},{1,9},{9,1},{2,10},{10,2},{3,11},{11,3},{4,12},{12,4},... | collective-permute-start | bytes 6291464 | tf_op jit(solution)/shard_map/ppermute | solution.py:521
  452.9 60.4 %collective-permute-start.25 = (bf16[1024,2048]{1,0:T(8,128)(2,1)}, bf16[1024,2048]{1,0:T(8,128)(2,1)}, u32[]{:S(2)}, u32[]{:S(2)}) collective-permute-start(bf16[1024,2048]{1,0:T(8,128)(2,1)} %pad_maximum_fusion.6), channel_id=1, source_target_pairs={{0,8},{8,0},{1,9},{9,1},{2,10},{10,2},{3,11},{11,3},{4,12},{12,4},... | collective-permute-start | bytes 12582920 | tf_op jit(solution)/shard_map/ppermute | solution.py:521
  453.3 27.0 %collective-permute-start.18 = (bf16[256,2048]{1,0:T(8,128)(2,1)S(1)}, bf16[256,2048]{1,0:T(8,128)(2,1)}, u32[]{:S(2)}, u32[]{:S(2)}) collective-permute-start(bf16[256,2048]{1,0:T(8,128)(2,1)S(1)} %add_convert_fusion.13), channel_id=1, source_target_pairs={{0,1},{1,0},{2,3},{3,2},{4,5},{5,4},{6,7},{7,6},{8,9},{9,8},{10,11... | collective-permute-start | bytes 3145736 | tf_op jit(solution)/shard_map/ppermute | solution.py:521
  479.9 18.0 %collective-permute-start.23 = (f32[512]{0:T(512)S(1)}, f32[512]{0:T(512)S(1)}, u32[]{:S(2)}, u32[]{:S(2)}) collective-permute-start(f32[512]{0:T(512)S(1)} %slice.594), channel_id=1, source_target_pairs={{0,8},{8,0},{1,9},{9,1},{2,10},{10,2},{3,11},{11,3},{4,12},{12,4},... | collective-permute-start | bytes 6152 | tf_op jit(solution)/shard_map/ppermute | solution.py:521
  487.6 34.0 %collective-permute-start.19 = (bf16[256,2048]{1,0:T(8,128)(2,1)}, bf16[256,2048]{1,0:T(8,128)(2,1)}, u32[]{:S(2)}, u32[]{:S(2)}) collective-permute-start(bf16[256,2048]{1,0:T(8,128)(2,1)} %multiply_convert_fusion.11), channel_id=1, source_target_pairs={{0,1},{1,0},{2,3},{3,2},{4,5},{5,4},{6,7},{7,6},{8,9},{9,8},{10,11... | collective-permute-start | bytes 3145736 | tf_op jit(solution)/shard_map/ppermute | solution.py:521
  497.9 32.0 %collective-permute-start.22 = (bf16[512,2048]{1,0:T(8,128)(2,1)}, bf16[512,2048]{1,0:T(8,128)(2,1)}, u32[]{:S(2)}, u32[]{:S(2)}) collective-permute-start(bf16[512,2048]{1,0:T(8,128)(2,1)} %slice.729), channel_id=1, source_target_pairs={{0,8},{8,0},{1,9},{9,1},{2,10},{10,2},{3,11},{11,3},{4,12},{12,4},... | collective-permute-start | bytes 6291464 | tf_op jit(solution)/shard_map/ppermute | solution.py:521
  498.9 499.5 %reduce-scatter.5.cloned.1.call-start = ((), (), s32[]{:S(2)}) async-start(), calls=%async_computation.13 | async-start | bytes 4718592 | tf_op jit(solution)/shard_map/reduce_scatter | solution.py:1109
  523.5 39.1 %collective-permute-start.20 = (bf16[512,2048]{1,0:T(8,128)(2,1)S(1)}, bf16[512,2048]{1,0:T(8,128)(2,1)}, u32[]{:S(2)}, u32[]{:S(2)}) collective-permute-start(bf16[512,2048]{1,0:T(8,128)(2,1)S(1)} %pad_maximum_fusion.13), channel_id=1, source_target_pairs={{0,8},{8,0},{1,9},{9,1},{2,10},{10,2},{3,11},{11,3},{4,12},{12,4},... | collective-permute-start | bytes 6291464 | tf_op jit(solution)/shard_map/ppermute | solution.py:521
  532.9 32.2 %collective-permute-start.26 = (bf16[256,2048]{1,0:T(8,128)(2,1)}, bf16[256,2048]{1,0:T(8,128)(2,1)}, u32[]{:S(2)}, u32[]{:S(2)}) collective-permute-start(bf16[256,2048]{1,0:T(8,128)(2,1)} %add_convert_fusion.12), channel_id=1, source_target_pairs={{0,1},{1,0},{2,3},{3,2},{4,5},{5,4},{6,7},{7,6},{8,9},{9,8},{10,11... | collective-permute-start | bytes 3145736 | tf_op jit(solution)/shard_map/ppermute | solution.py:521
  570.2 47.4 %collective-permute-start.31 = (bf16[256,2048]{1,0:T(8,128)(2,1)S(1)}, bf16[256,2048]{1,0:T(8,128)(2,1)}, u32[]{:S(2)}, u32[]{:S(2)}) collective-permute-start(bf16[256,2048]{1,0:T(8,128)(2,1)S(1)} %multiply_convert_fusion.10), channel_id=1, source_target_pairs={{0,1},{1,0},{2,3},{3,2},{4,5},{5,4},{6,7},{7,6},{8,9},{9,8},{10,11... | collective-permute-start | bytes 3145736 | tf_op jit(solution)/shard_map/ppermute | solution.py:521
  628.7 43.6 %collective-permute-start.30 = (bf16[256,2048]{1,0:T(8,128)(2,1)S(1)}, bf16[256,2048]{1,0:T(8,128)(2,1)S(1)}, u32[]{:S(2)}, u32[]{:S(2)}) collective-permute-start(bf16[256,2048]{1,0:T(8,128)(2,1)S(1)} %add_convert_fusion.11), channel_id=1, source_target_pairs={{0,1},{1,0},{2,3},{3,2},{4,5},{5,4},{6,7},{7,6},{8,9},{9,8},{10,11... | collective-permute-start | bytes 3145736 | tf_op jit(solution)/shard_map/ppermute | solution.py:521
  690.4 24.5 %collective-permute-start.40 = (bf16[256,2048]{1,0:T(8,128)(2,1)S(1)}, bf16[256,2048]{1,0:T(8,128)(2,1)S(1)}, u32[]{:S(2)}, u32[]{:S(2)}) collective-permute-start(bf16[256,2048]{1,0:T(8,128)(2,1)S(1)} %add_convert_fusion.9), channel_id=1, source_target_pairs={{0,1},{1,0},{2,3},{3,2},{4,5},{5,4},{6,7},{7,6},{8,9},{9,8},{10,11... | collective-permute-start | bytes 3145736 | tf_op jit(solution)/shard_map/ppermute | solution.py:521
  694.0 20.8 %collective-permute-start.37 = (f32[1,256]{1,0:T(1,128)S(1)}, f32[1,256]{1,0:T(1,128)S(1)}, u32[]{:S(2)}, u32[]{:S(2)}) collective-permute-start(f32[1,256]{1,0:T(1,128)S(1)} %bitcast.336), channel_id=1, source_target_pairs={{0,1},{1,0},{2,3},{3,2},{4,5},{5,4},{6,7},{7,6},{8,9},{9,8},{10,11... | collective-permute-start | bytes 3080 | tf_op jit(solution)/shard_map/ppermute | solution.py:521
  814.9 16.5 %collective-permute-start.43 = (bf16[512,2048]{1,0:T(8,128)(2,1)}, bf16[512,2048]{1,0:T(8,128)(2,1)S(1)}, u32[]{:S(2)}, u32[]{:S(2)}) collective-permute-start(bf16[512,2048]{1,0:T(8,128)(2,1)} %slice.755), channel_id=1, source_target_pairs={{0,8},{8,0},{1,9},{9,1},{2,10},{10,2},{3,11},{11,3},{4,12},{12,4},... | collective-permute-start | bytes 6291464 | tf_op jit(solution)/shard_map/ppermute | solution.py:521
  831.8 50.7 %collective-permute-start.48 = (bf16[256,2048]{1,0:T(8,128)(2,1)S(1)}, bf16[256,2048]{1,0:T(8,128)(2,1)S(1)}, u32[]{:S(2)}, u32[]{:S(2)}) collective-permute-start(bf16[256,2048]{1,0:T(8,128)(2,1)S(1)} %add_convert_fusion.8), channel_id=1, source_target_pairs={{0,1},{1,0},{2,3},{3,2},{4,5},{5,4},{6,7},{7,6},{8,9},{9,8},{10,11... | collective-permute-start | bytes 3145736 | tf_op jit(solution)/shard_map/ppermute | solution.py:521
  889.7 25.1 %collective-permute-start.49 = (bf16[256,2048]{1,0:T(8,128)(2,1)S(1)}, bf16[256,2048]{1,0:T(8,128)(2,1)}, u32[]{:S(2)}, u32[]{:S(2)}) collective-permute-start(bf16[256,2048]{1,0:T(8,128)(2,1)S(1)} %get-tuple-element.167), channel_id=1, source_target_pairs={{0,1},{1,0},{2,3},{3,2},{4,5},{5,4},{6,7},{7,6},{8,9},{9,8},{10,11... | collective-permute-start | bytes 3145736 | tf_op jit(solution)/shard_map/ppermute | solution.py:521
  890.8 356.2 %reduce-scatter.7.cloned.1.call-start = ((), (), s32[]{:S(2)}) async-start(), calls=%async_computation.14 | async-start | bytes 11206656 | tf_op jit(solution)/shard_map/reduce_scatter | solution.py:1109
  920.5 38.1 %collective-permute-start.53 = (bf16[256,2048]{1,0:T(8,128)(2,1)}, bf16[256,2048]{1,0:T(8,128)(2,1)}, u32[]{:S(2)}, u32[]{:S(2)}) collective-permute-start(bf16[256,2048]{1,0:T(8,128)(2,1)} %get-tuple-element.222), channel_id=1, source_target_pairs={{0,1},{1,0},{2,3},{3,2},{4,5},{5,4},{6,7},{7,6},{8,9},{9,8},{10,11... | collective-permute-start | bytes 3145736 | tf_op jit(solution)/shard_map/ppermute | solution.py:521
  1031.0 23.7 %collective-permute-start.51 = (bf16[512,2048]{1,0:T(8,128)(2,1)}, bf16[512,2048]{1,0:T(8,128)(2,1)}, u32[]{:S(2)}, u32[]{:S(2)}) collective-permute-start(bf16[512,2048]{1,0:T(8,128)(2,1)} %slice.761), channel_id=1, source_target_pairs={{0,8},{8,0},{1,9},{9,1},{2,10},{10,2},{3,11},{11,3},{4,12},{12,4},... | collective-permute-start | bytes 6291464 | tf_op jit(solution)/shard_map/ppermute | solution.py:521
  1040.9 206.0 %all-to-all-start.3 = ((bf16[4,64,1024]{2,1,0:T(8,128)(2,1)}), bf16[4,64,1024]{2,1,0:T(8,128)(2,1)}, u32[]{:S(2)}, u32[]{:S(2)}) async-start(bf16[4,64,1024]{2,1,0:T(8,128)(2,1)} %bitcast.91), calls=%async_computation.5 | async-start | bytes 1048576 | tf_op jit(solution)/shard_map/all_to_all | solution.py:714
  1045.1 412.1 %reduce-scatter.11.cloned.1.call-start = ((), (), s32[]{:S(2)}) async-start(), calls=%async_computation.16 | async-start | bytes 4718592 | tf_op jit(solution)/shard_map/reduce_scatter | solution.py:1109
  1056.6 52.1 %collective-permute-start.52 = (bf16[256,2048]{1,0:T(8,128)(2,1)S(1)}, bf16[256,2048]{1,0:T(8,128)(2,1)S(1)}, u32[]{:S(2)}, u32[]{:S(2)}) collective-permute-start(bf16[256,2048]{1,0:T(8,128)(2,1)S(1)} %add_convert_fusion.6), channel_id=1, source_target_pairs={{0,1},{1,0},{2,3},{3,2},{4,5},{5,4},{6,7},{7,6},{8,9},{9,8},{10,11... | collective-permute-start | bytes 3145736 | tf_op jit(solution)/shard_map/ppermute | solution.py:521
  1115.8 31.9 %collective-permute-start.59 = (bf16[256,2048]{1,0:T(8,128)(2,1)S(1)}, bf16[256,2048]{1,0:T(8,128)(2,1)}, u32[]{:S(2)}, u32[]{:S(2)}) collective-permute-start(bf16[256,2048]{1,0:T(8,128)(2,1)S(1)} %get-tuple-element.220), channel_id=1, source_target_pairs={{0,1},{1,0},{2,3},{3,2},{4,5},{5,4},{6,7},{7,6},{8,9},{9,8},{10,11... | collective-permute-start | bytes 3145736 | tf_op jit(solution)/shard_map/ppermute | solution.py:521
  1115.9 25.0 %collective-permute-start.64 = (f32[1,256]{1,0:T(1,128)S(1)}, f32[1,256]{1,0:T(1,128)S(1)}, u32[]{:S(2)}, u32[]{:S(2)}) collective-permute-start(f32[1,256]{1,0:T(1,128)S(1)} %bitcast.348), channel_id=1, source_target_pairs={{0,1},{1,0},{2,3},{3,2},{4,5},{5,4},{6,7},{7,6},{8,9},{9,8},{10,11... | collective-permute-start | bytes 3080 | tf_op jit(solution)/shard_map/ppermute | solution.py:521
  1133.5 32.5 %collective-permute-start.63 = (bf16[512,2048]{1,0:T(8,128)(2,1)}, bf16[512,2048]{1,0:T(8,128)(2,1)}, u32[]{:S(2)}, u32[]{:S(2)}) collective-permute-start(bf16[512,2048]{1,0:T(8,128)(2,1)} %slice.772), channel_id=1, source_target_pairs={{0,8},{8,0},{1,9},{9,1},{2,10},{10,2},{3,11},{11,3},{4,12},{12,4},... | collective-permute-start | bytes 6291464 | tf_op jit(solution)/shard_map/ppermute | solution.py:521
  1149.4 20.0 %collective-permute-start.60 = (bf16[512,2048]{1,0:T(8,128)(2,1)S(1)}, bf16[512,2048]{1,0:T(8,128)(2,1)S(1)}, u32[]{:S(2)}, u32[]{:S(2)}) collective-permute-start(bf16[512,2048]{1,0:T(8,128)(2,1)S(1)} %pad_maximum_fusion.19), channel_id=1, source_target_pairs={{0,8},{8,0},{1,9},{9,1},{2,10},{10,2},{3,11},{11,3},{4,12},{12,4},... | collective-permute-start | bytes 6291464 | tf_op jit(solution)/shard_map/ppermute | solution.py:521
  1169.0 71.3 %collective-permute-start.66 = (bf16[256,2048]{1,0:T(8,128)(2,1)}, bf16[256,2048]{1,0:T(8,128)(2,1)S(1)}, u32[]{:S(2)}, u32[]{:S(2)}) collective-permute-start(bf16[256,2048]{1,0:T(8,128)(2,1)} %add_convert_fusion.5), channel_id=1, source_target_pairs={{0,1},{1,0},{2,3},{3,2},{4,5},{5,4},{6,7},{7,6},{8,9},{9,8},{10,11... | collective-permute-start | bytes 3145736 | tf_op jit(solution)/shard_map/ppermute | solution.py:521
  1247.0 20.9 %all-to-all-start.2 = ((bf16[4,64,2432]{2,1,0:T(8,128)(2,1)}), bf16[4,64,2432]{2,1,0:T(8,128)(2,1)}, u32[]{:S(2)}, u32[]{:S(2)}) async-start(bf16[4,64,2432]{2,1,0:T(8,128)(2,1)} %bitcast.276), calls=%async_computation.4 | async-start | bytes 2490368 | tf_op jit(solution)/shard_map/all_to_all | solution.py:714
  1251.3 253.2 %reduce-scatter.9.cloned.1.call-start = ((), (), s32[]{:S(2)}) async-start(), calls=%async_computation.15 | async-start | bytes 11206656 | tf_op jit(solution)/shard_map/reduce_scatter | solution.py:1109
  1308.8 25.3 %collective-permute-start.70 = (bf16[256,2048]{1,0:T(8,128)(2,1)S(1)}, bf16[256,2048]{1,0:T(8,128)(2,1)S(1)}, u32[]{:S(2)}, u32[]{:S(2)}) collective-permute-start(bf16[256,2048]{1,0:T(8,128)(2,1)S(1)} %add_convert_fusion.4), channel_id=1, source_target_pairs={{0,1},{1,0},{2,3},{3,2},{4,5},{5,4},{6,7},{7,6},{8,9},{9,8},{10,11... | collective-permute-start | bytes 3145736 | tf_op jit(solution)/shard_map/ppermute | solution.py:521
  1338.7 26.2 %collective-permute-start.46 = (bf16[256,2048]{1,0:T(8,128)(2,1)S(1)}, bf16[256,2048]{1,0:T(8,128)(2,1)S(1)}, u32[]{:S(2)}, u32[]{:S(2)}) collective-permute-start(bf16[256,2048]{1,0:T(8,128)(2,1)S(1)} %get-tuple-element.164), channel_id=1, source_target_pairs={{0,1},{1,0},{2,3},{3,2},{4,5},{5,4},{6,7},{7,6},{8,9},{9,8},{10,11... | collective-permute-start | bytes 3145736 | tf_op jit(solution)/shard_map/ppermute | solution.py:521
  1339.3 48.1 %collective-permute-start.73 = (bf16[256,2048]{1,0:T(8,128)(2,1)}, bf16[256,2048]{1,0:T(8,128)(2,1)S(1)}, u32[]{:S(2)}, u32[]{:S(2)}) collective-permute-start(bf16[256,2048]{1,0:T(8,128)(2,1)} %fusion.11), channel_id=1, source_target_pairs={{0,1},{1,0},{2,3},{3,2},{4,5},{5,4},{6,7},{7,6},{8,9},{9,8},{10,11... | collective-permute-start | bytes 3145736 | tf_op jit(solution)/shard_map/ppermute | solution.py:521
  1365.0 45.6 %collective-permute-start.47 = (bf16[512,2048]{1,0:T(8,128)(2,1)S(1)}, bf16[512,2048]{1,0:T(8,128)(2,1)}, u32[]{:S(2)}, u32[]{:S(2)}) collective-permute-start(bf16[512,2048]{1,0:T(8,128)(2,1)S(1)} %pad_maximum_fusion.16), channel_id=1, source_target_pairs={{0,8},{8,0},{1,9},{9,1},{2,10},{10,2},{3,11},{11,3},{4,12},{12,4},... | collective-permute-start | bytes 6291464 | tf_op jit(solution)/shard_map/ppermute | solution.py:521
  1365.1 43.1 %collective-permute-start.71 = (bf16[256,2048]{1,0:T(8,128)(2,1)S(1)}, bf16[256,2048]{1,0:T(8,128)(2,1)S(1)}, u32[]{:S(2)}, u32[]{:S(2)}) collective-permute-start(bf16[256,2048]{1,0:T(8,128)(2,1)S(1)} %get-tuple-element.239), channel_id=1, source_target_pairs={{0,1},{1,0},{2,3},{3,2},{4,5},{5,4},{6,7},{7,6},{8,9},{9,8},{10,11... | collective-permute-start | bytes 3145736 | tf_op jit(solution)/shard_map/ppermute | solution.py:521
  1390.3 47.3 %collective-permute-start.74 = (bf16[512,2048]{1,0:T(8,128)(2,1)}, bf16[512,2048]{1,0:T(8,128)(2,1)}, u32[]{:S(2)}, u32[]{:S(2)}) collective-permute-start(bf16[512,2048]{1,0:T(8,128)(2,1)} %pad_maximum_fusion.21), channel_id=1, source_target_pairs={{0,8},{8,0},{1,9},{9,1},{2,10},{10,2},{3,11},{11,3},{4,12},{12,4},... | collective-permute-start | bytes 6291464 | tf_op jit(solution)/shard_map/ppermute | solution.py:521
  1409.8 27.8 %collective-permute-start.72 = (bf16[512,2048]{1,0:T(8,128)(2,1)}, bf16[512,2048]{1,0:T(8,128)(2,1)}, u32[]{:S(2)}, u32[]{:S(2)}) collective-permute-start(bf16[512,2048]{1,0:T(8,128)(2,1)} %pad_maximum_fusion.20), channel_id=1, source_target_pairs={{0,8},{8,0},{1,9},{9,1},{2,10},{10,2},{3,11},{11,3},{4,12},{12,4},... | collective-permute-start | bytes 6291464 | tf_op jit(solution)/shard_map/ppermute | solution.py:521
  1434.1 42.3 %collective-permute-start.68 = (bf16[256,2048]{1,0:T(8,128)(2,1)}, bf16[256,2048]{1,0:T(8,128)(2,1)}, u32[]{:S(2)}, u32[]{:S(2)}) collective-permute-start(bf16[256,2048]{1,0:T(8,128)(2,1)} %get-tuple-element.241), channel_id=1, source_target_pairs={{2,0},{0,2},{10,4},{8,6},{6,8},{4,10},{14,12},{12,14},{3,1},{1,3},... | collective-permute-start | bytes 3145736 | tf_op jit(solution)/shard_map/ppermute | solution.py:650
  1435.8 40.7 %collective-permute-start.67 = (bf16[256,2048]{1,0:T(8,128)(2,1)}, bf16[256,2048]{1,0:T(8,128)(2,1)S(1)}, u32[]{:S(2)}, u32[]{:S(2)}) collective-permute-start(bf16[256,2048]{1,0:T(8,128)(2,1)} %get-tuple-element.242), channel_id=1, source_target_pairs={{0,0},{2,2},{8,4},{10,6},{4,8},{6,10},{12,12},{14,14},{1,1},{3,3},... | collective-permute-start | bytes 3145736 | tf_op jit(solution)/shard_map/ppermute | solution.py:650
  1455.1 45.6 %collective-permute-start.76 = (bf16[256,2048]{1,0:T(8,128)(2,1)}, bf16[256,2048]{1,0:T(8,128)(2,1)}, u32[]{:S(2)}, u32[]{:S(2)}) collective-permute-start(bf16[256,2048]{1,0:T(8,128)(2,1)} %get-tuple-element.237), channel_id=1, source_target_pairs={{2,0},{0,2},{10,4},{8,6},{6,8},{4,10},{14,12},{12,14},{3,1},{1,3},... | collective-permute-start | bytes 3145736 | tf_op jit(solution)/shard_map/ppermute | solution.py:650
  1455.4 45.3 %collective-permute-start.75 = (bf16[256,2048]{1,0:T(8,128)(2,1)}, bf16[256,2048]{1,0:T(8,128)(2,1)S(1)}, u32[]{:S(2)}, u32[]{:S(2)}) collective-permute-start(bf16[256,2048]{1,0:T(8,128)(2,1)} %get-tuple-element.238), channel_id=1, source_target_pairs={{0,0},{2,2},{8,4},{10,6},{4,8},{6,10},{12,12},{14,14},{1,1},{3,3},... | collective-permute-start | bytes 3145736 | tf_op jit(solution)/shard_map/ppermute | solution.py:650
  1457.3 47.3 %all-to-all-start.5 = ((bf16[4,64,1024]{2,1,0:T(8,128)(2,1)}), bf16[4,64,1024]{2,1,0:T(8,128)(2,1)S(1)}, u32[]{:S(2)}, u32[]{:S(2)}) async-start(bf16[4,64,1024]{2,1,0:T(8,128)(2,1)} %bitcast.287), calls=%async_computation.9 | async-start | bytes 1048576 | tf_op jit(solution)/shard_map/all_to_all | solution.py:714
  1504.6 65.3 %all-to-all-start.4 = ((bf16[4,64,2432]{2,1,0:T(8,128)(2,1)}), bf16[4,64,2432]{2,1,0:T(8,128)(2,1)S(1)}, u32[]{:S(2)}, u32[]{:S(2)}) async-start(bf16[4,64,2432]{2,1,0:T(8,128)(2,1)} %bitcast.277), calls=%async_computation.7 | async-start | bytes 2490368 | tf_op jit(solution)/shard_map/all_to_all | solution.py:714
  (139 other events, 3403.6 us)
Sparse Core Ops, SparseCore 0:
  90.7 115.7 all-gather.3
  310.2 167.6 all-gather.5
  499.0 93.0 all-gather.7
  890.9 107.4 reduce-scatter.4
  1018.8 170.4 reduce-scatter.6
  1193.3 87.0 reduce-scatter.10
  1288.9 183.1 reduce-scatter.8

commit v3 on v2

--- a/solution.py
+++ b/solution.py
@@ -81,6 +81,15 @@
     e = jnp.exp(cum) * meta_ref[:, 3:4]
     decay = jnp.exp(cum[chunk - 1 : chunk, :] - cum) * meta_ref[:, 4:5]
     return raw, steps, cum, e, decay
+
+
+def row_blocks(chunk):
+    return [(at, at + LANES) for at in range(0, chunk, LANES)]
+
+
+def block_decays(cumb, cumt, mask_ref, top, end):
+    rows = jnp.concatenate([cumb[top:end]] * (end // LANES), axis=1)
+    return jnp.exp(rows - cumt[:, :end] + mask_ref[top:end, :end])
 
 
 def conv_parts(pad_ref, sl, chunk, cw, masks):
@@ -145,9 +154,13 @@
         for k in range(2):
             h = 2 * p + k
             cumb = cumb_ref[:, pl.ds(pl.multiple_of(h * LANES, LANES), LANES)]
-            cumb = jnp.concatenate([cumb] * (chunk // LANES), axis=1)
-            decays = jnp.exp(cumb - cumt_ref[pl.ds(h, 1), :] + mask_ref[...])
-            halves.append(dot((g_ref[...] * decays).astype(jnp.bfloat16), xs))
+            cumt = cumt_ref[pl.ds(h, 1), :]
+            parts = []
+            for top, end in row_blocks(chunk):
+                decays = block_decays(cumb, cumt, mask_ref, top, end)
+                weights = (g_ref[top:end, :end] * decays).astype(jnp.bfloat16)
+                parts.append(dot(weights, xs[:end]))
+            halves.append(jnp.concatenate(parts))
         inner = jnp.where(low_lane, halves[0], halves[1])
         state = sout_ref[:, sl]
         into = eexp[:, sl]
@@ -162,7 +175,7 @@
         ss_ref[...] += gated * gated
         return carry
 
-    lax.fori_loop(0, width // LANES, pair, 0)
+    lax.fori_loop(0, width // LANES, pair, 0, unroll=4)
 
 
 def common_specs(chunk, width, order):
@@ -265,7 +278,7 @@
     mix_ref, u_ref, fs_ref, states_ref, ds0_ref, tx0_ref, tbc0_ref,
     gproj_ref, acc_ref, accbc_ref, acch_ref, ds_ref, tx_ref, tbc_ref,
     xpad, bpad, masks, cumb_ref, cumt_ref, mask_ref, sexp, eexp, dexp, wide_ref, tall_ref, g_ref,
-    dg_ref, db_ref, dc_ref, dcum_ref, dsx_ref, dpad, fac_ref, sb_ref,
+    dg_ref, dcb_ref, dcum_ref, dpad, fac_ref, sb_ref,
 ):
     chunk, width = x_ref.shape
     step = pl.program_id(0)
@@ -314,10 +327,9 @@
     low_lane = lax.broadcasted_iota(jnp.int32, (chunk, LANES), 1) < HEAD
     last_row = lax.broadcasted_iota(jnp.int32, (chunk, LANES), 0) == chunk - 1
     dg_ref[...] = jnp.zeros_like(dg_ref)
-    db_ref[...] = jnp.zeros_like(db_ref)
-    dc_ref[...] = jnp.zeros_like(dc_ref)
+    dcb_ref[...] = jnp.zeros_like(dcb_ref)
     dcum_ref[...] = jnp.zeros_like(dcum_ref)
-    dsx_ref[...] = jnp.zeros_like(dsx_ref)
+    cbmat = jnp.concatenate([cmat, bmat], axis=1)
 
     def pair(p, carry):
         start = pl.multiple_of(p * LANES, LANES)
@@ -345,14 +357,22 @@
         for k in range(2):
             h = 2 * p + k
             cumb = cumb_ref[:, pl.ds(pl.multiple_of(h * LANES, LANES), LANES)]
-            cumb = jnp.concatenate([cumb] * (chunk // LANES), axis=1)
-            decays = jnp.exp(cumb - cumt_ref[pl.ds(h, 1), :] + mask_ref[...])
-            weights = (g_ref[...] * decays).astype(jnp.bfloat16)
+            cumt = cumt_ref[pl.ds(h, 1), :]
             own = low_lane if k == 0 else jnp.logical_not(low_lane)
-            pulls = dot_nt(jnp.where(own, dy, 0.0).astype(jnp.bfloat16), xs)
-            dg_ref[...] += pulls * decays
-            ys.append(dot(weights, xs))
-            dxs.append(dot_tn(weights, gm))
+            dyown = jnp.where(own, dy, 0.0).astype(jnp.bfloat16)
+            parts, total = [], None
+            for top, end in reversed(row_blocks(chunk)):
+                decays = block_decays(cumb, cumt, mask_ref, top, end)
+                weights = (g_ref[top:end, :end] * decays).astype(jnp.bfloat16)
+                dg_ref[top:end, :end] += dot_nt(dyown[top:end], xs[:end]) * decays
+                parts.insert(0, dot(weights, xs[:end]))
+                found = dot_tn(weights, gm[top:end])
+                if total is None:
+                    total = found
+                else:
+                    total = jnp.concatenate([total[:end] + found, total[end:]])
+            ys.append(jnp.concatenate(parts))
+            dxs.append(total)
         inner = jnp.where(low_lane, ys[0], ys[1])
         dinner = jnp.where(low_lane, dxs[0], dxs[1])
         state = states_ref[0, :, sl]
@@ -361,11 +381,16 @@
         dstateb = dstate.astype(jnp.bfloat16)
         into = eexp[:, sl]
         dec = dexp[:, sl]
-        carried = dot(cmat, stateb) * into
+        none = jnp.zeros_like(stateb)
+        both = jnp.concatenate(
+            [jnp.concatenate([stateb, none], axis=1), jnp.concatenate([none, dstateb], axis=1)]
+        )
+        product = dot(cbmat, both)
+        carried = product[:, :LANES] * into
+        bds = product[:, LANES:] * dec
         edy = (dy * into).astype(jnp.bfloat16)
-        dc_ref[...] += dot_nt(edy, stateb)
-        bds = dot(bmat, dstateb) * dec
-        db_ref[...] += dot_nt((xsf * dec).astype(jnp.bfloat16), dstateb)
+        pulled = jnp.concatenate([edy, (xsf * dec).astype(jnp.bfloat16)], axis=1)
+        dcb_ref[...] += dot_nt(pulled, both)
         tails = xsf * bds
         ends = jnp.sum(tails, axis=0, keepdims=True) + into[chunk - 1 : chunk, :] * jnp.sum(
             dstate * state, axis=0, keepdims=True
@@ -375,10 +400,12 @@
         row = lax.broadcasted_iota(jnp.int32, (LANES, LANES), 0)
         col = lax.broadcasted_iota(jnp.int32, (LANES, LANES), 1)
         gather = (col == 2 * p + row // HEAD).astype(jnp.bfloat16)
+        aside = (col == HEAD + 2 * p + row // HEAD).astype(jnp.bfloat16)
         hi, mid, lo = split3(rowq)
-        dcum_ref[...] += dot(hi, gather) + dot(mid, gather) + dot(lo, gather)
-        hi, mid, lo = split3(xact * dxsum)
-        dsx_ref[...] += dot(hi, gather) + dot(mid, gather)
+        steps_hi = (xact * dxsum).astype(jnp.bfloat16)
+        dcum_ref[...] += dot(
+            jnp.concatenate([hi, mid], axis=1), jnp.concatenate([gather, gather])
+        ) + dot(jnp.concatenate([lo, steps_hi], axis=1), jnp.concatenate([gather, aside]))
         ds_ref[:, sl] = dstate * into[chunk - 1 : chunk, :] + dot_tn(cmat, edy)
         acc_ref[5:6, sl] += jnp.sum(dy * xact, axis=0, keepdims=True)
         dact = sx * dxsum + cw[5:6, :] * dy
@@ -387,9 +414,9 @@
         gproj_ref[:, pl.ds(pl.multiple_of(width + start, LANES), LANES)] = grad.astype(jnp.bfloat16)
         return carry
 
-    lax.fori_loop(0, width // LANES, pair, 0)
+    lax.fori_loop(0, width // LANES, pair, 0, unroll=4)
     dgb = dg_ref[...].astype(jnp.bfloat16)
-    grads = (db_ref[...] + dot_tn(dgb, cmat), dc_ref[...] + dot(dgb, bmat))
+    grads = (dcb_ref[:, N:] + dot_tn(dgb, cmat), dcb_ref[:, :N] + dot(dgb, bmat))
     for half in range(2):
         sl = slice(half * LANES, (half + 1) * LANES)
         cw = cbc_ref[:, sl]
@@ -402,8 +429,11 @@
     row = lax.broadcasted_iota(jnp.int32, (chunk, chunk), 0)
     col = lax.broadcasted_iota(jnp.int32, (chunk, chunk), 1)
     upper = (col >= row).astype(jnp.bfloat16)
-    dlogs = exact_left(upper, dcum_ref[...])
-    dsteps = dsx_ref[...] + dlogs * hp_ref[1:2, :]
+    found = dcum_ref[...]
+    below = lax.broadcasted_iota(jnp.int32, found.shape, 1) < HEAD
+    dlogs = exact_left(upper, jnp.where(below, found, 0.0))
+    direct = jnp.where(below, pltpu.roll(found, HEAD, 1), 0.0)
+    dsteps = direct + dlogs * hp_ref[1:2, :]
     draw = dsteps * sigmoid(raw)
     gproj_ref[:, 2 * width + 256 :] = draw.astype(jnp.bfloat16)
     acch_ref[0:1, :] += jnp.sum(draw, axis=0, keepdims=True)
@@ -470,9 +500,7 @@
             pltpu.VMEM((LANES, 2 * width), jnp.bfloat16),
             pltpu.VMEM((chunk, chunk), f32),
             pltpu.VMEM((chunk, chunk), f32),
-            pltpu.VMEM((chunk, N), f32),
-            pltpu.VMEM((chunk, N), f32),
-            pltpu.VMEM((chunk, LANES), f32),
+            pltpu.VMEM((chunk, 2 * N), f32),
             pltpu.VMEM((chunk, LANES), f32),
             pltpu.VMEM((3, chunk + 8, LANES), f32),
             pltpu.VMEM((chunk, LANES), f32),
@@ -988,7 +1016,8 @@
         for i in range(PARTS):
             rows = states[i]
             if layer == 0:
-                normed = normed_rows(everything[i].astype(f32), gain)
+                every = everything[i].astype(f32)
+                normed = (every * row_scale(every) * gain).astype(bf16)
             else:
                 normed = gathered_rows[i]
             proj = jnp.dot(turn(normed), w_cols[layer], preferred_element_type=f32).astype(bf16)
@@ -1152,7 +1181,10 @@
                 out_parts[i], came = team_gather(after(states[i].astype(bf16), gproj))
                 if i + 1 < PARTS:
                     needed += (out_parts[i + 1],)
+            if layer == top - 1 and i == PARTS - 1:
+                needed += (sum_out_done,)
             if layer == 0 and i == 0:
+                needed += (out_parts[0],)
                 sum_in = add_in(layer, i, gproj, sum_in, *needed, *splits[1:], *outs[1:])
                 sum_in = done(with_small(sum_in, carry[1], layer))
                 splits[layer] = plane_sum(sum_in)
@@ -1165,7 +1197,7 @@
                 summed_out = plane_sum(sum_out)
         if layer > 0:
             for i in reversed(range(PARTS)):
-                wait = (next_gouts[i + 1][1], sum_out_done) if i + 1 < PARTS else ()
+                wait = next_gouts[i + 1][1:] if i + 1 < PARTS else ()
                 sum_in = add_in(layer, i, kept[i], sum_in, *wait)
             sum_in = done(with_small(sum_in, carry[1], layer))
             splits[layer] = from_plane(plane_sum(sum_in))

time: 1600 us -> 1540 us (0.963)
  waiting for transfers between devices: 378 us -> 412 us
  Pallas kernels: 316 us -> 284 us
  starting transfers between devices: 200 us -> 169 us
  other arithmetic: 172 us -> 150 us
    all_to_all x4, starting transfers between devices: 62.2 us -> 37.1 us  [from_plane(): lax.all_to_all(blocks, ('core', 'x'), split_axis=0, concat_axis=0, tiled=...]
    pallas_call x4, Pallas kernels: 198 us -> 178 us  [mixer_backward(): pl.pallas_call(backward_kernel, grid_spec=pltpu.PrefetchScalarGridSpec(nu...]
  transfers between devices with their start and end apart: 90 -> 90, of which waited for: 35 -> 35; matrix products, arithmetic and copies ran while one was open for 35% -> 35% of each run, Pallas kernels for 17% -> 15%
where the time goes in v3:
time: 1540 us; the launch traced here: 1530 us
  waiting for transfers between devices  412 us (27%)
  Pallas kernels  284 us (18%)
  matrix products  280 us (18%)
  local copies, waits for them, and re-layouts  207 us (13%)
  starting transfers between devices  169 us (11%)
  other arithmetic  150 us (10%)
  between operations  29.4 us (2%)
    ppermute x62, waiting for transfers between devices, swap(): return lax.ppermute(value, axis, SWAP)  214 us
    pallas_call x4, Pallas kernels, mixer_backward(): pl.pallas_call(backward_kernel, grid_spec=pltpu.PrefetchScalarGridSpec(nu...  178 us
    dot_general x8, matrix products, dot_tn(): lax.dot_general(a, b, (((0,), (0,)), ((), ())), preferred_element_type=jn...  96.5 us
    dot_general x8, matrix products, dot_nt(): lax.dot_general(a, b, (((1,), (1,)), ((), ())), preferred_element_type=jn...  89.7 us
    pallas_call x4, Pallas kernels, mixer_forward(): pl.pallas_call(forward_kernel, grid_spec=pltpu.PrefetchScalarGridSpec(num...  86.1 us
    ppermute x62, starting transfers between devices, swap(): return lax.ppermute(value, axis, SWAP)  65 us
    dot_general x4, matrix products, per_device(): jnp.dot(turn(normed), w_cols[layer], preferred_element_type=f32)  59.8 us
    ppermute x4, waiting for transfers between devices, from_team(): lax.ppermute(v, ('core', 'z'), [(b, a) for a, b in pairs])  50.2 us
  transfers between devices with their start and end apart: 90, of which 35 were waited for; matrix products, arithmetic and copies ran while one was open for 35% of the time, Pallas kernels for 15%

profile of v3, /device:TPU:0, one launch (start us, length us, event | category | flops | bytes accessed | tf_op | source)
XLA Modules:
  0.0 1530.6 jit_solution(15258481245862406560)
XLA Ops:
  38.5 5.8 concatenate.285
  91.3 25.5 %collective-permute-done.2 = bf16[512,2048]{1,0:T(8,128)(2,1)} collective-permute-done((bf16[512,2048]{1,0:T(8,128)(2,1)}, bf16[512,2048]{1,0:T(8,128)(2,1)}, u32[]{:S(2)}, u32[]{:S(2)}) %collective-permute-start.2) | collective-permute-done | bytes 2097184 | tf_op jit(solution)/shard_map/ppermute | solution.py:549
  120.4 16.1 %collective-permute-start.3 = (bf16[1024,2048]{1,0:T(8,128)(2,1)}, bf16[1024,2048]{1,0:T(8,128)(2,1)}, u32[]{:S(2)}, u32[]{:S(2)}) collective-permute-start(bf16[1024,2048]{1,0:T(8,128)(2,1)} %pad_maximum_fusion.4), channel_id=1, source_target_pairs={{0,8},{8,0},{1,9},{9,1},{2,10},{10,2},{3,11},{11,3},{4,12},{12,4},... | collective-permute-start | bytes 12582920 | tf_op jit(solution)/shard_map/ppermute | solution.py:549
  140.6 34.7 %collective-permute-start.7 = (bf16[256,2432]{1,0:T(8,128)(2,1)}, bf16[256,2432]{1,0:T(8,128)(2,1)}, u32[]{:S(2)}, u32[]{:S(2)}) collective-permute-start(bf16[256,2432]{1,0:T(8,128)(2,1)} %collective-permute-done.5), channel_id=1, source_target_pairs={{0,2},{2,4},{4,6},{6,22},{22,20},{20,18},{18,16},{16,0},{1,3},{3,5... | collective-permute-start | bytes 3735560 | tf_op jit(solution)/shard_map/ppermute | solution.py:622
  185.7 31.8 %collective-permute-done.8 = bf16[256,2432]{1,0:T(8,128)(2,1)} collective-permute-done((bf16[256,2432]{1,0:T(8,128)(2,1)}, bf16[256,2432]{1,0:T(8,128)(2,1)}, u32[]{:S(2)}, u32[]{:S(2)}) %collective-permute-start.8) | collective-permute-done | bytes 1245216 | tf_op jit(solution)/shard_map/ppermute | solution.py:625
  234.4 13.1 collective-permute-done.10
  252.3 8.5 pad_maximum_fusion
  263.7 13.3 gather_fusion
  277.0 13.3 gather_fusion.1
  310.4 16.7 %convolution_convert_fusion.5.gate_ref.x_ref.bc_ref.st_ref.hx_ref.hbc_ref.px_ref.pbc_ref = bf16[1024,2432]{1,0:T(8,128)(2,1)} fusion(bf16[1024,2048]{1,0:T(8,128)(2,1)S(1)} %get-tuple-element.260, bf16[2048,2432]{0,1:T(8,128)(2,1)} %constant_dynamic-update-slice_fusion), kind=kOutput, calls=%fused_computation.31 | convolution fusion | flops 10203037696 | bytes 19136512 | tf_op jit(solution)/shard_map/dot_general | solution.py:1023
  329.4 24.3 %collective-permute-done.13 = bf16[256,2048]{1,0:T(8,128)(2,1)} collective-permute-done((bf16[256,2048]{1,0:T(8,128)(2,1)}, bf16[256,2048]{1,0:T(8,128)(2,1)}, u32[]{:S(2)}, u32[]{:S(2)}) %collective-permute-start.13) | collective-permute-done | bytes 1048608 | tf_op jit(solution)/shard_map/ppermute | solution.py:673
  354.8 21.4 %mix_fwd.4 = (bf16[1024,1024]{1,0:T(8,128)(2,1)}, bf16[1024,1024]{1,0:T(8,128)(2,1)}, f32[1024,128]{1,0:T(8,128)S(1)}, f32[4,128,1024]{2,1,0:T(8,128)}, f32[128,1024]{1,0:T(8,128)S(1)}) custom-call(s32[4]{0:T(128)S(1)} %add_xor_fusion.perm_ref, bf16[1024,2432]{1,0:T(8,128)(2,1)} %convolution_convert_fusion.5.gate_ref.x_ref.bc_ref.st_ref.hx_ref.hbc_ref.px_ref.pbc_ref, ...), custom_call_target="tpu_custom_call" | custom-call | flops 29360128000 | bytes 12582912 | tf_op jit(solution)/shard_map/mix_fwd/pallas_call | solution.py:207
  376.4 10.7 collective-permute-start.16
  393.1 7.4 convolution_convert_fusion.15
  404.2 15.2 convolution_convert_fusion.4.gate_ref.x_ref.bc_ref.st_ref.px_ref.pbc_ref
  419.4 19.9 %collective-permute-done.21 = bf16[512,2048]{1,0:T(8,128)(2,1)} collective-permute-done((bf16[512,2048]{1,0:T(8,128)(2,1)}, bf16[512,2048]{1,0:T(8,128)(2,1)}, u32[]{:S(2)}, u32[]{:S(2)}) %collective-permute-start.21) | collective-permute-done | bytes 2097184 | tf_op jit(solution)/shard_map/ppermute | solution.py:549
  445.2 21.8 %mix_fwd.5 = (bf16[1024,1024]{1,0:T(8,128)(2,1)}, bf16[1024,1024]{1,0:T(8,128)(2,1)}, f32[1024,128]{1,0:T(8,128)S(1)}, f32[4,128,1024]{2,1,0:T(8,128)}, f32[128,1024]{1,0:T(8,128)}) custom-call(s32[4]{0:T(128)S(1)} %add_xor_fusion.perm_ref, bf16[1024,2432]{1,0:T(8,128)(2,1)} %convolution_convert_fusion.4.gate_ref.x_ref.bc_ref.st_ref.px_ref.pbc_ref, ...), custom_call_target="tpu_custom_call" | custom-call | flops 29360128000 | bytes 12582912 | tf_op jit(solution)/shard_map/mix_fwd/pallas_call | solution.py:207
  478.3 6.4 convolution_convert_fusion.14
  487.7 13.9 collective-permute-done.24
  501.7 8.3 pad_maximum_fusion.1
  524.7 13.5 gather_fusion.3
  538.2 13.3 gather_fusion.2
  559.8 12.8 convolution_convert_fusion.3.gate_ref.x_ref.bc_ref.st_ref.hx_ref.hbc_ref.px_ref.pbc_ref
  572.6 21.4 %mix_fwd.6 = (bf16[1024,1024]{1,0:T(8,128)(2,1)}, bf16[1024,1024]{1,0:T(8,128)(2,1)}, f32[1024,128]{1,0:T(8,128)S(1)}, f32[4,128,1024]{2,1,0:T(8,128)}, f32[128,1024]{1,0:T(8,128)S(1)}) custom-call(s32[4]{0:T(128)S(1)} %add_xor_fusion.perm_ref, bf16[1024,2432]{1,0:T(8,128)(2,1)} %convolution_convert_fusion.3.gate_ref.x_ref.bc_ref.st_ref.hx_ref.hbc_ref.px_ref.pbc_ref, ...), custom_call_target="tpu_custom_call" | custom-call | flops 29360128000 | bytes 12582912 | tf_op jit(solution)/shard_map/mix_fwd/pallas_call | solution.py:207
  594.0 7.5 convolution_convert_fusion.13
  618.8 15.2 convolution_convert_fusion.2.gate_ref.x_ref.bc_ref.st_ref.px_ref.pbc_ref
  633.9 21.6 %mix_fwd.7 = (bf16[1024,1024]{1,0:T(8,128)(2,1)}, bf16[1024,1024]{1,0:T(8,128)(2,1)}, f32[1024,128]{1,0:T(8,128)S(1)}, f32[4,128,1024]{2,1,0:T(8,128)}, f32[128,1024]{1,0:T(8,128)}) custom-call(s32[4]{0:T(128)S(1)} %add_xor_fusion.perm_ref, bf16[1024,2432]{1,0:T(8,128)(2,1)} %convolution_convert_fusion.2.gate_ref.x_ref.bc_ref.st_ref.px_ref.pbc_ref, ...), custom_call_target="tpu_custom_call" | custom-call | flops 29360128000 | bytes 12582912 | tf_op jit(solution)/shard_map/mix_fwd/pallas_call | solution.py:207
  655.5 7.2 convolution_convert_fusion.12
  678.6 19.4 %collective-permute-done.37 = f32[1,256]{1,0:T(1,128)S(1)} collective-permute-done((f32[1,256]{1,0:T(1,128)S(1)}, f32[1,256]{1,0:T(1,128)S(1)}, u32[]{:S(2)}, u32[]{:S(2)}) %collective-permute-start.37) | collective-permute-done | bytes 1056 | tf_op jit(solution)/shard_map/ppermute | solution.py:549
  708.0 7.7 convolution_convert_fusion.11
  715.8 6.8 add_convert_fusion.3
  722.6 9.2 convolution_convert_fusion.19.u_ref
  731.9 44.1 %mix_bwd.4 = (bf16[1024,2432]{1,0:T(8,128)(2,1)}, f32[8,1024]{1,0:T(8,128)S(1)}, f32[8,256]{1,0:T(8,128)S(1)}, f32[8,128]{1,0:T(8,128)S(1)}, f32[128,1024]{1,0:T...) custom-call(s32[4]{0:T(128)S(1)} %add_xor_fusion.perm_ref, ...), custom_call_target="tpu_custom_call" | custom-call | flops 58720256000 | bytes 25165824 | tf_op jit(solution)/shard_map/mix_bwd/pallas_call | solution.py:456
  776.0 15.5 %convolution_convert_fusion.9 = bf16[1024,2048]{1,0:T(8,128)(2,1)S(1)} fusion(bf16[1024,2432]{1,0:T(8,128)(2,1)} %get-tuple-element.170, bf16[2048,2432]{1,0:T(8,128)(2,1)} %all-gather.6.cloned.1.call-done), kind=kOutput, calls=%fused_computation.47 | convolution fusion | flops 10202644480 | bytes 19136512 | tf_op jit(solution)/shard_map/dot_general | solution.py:32
  800.2 9.4 convolution_convert_fusion.18.u_ref
  810.8 44.3 %mix_bwd.5 = (bf16[1024,2432]{1,0:T(8,128)(2,1)}, f32[8,1024]{1,0:T(8,128)S(1)}, f32[8,256]{1,0:T(8,128)S(1)}, f32[8,128]{1,0:T(8,128)S(1)}, f32[128,1024]{1,0:T...) custom-call(s32[4]{0:T(128)S(1)} %add_xor_fusion.perm_ref, ...), custom_call_target="tpu_custom_call" | custom-call | flops 58720256000 | bytes 25165824 | tf_op jit(solution)/shard_map/mix_bwd/pallas_call | solution.py:456
  864.1 23.6 %collective-permute-done.49 = bf16[256,2048]{1,0:T(8,128)(2,1)S(1)} collective-permute-done((bf16[256,2048]{1,0:T(8,128)(2,1)S(1)}, bf16[256,2048]{1,0:T(8,128)(2,1)S(1)}, u32[]{:S(2)}, u32[]{:S(2)}) %collective-permute-start.49) | collective-permute-done | bytes 1048608 | tf_op jit(solution)/shard_map/ppermute | solution.py:549
  897.5 16.6 %convolution_convert_fusion.8 = bf16[1024,2048]{1,0:T(8,128)(2,1)} fusion(bf16[1024,2432]{1,0:T(8,128)(2,1)} %get-tuple-element.171, bf16[2048,2432]{1,0:T(8,128)(2,1)} %all-gather.6.cloned.1.call-done), kind=kOutput, calls=%fused_computation.46 | convolution fusion | flops 10202644480 | bytes 19136512 | tf_op jit(solution)/shard_map/dot_general | solution.py:32
  914.1 16.1 %convolution_convert_fusion.1 = bf16[2048,2432]{1,0:T(8,128)(2,1)} fusion(bf16[1024,2432]{1,0:T(8,128)(2,1)S(1)} %bitcast.359, bf16[512,2048]{1,0:T(8,128)(2,1)} %collective-permute-done.32, bf16[512,2048]{1,0:T(8,128)(2,1)} %pad_maximum_fusion.15), kind=kOutput, calls=%fused_computation.11 | convolution fusion | flops 10213916672 | bytes 19136512 | tf_op jit(solution)/shard_map/dot_general | solution.py:36
  931.1 18.3 %add_convert_fusion.1 = bf16[2048,2432]{1,0:T(8,128)(2,1)} fusion(bf16[2048,2432]{1,0:T(8,128)(2,1)} %convolution_convert_fusion.1, bf16[1024,2432]{1,0:T(8,128)(2,1)} %get-tuple-element.171, bf16[512,2048]{1,0:T(8,128)(2,1)} %collective-permute-done.20, bf16[512,2048]{1,0:T(8,128)(2,1)S(1)} %copy-done.35), kind=kOutput, calls=%fused_computation.7 | convolution fusion | flops 10223878144 | bytes 29097984 | tf_op jit(solution)/shard_map/dot_general | solution.py:36
  977.6 18.7 %reduce-scatter.5.cloned.1.call-done = bf16[256,1024]{1,0:T(8,128)(2,1)} async-done(((bf16[2048,1024]{1,0:T(8,128)(2,1)}), bf16[256,1024]{1,0:T(8,128)(2,1)}) %reduce-scatter.5.cloned.1.call-update) | async-done | bytes 524304 | tf_op jit(solution)/shard_map/reduce_scatter | solution.py:1138
  1004.5 44.8 %mix_bwd.6 = (bf16[1024,2432]{1,0:T(8,128)(2,1)}, f32[8,1024]{1,0:T(8,128)S(1)}, f32[8,256]{1,0:T(8,128)S(1)}, f32[8,128]{1,0:T(8,128)S(1)}, f32[128,1024]{1,0:T...) custom-call(s32[4]{0:T(128)S(1)} %add_xor_fusion.perm_ref, ...), custom_call_target="tpu_custom_call" | custom-call | flops 58720256000 | bytes 25165824 | tf_op jit(solution)/shard_map/mix_bwd/pallas_call | solution.py:456
  1059.4 13.8 convolution_convert_fusion.7
  1075.2 8.4 collective-permute-done.64
  1083.6 6.9 convolution_convert_fusion.10
  1092.7 11.7 collective-permute-done.46
  1109.5 15.7 %convolution_convert_fusion = bf16[2048,2432]{1,0:T(8,128)(2,1)} fusion(bf16[1024,2048]{1,0:T(8,128)(2,1)S(1)} %copy-done.44, bf16[1024,2432]{1,0:T(8,128)(2,1)} %get-tuple-element.185), kind=kOutput, calls=%fused_computation.10 | convolution fusion | flops 10205528064 | bytes 19136512 | tf_op jit(solution)/shard_map/dot_general | solution.py:36
  1132.1 6.6 add_convert_fusion.2
  1138.7 9.3 convolution_convert_fusion.16.u_ref
  1148.1 44.4 %mix_bwd.7 = (bf16[1024,2432]{1,0:T(8,128)(2,1)}, f32[8,1024]{1,0:T(8,128)S(1)}, f32[8,256]{1,0:T(8,128)S(1)}, f32[8,128]{1,0:T(8,128)S(1)}, f32[128,1024]{1,0:T...) custom-call(s32[4]{0:T(128)S(1)} %add_xor_fusion.perm_ref, ...), custom_call_target="tpu_custom_call" | custom-call | flops 58720256000 | bytes 25165824 | tf_op jit(solution)/shard_map/mix_bwd/pallas_call | solution.py:456
  1214.0 11.0 all-to-all-done.2.refs_1_
  1225.0 18.4 %add_convert_fusion = bf16[2048,2432]{1,0:T(8,128)(2,1)} fusion(bf16[2048,2432]{1,0:T(8,128)(2,1)} %convolution_convert_fusion, bf16[1024,2048]{1,0:T(8,128)(2,1)} %copy-done.42, bf16[1024,2432]{1,0:T(8,128)(2,1)} %get-tuple-element.202), kind=kOutput, calls=%fused_computation.6 | convolution fusion | flops 10215489536 | bytes 29097984 | tf_op jit(solution)/shard_map/dot_general | solution.py:36
  1245.7 15.4 %convolution_convert_fusion.6 = bf16[1024,2048]{1,0:T(8,128)(2,1)S(1)} fusion(bf16[1024,2432]{1,0:T(8,128)(2,1)} %get-tuple-element.202, bf16[2048,2432]{0,1:T(8,128)(2,1)} %constant_dynamic-update-slice_fusion), kind=kOutput, calls=%fused_computation.44 | convolution fusion | flops 10202644480 | bytes 19136512 | tf_op jit(solution)/shard_map/dot_general | solution.py:32
  1268.1 24.0 %collective-permute-done.70 = bf16[256,2048]{1,0:T(8,128)(2,1)S(1)} collective-permute-done((bf16[256,2048]{1,0:T(8,128)(2,1)S(1)}, bf16[256,2048]{1,0:T(8,128)(2,1)S(1)}, u32[]{:S(2)}, u32[]{:S(2)}) %collective-permute-start.70) | collective-permute-done | bytes 1048608 | tf_op jit(solution)/shard_map/ppermute | solution.py:549
  1295.8 18.8 %collective-permute-done.73 = bf16[256,2048]{1,0:T(8,128)(2,1)S(1)} collective-permute-done((bf16[256,2048]{1,0:T(8,128)(2,1)S(1)}, bf16[256,2048]{1,0:T(8,128)(2,1)S(1)}, u32[]{:S(2)}, u32[]{:S(2)}) %collective-permute-start.73) | collective-permute-done | bytes 1048608 | tf_op jit(solution)/shard_map/ppermute | solution.py:549
  1316.1 20.1 %collective-permute-done.71 = bf16[256,2048]{1,0:T(8,128)(2,1)S(1)} collective-permute-done((bf16[256,2048]{1,0:T(8,128)(2,1)S(1)}, bf16[256,2048]{1,0:T(8,128)(2,1)S(1)}, u32[]{:S(2)}, u32[]{:S(2)}) %collective-permute-start.71) | collective-permute-done | bytes 1048608 | tf_op jit(solution)/shard_map/ppermute | solution.py:549
  1338.6 8.6 pad_maximum_fusion.2
  1347.3 9.0 gather_fusion.4
  1361.6 7.1 pad_maximum_fusion.3
  1368.7 9.8 gather_fusion.5
  1392.4 50.2 %collective-permute-done.76.second_ref = bf16[256,2048]{1,0:T(8,128)(2,1)} collective-permute-done((bf16[256,2048]{1,0:T(8,128)(2,1)}, bf16[256,2048]{1,0:T(8,128)(2,1)}, u32[]{:S(2)}, u32[]{:S(2)}) %collective-permute-start.76) | collective-permute-done | bytes 1048608 | tf_op jit(solution)/shard_map/ppermute | solution.py:678
  1446.4 28.6 %reduce-scatter.9.cloned.1.call-done = bf16[256,2432]{1,0:T(8,128)(2,1)} async-done(((bf16[2048,2432]{1,0:T(8,128)(2,1)}), bf16[256,2432]{1,0:T(8,128)(2,1)}) %reduce-scatter.9.cloned.1.call-update) | async-done | bytes 1245200 | tf_op jit(solution)/shard_map/reduce_scatter | solution.py:1138
  1474.9 23.0 %all-to-all-start.4 = ((bf16[4,64,2432]{2,1,0:T(8,128)(2,1)}), bf16[4,64,2432]{2,1,0:T(8,128)(2,1)S(1)}, u32[]{:S(2)}, u32[]{:S(2)}) async-start(bf16[4,64,2432]{2,1,0:T(8,128)(2,1)} %bitcast.272), calls=%async_computation.7 | async-start | bytes 2490368 | tf_op jit(solution)/shard_map/all_to_all | solution.py:742
  1500.4 14.4 all-to-all-done.4.refs_0_
  (788 shorter events, 391.2 us)
Async XLA Ops:
  21.8 22.5 %all-to-all-start = ((bf16[64,4,2432]{2,0,1:T(8,128)(2,1)}), bf16[64,4,2432]{2,0,1:T(8,128)(2,1)}, u32[]{:S(2)}, u32[]{:S(2)}) async-start(bf16[64,4,2432]{2,0,1:T(8,128)(2,1)} %concatenate.282), calls=%async_computation | async-start | bytes 2490368 | tf_op jit(solution)/shard_map/all_to_all | solution.py:731
  45.9 39.9 %all-to-all-start.1 = ((bf16[64,4,4480]{2,0,1:T(8,128)(2,1)}), bf16[64,4,4480]{2,0,1:T(8,128)(2,1)}, u32[]{:S(2)}, u32[]{:S(2)}) async-start(bf16[64,4,4480]{2,0,1:T(8,128)(2,1)} %copy.192), calls=%async_computation.1 | async-start | bytes 4587520 | tf_op jit(solution)/shard_map/all_to_all | solution.py:731
  50.5 342.6 %all-gather.4.cloned.1.call-start = ((), (), s32[]{:S(2)}) async-start(), calls=%async_computation.10 | async-start | bytes 4718592 | tf_op jit(solution)/shard_map/all_gather | solution.py:736
  53.5 22.1 %collective-permute-start = (bf16[256,2048]{1,0:T(8,128)(2,1)S(1)}, bf16[256,2048]{1,0:T(8,128)(2,1)S(1)}, u32[]{:S(2)}, u32[]{:S(2)}) collective-permute-start(bf16[256,2048]{1,0:T(8,128)(2,1)S(1)} %get-tuple-element.110), channel_id=1, source_target_pairs={{0,0},{2,2},{4,8},{6,10},{8,4},{10,6},{12,12},{14,14},{1,1},{3,3},... | collective-permute-start | bytes 3145736 | tf_op jit(solution)/shard_map/ppermute | solution.py:673
  54.2 26.8 %collective-permute-start.1 = (bf16[256,2048]{1,0:T(8,128)(2,1)}, bf16[256,2048]{1,0:T(8,128)(2,1)}, u32[]{:S(2)}, u32[]{:S(2)}) collective-permute-start(bf16[256,2048]{1,0:T(8,128)(2,1)} %get-tuple-element.111), channel_id=1, source_target_pairs={{0,2},{2,0},{4,10},{6,8},{8,6},{10,4},{12,14},{14,12},{1,3},{3,1},... | collective-permute-start | bytes 3145736 | tf_op jit(solution)/shard_map/ppermute | solution.py:673
  57.3 17.5 %collective-permute-start.14 = (s32[2,1,3]{2,1,0:T(1,128)S(1)}, s32[2,1,3]{2,1,0:T(1,128)S(1)}, u32[]{:S(2)}, u32[]{:S(2)}) collective-permute-start(s32[2,1,3]{2,1,0:T(1,128)S(1)} %copy-done.102), channel_id=1, source_target_pairs={{0,8},{8,0},{1,9},{9,1},{2,10},{10,2},{3,11},{11,3},{4,12},{12,4},... | collective-permute-start | bytes 80 | tf_op jit(solution)/shard_map/ppermute | solution.py:549
  61.0 27.8 %collective-permute-start.4 = (s32[2,1,2048]{2,1,0:T(1,128)S(1)}, s32[2,1,2048]{2,1,0:T(1,128)S(1)}, u32[]{:S(2)}, u32[]{:S(2)}) collective-permute-start(s32[2,1,2048]{2,1,0:T(1,128)S(1)} %copy-done.72), channel_id=1, source_target_pairs={{0,8},{8,0},{1,9},{9,1},{2,10},{10,2},{3,11},{11,3},{4,12},{12,4},... | collective-permute-start | bytes 49160 | tf_op jit(solution)/shard_map/ppermute | solution.py:549
  84.0 32.8 %collective-permute-start.2 = (bf16[512,2048]{1,0:T(8,128)(2,1)}, bf16[512,2048]{1,0:T(8,128)(2,1)}, u32[]{:S(2)}, u32[]{:S(2)}) collective-permute-start(bf16[512,2048]{1,0:T(8,128)(2,1)} %pad_maximum_fusion.12), channel_id=1, source_target_pairs={{0,1},{1,0},{2,3},{3,2},{4,5},{5,4},{6,7},{7,6},{8,9},{9,8},{10,11... | collective-permute-start | bytes 6291464 | tf_op jit(solution)/shard_map/ppermute | solution.py:549
  88.0 384.3 %all-gather.6.cloned.1.call-start = ((), (), s32[]{:S(2)}) async-start(), calls=%async_computation.11 | async-start | bytes 11206656 | tf_op jit(solution)/shard_map/all_gather | solution.py:736
  88.9 49.7 %collective-permute-start.6 = (bf16[256,2432]{1,0:T(8,128)(2,1)}, bf16[256,2432]{1,0:T(8,128)(2,1)}, u32[]{:S(2)}, u32[]{:S(2)}) collective-permute-start(bf16[256,2432]{1,0:T(8,128)(2,1)} %bitcast.15), channel_id=1, source_target_pairs={{2,0},{4,2},{6,4},{22,6},{20,22},{18,20},{16,18},{0,16},{3,1},{5,3... | collective-permute-start | bytes 3735560 | tf_op jit(solution)/shard_map/ppermute | solution.py:625
  91.3 49.3 %collective-permute-start.5 = (bf16[256,2432]{1,0:T(8,128)(2,1)}, bf16[256,2432]{1,0:T(8,128)(2,1)}, u32[]{:S(2)}, u32[]{:S(2)}) collective-permute-start(bf16[256,2432]{1,0:T(8,128)(2,1)} %bitcast.15), channel_id=1, source_target_pairs={{0,2},{2,4},{4,6},{6,22},{22,20},{20,18},{18,16},{16,0},{1,3},{3,5... | collective-permute-start | bytes 3735560 | tf_op jit(solution)/shard_map/ppermute | solution.py:622
  120.4 131.8 %collective-permute-start.3 = (bf16[1024,2048]{1,0:T(8,128)(2,1)}, bf16[1024,2048]{1,0:T(8,128)(2,1)}, u32[]{:S(2)}, u32[]{:S(2)}) collective-permute-start(bf16[1024,2048]{1,0:T(8,128)(2,1)} %pad_maximum_fusion.4), channel_id=1, source_target_pairs={{0,8},{8,0},{1,9},{9,1},{2,10},{10,2},{3,11},{11,3},{4,12},{12,4},... | collective-permute-start | bytes 12582920 | tf_op jit(solution)/shard_map/ppermute | solution.py:549
  138.6 78.9 %collective-permute-start.8 = (bf16[256,2432]{1,0:T(8,128)(2,1)}, bf16[256,2432]{1,0:T(8,128)(2,1)}, u32[]{:S(2)}, u32[]{:S(2)}) collective-permute-start(bf16[256,2432]{1,0:T(8,128)(2,1)} %collective-permute-done.6), channel_id=1, source_target_pairs={{2,0},{4,2},{6,4},{22,6},{20,22},{18,20},{16,18},{0,16},{3,1},{5,3... | collective-permute-start | bytes 3735560 | tf_op jit(solution)/shard_map/ppermute | solution.py:625
  140.6 76.9 %collective-permute-start.7 = (bf16[256,2432]{1,0:T(8,128)(2,1)}, bf16[256,2432]{1,0:T(8,128)(2,1)}, u32[]{:S(2)}, u32[]{:S(2)}) collective-permute-start(bf16[256,2432]{1,0:T(8,128)(2,1)} %collective-permute-done.5), channel_id=1, source_target_pairs={{0,2},{2,4},{4,6},{6,22},{22,20},{20,18},{18,16},{16,0},{1,3},{3,5... | collective-permute-start | bytes 3735560 | tf_op jit(solution)/shard_map/ppermute | solution.py:622
  217.5 30.1 %collective-permute-start.10 = (bf16[256,2432]{1,0:T(8,128)(2,1)}, bf16[256,2432]{1,0:T(8,128)(2,1)}, u32[]{:S(2)}, u32[]{:S(2)}) collective-permute-start(bf16[256,2432]{1,0:T(8,128)(2,1)} %collective-permute-done.8), channel_id=1, source_target_pairs={{2,0},{4,2},{6,4},{22,6},{20,22},{18,20},{16,18},{0,16},{3,1},{5,3... | collective-permute-start | bytes 3735560 | tf_op jit(solution)/shard_map/ppermute | solution.py:625
  217.5 31.9 %collective-permute-start.9 = (bf16[256,2432]{1,0:T(8,128)(2,1)}, bf16[256,2432]{1,0:T(8,128)(2,1)}, u32[]{:S(2)}, u32[]{:S(2)}) collective-permute-start(bf16[256,2432]{1,0:T(8,128)(2,1)} %collective-permute-done.7), channel_id=1, source_target_pairs={{0,2},{2,4},{4,6},{6,22},{22,20},{20,18},{18,16},{16,0},{1,3},{3,5... | collective-permute-start | bytes 3735560 | tf_op jit(solution)/shard_map/ppermute | solution.py:622
  260.8 39.2 %collective-permute-start.11 = (bf16[256,2432]{1,0:T(8,128)(2,1)}, bf16[256,2432]{1,0:T(8,128)(2,1)}, u32[]{:S(2)}, u32[]{:S(2)}) collective-permute-start(bf16[256,2432]{1,0:T(8,128)(2,1)} %collective-permute-done.9), channel_id=1, source_target_pairs={{0,2},{2,4},{4,6},{6,22},{22,20},{20,18},{18,16},{16,0},{1,3},{3,5... | collective-permute-start | bytes 3735560 | tf_op jit(solution)/shard_map/ppermute | solution.py:622
  293.3 36.1 %collective-permute-start.12 = (bf16[256,2048]{1,0:T(8,128)(2,1)S(1)}, bf16[256,2048]{1,0:T(8,128)(2,1)}, u32[]{:S(2)}, u32[]{:S(2)}) collective-permute-start(bf16[256,2048]{1,0:T(8,128)(2,1)S(1)} %get-tuple-element.117), channel_id=1, source_target_pairs={{0,0},{2,2},{4,8},{6,10},{8,4},{10,6},{12,12},{14,14},{1,1},{3,3},... | collective-permute-start | bytes 3145736 | tf_op jit(solution)/shard_map/ppermute | solution.py:673
  294.9 58.9 %collective-permute-start.13 = (bf16[256,2048]{1,0:T(8,128)(2,1)}, bf16[256,2048]{1,0:T(8,128)(2,1)}, u32[]{:S(2)}, u32[]{:S(2)}) collective-permute-start(bf16[256,2048]{1,0:T(8,128)(2,1)} %get-tuple-element.118), channel_id=1, source_target_pairs={{0,2},{2,0},{4,10},{6,8},{8,6},{10,4},{12,14},{14,12},{1,3},{3,1},... | collective-permute-start | bytes 3145736 | tf_op jit(solution)/shard_map/ppermute | solution.py:673
  295.4 298.6 %all-gather.8.cloned.1.call-start = ((), (), s32[]{:S(2)}) async-start(), calls=%async_computation.12 | async-start | bytes 4718592 | tf_op jit(solution)/shard_map/all_gather | solution.py:736
  391.1 48.2 %collective-permute-start.21 = (bf16[512,2048]{1,0:T(8,128)(2,1)}, bf16[512,2048]{1,0:T(8,128)(2,1)}, u32[]{:S(2)}, u32[]{:S(2)}) collective-permute-start(bf16[512,2048]{1,0:T(8,128)(2,1)} %pad_maximum_fusion.14), channel_id=1, source_target_pairs={{0,1},{1,0},{2,3},{3,2},{4,5},{5,4},{6,7},{7,6},{8,9},{9,8},{10,11... | collective-permute-start | bytes 6291464 | tf_op jit(solution)/shard_map/ppermute | solution.py:549
  400.8 42.2 %collective-permute-start.15 = (bf16[512,2048]{1,0:T(8,128)(2,1)S(1)}, bf16[512,2048]{1,0:T(8,128)(2,1)S(1)}, u32[]{:S(2)}, u32[]{:S(2)}) collective-permute-start(bf16[512,2048]{1,0:T(8,128)(2,1)S(1)} %slice.719), channel_id=1, source_target_pairs={{0,8},{8,0},{1,9},{9,1},{2,10},{10,2},{3,11},{11,3},{4,12},{12,4},... | collective-permute-start | bytes 6291464 | tf_op jit(solution)/shard_map/ppermute | solution.py:549
  443.0 58.7 %collective-permute-start.25 = (bf16[1024,2048]{1,0:T(8,128)(2,1)}, bf16[1024,2048]{1,0:T(8,128)(2,1)}, u32[]{:S(2)}, u32[]{:S(2)}) collective-permute-start(bf16[1024,2048]{1,0:T(8,128)(2,1)} %pad_maximum_fusion.6), channel_id=1, source_target_pairs={{0,8},{8,0},{1,9},{9,1},{2,10},{10,2},{3,11},{11,3},{4,12},{12,4},... | collective-permute-start | bytes 12582920 | tf_op jit(solution)/shard_map/ppermute | solution.py:549
  443.4 25.7 %collective-permute-start.18 = (bf16[256,2048]{1,0:T(8,128)(2,1)S(1)}, bf16[256,2048]{1,0:T(8,128)(2,1)}, u32[]{:S(2)}, u32[]{:S(2)}) collective-permute-start(bf16[256,2048]{1,0:T(8,128)(2,1)S(1)} %add_convert_fusion.13), channel_id=1, source_target_pairs={{0,1},{1,0},{2,3},{3,2},{4,5},{5,4},{6,7},{7,6},{8,9},{9,8},{10,11... | collective-permute-start | bytes 3145736 | tf_op jit(solution)/shard_map/ppermute | solution.py:549
  467.3 20.1 %collective-permute-start.23 = (f32[512]{0:T(512)S(1)}, f32[512]{0:T(512)S(1)}, u32[]{:S(2)}, u32[]{:S(2)}) collective-permute-start(f32[512]{0:T(512)S(1)} %slice.594), channel_id=1, source_target_pairs={{0,8},{8,0},{1,9},{9,1},{2,10},{10,2},{3,11},{11,3},{4,12},{12,4},... | collective-permute-start | bytes 6152 | tf_op jit(solution)/shard_map/ppermute | solution.py:549
  476.5 33.5 %collective-permute-start.19 = (bf16[256,2048]{1,0:T(8,128)(2,1)}, bf16[256,2048]{1,0:T(8,128)(2,1)}, u32[]{:S(2)}, u32[]{:S(2)}) collective-permute-start(bf16[256,2048]{1,0:T(8,128)(2,1)} %multiply_convert_fusion.9), channel_id=1, source_target_pairs={{0,1},{1,0},{2,3},{3,2},{4,5},{5,4},{6,7},{7,6},{8,9},{9,8},{10,11... | collective-permute-start | bytes 3145736 | tf_op jit(solution)/shard_map/ppermute | solution.py:549
  487.3 31.0 %collective-permute-start.22 = (bf16[512,2048]{1,0:T(8,128)(2,1)}, bf16[512,2048]{1,0:T(8,128)(2,1)}, u32[]{:S(2)}, u32[]{:S(2)}) collective-permute-start(bf16[512,2048]{1,0:T(8,128)(2,1)} %slice.729), channel_id=1, source_target_pairs={{0,8},{8,0},{1,9},{9,1},{2,10},{10,2},{3,11},{11,3},{4,12},{12,4},... | collective-permute-start | bytes 6291464 | tf_op jit(solution)/shard_map/ppermute | solution.py:549
  487.3 14.3 collective-permute-start.24
  487.7 508.7 %reduce-scatter.5.cloned.1.call-start = ((), (), s32[]{:S(2)}) async-start(), calls=%async_computation.13 | async-start | bytes 4718592 | tf_op jit(solution)/shard_map/reduce_scatter | solution.py:1138
  511.9 39.9 %collective-permute-start.20 = (bf16[512,2048]{1,0:T(8,128)(2,1)S(1)}, bf16[512,2048]{1,0:T(8,128)(2,1)}, u32[]{:S(2)}, u32[]{:S(2)}) collective-permute-start(bf16[512,2048]{1,0:T(8,128)(2,1)S(1)} %pad_maximum_fusion.13), channel_id=1, source_target_pairs={{0,8},{8,0},{1,9},{9,1},{2,10},{10,2},{3,11},{11,3},{4,12},{12,4},... | collective-permute-start | bytes 6291464 | tf_op jit(solution)/shard_map/ppermute | solution.py:549
  521.2 33.1 %collective-permute-start.26 = (bf16[256,2048]{1,0:T(8,128)(2,1)}, bf16[256,2048]{1,0:T(8,128)(2,1)}, u32[]{:S(2)}, u32[]{:S(2)}) collective-permute-start(bf16[256,2048]{1,0:T(8,128)(2,1)} %add_convert_fusion.12), channel_id=1, source_target_pairs={{0,1},{1,0},{2,3},{3,2},{4,5},{5,4},{6,7},{7,6},{8,9},{9,8},{10,11... | collective-permute-start | bytes 3145736 | tf_op jit(solution)/shard_map/ppermute | solution.py:549
  559.4 43.7 %collective-permute-start.31 = (bf16[256,2048]{1,0:T(8,128)(2,1)S(1)}, bf16[256,2048]{1,0:T(8,128)(2,1)}, u32[]{:S(2)}, u32[]{:S(2)}) collective-permute-start(bf16[256,2048]{1,0:T(8,128)(2,1)S(1)} %multiply_convert_fusion.8), channel_id=1, source_target_pairs={{0,1},{1,0},{2,3},{3,2},{4,5},{5,4},{6,7},{7,6},{8,9},{9,8},{10,11... | collective-permute-start | bytes 3145736 | tf_op jit(solution)/shard_map/ppermute | solution.py:549
  614.3 41.2 %collective-permute-start.30 = (bf16[256,2048]{1,0:T(8,128)(2,1)S(1)}, bf16[256,2048]{1,0:T(8,128)(2,1)S(1)}, u32[]{:S(2)}, u32[]{:S(2)}) collective-permute-start(bf16[256,2048]{1,0:T(8,128)(2,1)S(1)} %add_convert_fusion.11), channel_id=1, source_target_pairs={{0,1},{1,0},{2,3},{3,2},{4,5},{5,4},{6,7},{7,6},{8,9},{9,8},{10,11... | collective-permute-start | bytes 3145736 | tf_op jit(solution)/shard_map/ppermute | solution.py:549
  673.9 24.1 %collective-permute-start.40 = (bf16[256,2048]{1,0:T(8,128)(2,1)S(1)}, bf16[256,2048]{1,0:T(8,128)(2,1)S(1)}, u32[]{:S(2)}, u32[]{:S(2)}) collective-permute-start(bf16[256,2048]{1,0:T(8,128)(2,1)S(1)} %add_convert_fusion.9), channel_id=1, source_target_pairs={{0,1},{1,0},{2,3},{3,2},{4,5},{5,4},{6,7},{7,6},{8,9},{9,8},{10,11... | collective-permute-start | bytes 3145736 | tf_op jit(solution)/shard_map/ppermute | solution.py:549
  677.0 21.0 %collective-permute-start.37 = (f32[1,256]{1,0:T(1,128)S(1)}, f32[1,256]{1,0:T(1,128)S(1)}, u32[]{:S(2)}, u32[]{:S(2)}) collective-permute-start(f32[1,256]{1,0:T(1,128)S(1)} %bitcast.332), channel_id=1, source_target_pairs={{0,1},{1,0},{2,3},{3,2},{4,5},{5,4},{6,7},{7,6},{8,9},{9,8},{10,11... | collective-permute-start | bytes 3080 | tf_op jit(solution)/shard_map/ppermute | solution.py:549
  793.2 16.4 %collective-permute-start.43 = (bf16[512,2048]{1,0:T(8,128)(2,1)}, bf16[512,2048]{1,0:T(8,128)(2,1)S(1)}, u32[]{:S(2)}, u32[]{:S(2)}) collective-permute-start(bf16[512,2048]{1,0:T(8,128)(2,1)} %slice.755), channel_id=1, source_target_pairs={{0,8},{8,0},{1,9},{9,1},{2,10},{10,2},{3,11},{11,3},{4,12},{12,4},... | collective-permute-start | bytes 6291464 | tf_op jit(solution)/shard_map/ppermute | solution.py:549
  810.0 45.1 %collective-permute-start.48 = (bf16[256,2048]{1,0:T(8,128)(2,1)S(1)}, bf16[256,2048]{1,0:T(8,128)(2,1)S(1)}, u32[]{:S(2)}, u32[]{:S(2)}) collective-permute-start(bf16[256,2048]{1,0:T(8,128)(2,1)S(1)} %add_convert_fusion.8), channel_id=1, source_target_pairs={{0,1},{1,0},{2,3},{3,2},{4,5},{5,4},{6,7},{7,6},{8,9},{9,8},{10,11... | collective-permute-start | bytes 3145736 | tf_op jit(solution)/shard_map/ppermute | solution.py:549
  862.7 25.0 %collective-permute-start.49 = (bf16[256,2048]{1,0:T(8,128)(2,1)S(1)}, bf16[256,2048]{1,0:T(8,128)(2,1)S(1)}, u32[]{:S(2)}, u32[]{:S(2)}) collective-permute-start(bf16[256,2048]{1,0:T(8,128)(2,1)S(1)} %get-tuple-element.167), channel_id=1, source_target_pairs={{0,1},{1,0},{2,3},{3,2},{4,5},{5,4},{6,7},{7,6},{8,9},{9,8},{10,11... | collective-permute-start | bytes 3145736 | tf_op jit(solution)/shard_map/ppermute | solution.py:549
  888.0 316.1 %reduce-scatter.7.cloned.1.call-start = ((), (), s32[]{:S(2)}) async-start(), calls=%async_computation.14 | async-start | bytes 11206656 | tf_op jit(solution)/shard_map/reduce_scatter | solution.py:1138
  891.5 38.7 %collective-permute-start.53 = (bf16[256,2048]{1,0:T(8,128)(2,1)}, bf16[256,2048]{1,0:T(8,128)(2,1)S(1)}, u32[]{:S(2)}, u32[]{:S(2)}) collective-permute-start(bf16[256,2048]{1,0:T(8,128)(2,1)} %get-tuple-element.222), channel_id=1, source_target_pairs={{0,1},{1,0},{2,3},{3,2},{4,5},{5,4},{6,7},{7,6},{8,9},{9,8},{10,11... | collective-permute-start | bytes 3145736 | tf_op jit(solution)/shard_map/ppermute | solution.py:549
  961.7 38.8 %collective-permute-start.51 = (bf16[512,2048]{1,0:T(8,128)(2,1)}, bf16[512,2048]{1,0:T(8,128)(2,1)}, u32[]{:S(2)}, u32[]{:S(2)}) collective-permute-start(bf16[512,2048]{1,0:T(8,128)(2,1)} %slice.761), channel_id=1, source_target_pairs={{0,8},{8,0},{1,9},{9,1},{2,10},{10,2},{3,11},{11,3},{4,12},{12,4},... | collective-permute-start | bytes 6291464 | tf_op jit(solution)/shard_map/ppermute | solution.py:549
  996.4 207.7 %all-to-all-start.3 = ((bf16[4,64,1024]{2,1,0:T(8,128)(2,1)}), bf16[4,64,1024]{2,1,0:T(8,128)(2,1)}, u32[]{:S(2)}, u32[]{:S(2)}) async-start(bf16[4,64,1024]{2,1,0:T(8,128)(2,1)} %bitcast.282), calls=%async_computation.5 | async-start | bytes 1048576 | tf_op jit(solution)/shard_map/all_to_all | solution.py:742
  1000.5 383.0 %reduce-scatter.11.cloned.1.call-start = ((), (), s32[]{:S(2)}) async-start(), calls=%async_computation.16 | async-start | bytes 4718592 | tf_op jit(solution)/shard_map/reduce_scatter | solution.py:1138
  1002.5 46.9 %collective-permute-start.52 = (bf16[256,2048]{1,0:T(8,128)(2,1)S(1)}, bf16[256,2048]{1,0:T(8,128)(2,1)S(1)}, u32[]{:S(2)}, u32[]{:S(2)}) collective-permute-start(bf16[256,2048]{1,0:T(8,128)(2,1)S(1)} %add_convert_fusion.6), channel_id=1, source_target_pairs={{0,1},{1,0},{2,3},{3,2},{4,5},{5,4},{6,7},{7,6},{8,9},{9,8},{10,11... | collective-permute-start | bytes 3145736 | tf_op jit(solution)/shard_map/ppermute | solution.py:549
  1057.3 50.1 %collective-permute-start.59 = (bf16[256,2048]{1,0:T(8,128)(2,1)S(1)}, bf16[256,2048]{1,0:T(8,128)(2,1)}, u32[]{:S(2)}, u32[]{:S(2)}) collective-permute-start(bf16[256,2048]{1,0:T(8,128)(2,1)S(1)} %get-tuple-element.220), channel_id=1, source_target_pairs={{0,1},{1,0},{2,3},{3,2},{4,5},{5,4},{6,7},{7,6},{8,9},{9,8},{10,11... | collective-permute-start | bytes 3145736 | tf_op jit(solution)/shard_map/ppermute | solution.py:549
  1057.6 25.9 %collective-permute-start.64 = (f32[1,256]{1,0:T(1,128)S(1)}, f32[1,256]{1,0:T(1,128)S(1)}, u32[]{:S(2)}, u32[]{:S(2)}) collective-permute-start(f32[1,256]{1,0:T(1,128)S(1)} %bitcast.342), channel_id=1, source_target_pairs={{0,1},{1,0},{2,3},{3,2},{4,5},{5,4},{6,7},{7,6},{8,9},{9,8},{10,11... | collective-permute-start | bytes 3080 | tf_op jit(solution)/shard_map/ppermute | solution.py:549
  1074.8 29.5 %collective-permute-start.46 = (bf16[256,2048]{1,0:T(8,128)(2,1)S(1)}, bf16[256,2048]{1,0:T(8,128)(2,1)}, u32[]{:S(2)}, u32[]{:S(2)}) collective-permute-start(bf16[256,2048]{1,0:T(8,128)(2,1)S(1)} %get-tuple-element.164), channel_id=1, source_target_pairs={{0,1},{1,0},{2,3},{3,2},{4,5},{5,4},{6,7},{7,6},{8,9},{9,8},{10,11... | collective-permute-start | bytes 3145736 | tf_op jit(solution)/shard_map/ppermute | solution.py:549
  1075.2 50.0 %collective-permute-start.63 = (bf16[512,2048]{1,0:T(8,128)(2,1)}, bf16[512,2048]{1,0:T(8,128)(2,1)}, u32[]{:S(2)}, u32[]{:S(2)}) collective-permute-start(bf16[512,2048]{1,0:T(8,128)(2,1)} %slice.772), channel_id=1, source_target_pairs={{0,8},{8,0},{1,9},{9,1},{2,10},{10,2},{3,11},{11,3},{4,12},{12,4},... | collective-permute-start | bytes 6291464 | tf_op jit(solution)/shard_map/ppermute | solution.py:549
  1108.9 19.2 %collective-permute-start.60 = (bf16[512,2048]{1,0:T(8,128)(2,1)S(1)}, bf16[512,2048]{1,0:T(8,128)(2,1)S(1)}, u32[]{:S(2)}, u32[]{:S(2)}) collective-permute-start(bf16[512,2048]{1,0:T(8,128)(2,1)S(1)} %pad_maximum_fusion.19), channel_id=1, source_target_pairs={{0,8},{8,0},{1,9},{9,1},{2,10},{10,2},{3,11},{11,3},{4,12},{12,4},... | collective-permute-start | bytes 6291464 | tf_op jit(solution)/shard_map/ppermute | solution.py:549
  1109.0 89.9 %collective-permute-start.47 = (bf16[512,2048]{1,0:T(8,128)(2,1)}, bf16[512,2048]{1,0:T(8,128)(2,1)}, u32[]{:S(2)}, u32[]{:S(2)}) collective-permute-start(bf16[512,2048]{1,0:T(8,128)(2,1)} %pad_maximum_fusion.16), channel_id=1, source_target_pairs={{0,8},{8,0},{1,9},{9,1},{2,10},{10,2},{3,11},{11,3},{4,12},{12,4},... | collective-permute-start | bytes 6291464 | tf_op jit(solution)/shard_map/ppermute | solution.py:549
  1127.8 64.9 %collective-permute-start.66 = (bf16[256,2048]{1,0:T(8,128)(2,1)S(1)}, bf16[256,2048]{1,0:T(8,128)(2,1)}, u32[]{:S(2)}, u32[]{:S(2)}) collective-permute-start(bf16[256,2048]{1,0:T(8,128)(2,1)S(1)} %add_convert_fusion.5), channel_id=1, source_target_pairs={{0,1},{1,0},{2,3},{3,2},{4,5},{5,4},{6,7},{7,6},{8,9},{9,8},{10,11... | collective-permute-start | bytes 3145736 | tf_op jit(solution)/shard_map/ppermute | solution.py:549
  1204.0 20.9 %all-to-all-start.2 = ((bf16[4,64,2432]{2,1,0:T(8,128)(2,1)}), bf16[4,64,2432]{2,1,0:T(8,128)(2,1)}, u32[]{:S(2)}, u32[]{:S(2)}) async-start(bf16[4,64,2432]{2,1,0:T(8,128)(2,1)} %bitcast.271), calls=%async_computation.4 | async-start | bytes 2490368 | tf_op jit(solution)/shard_map/all_to_all | solution.py:742
  1208.4 266.6 %reduce-scatter.9.cloned.1.call-start = ((), (), s32[]{:S(2)}) async-start(), calls=%async_computation.15 | async-start | bytes 11206656 | tf_op jit(solution)/shard_map/reduce_scatter | solution.py:1138
  1266.0 26.1 %collective-permute-start.70 = (bf16[256,2048]{1,0:T(8,128)(2,1)S(1)}, bf16[256,2048]{1,0:T(8,128)(2,1)S(1)}, u32[]{:S(2)}, u32[]{:S(2)}) collective-permute-start(bf16[256,2048]{1,0:T(8,128)(2,1)S(1)} %add_convert_fusion.4), channel_id=1, source_target_pairs={{0,1},{1,0},{2,3},{3,2},{4,5},{5,4},{6,7},{7,6},{8,9},{9,8},{10,11... | collective-permute-start | bytes 3145736 | tf_op jit(solution)/shard_map/ppermute | solution.py:549
  1266.3 48.3 %collective-permute-start.73 = (bf16[256,2048]{1,0:T(8,128)(2,1)S(1)}, bf16[256,2048]{1,0:T(8,128)(2,1)S(1)}, u32[]{:S(2)}, u32[]{:S(2)}) collective-permute-start(bf16[256,2048]{1,0:T(8,128)(2,1)S(1)} %copy-done.52), channel_id=1, source_target_pairs={{0,1},{1,0},{2,3},{3,2},{4,5},{5,4},{6,7},{7,6},{8,9},{9,8},{10,11... | collective-permute-start | bytes 3145736 | tf_op jit(solution)/shard_map/ppermute | solution.py:549
  1295.5 40.7 %collective-permute-start.71 = (bf16[256,2048]{1,0:T(8,128)(2,1)S(1)}, bf16[256,2048]{1,0:T(8,128)(2,1)S(1)}, u32[]{:S(2)}, u32[]{:S(2)}) collective-permute-start(bf16[256,2048]{1,0:T(8,128)(2,1)S(1)} %fusion.13), channel_id=1, source_target_pairs={{0,1},{1,0},{2,3},{3,2},{4,5},{5,4},{6,7},{7,6},{8,9},{9,8},{10,11... | collective-permute-start | bytes 3145736 | tf_op jit(solution)/shard_map/ppermute | solution.py:549
  1316.1 45.4 %collective-permute-start.74 = (bf16[512,2048]{1,0:T(8,128)(2,1)}, bf16[512,2048]{1,0:T(8,128)(2,1)}, u32[]{:S(2)}, u32[]{:S(2)}) collective-permute-start(bf16[512,2048]{1,0:T(8,128)(2,1)} %pad_maximum_fusion.21), channel_id=1, source_target_pairs={{0,8},{8,0},{1,9},{9,1},{2,10},{10,2},{3,11},{11,3},{4,12},{12,4},... | collective-permute-start | bytes 6291464 | tf_op jit(solution)/shard_map/ppermute | solution.py:549
  1337.8 23.8 %collective-permute-start.72 = (bf16[512,2048]{1,0:T(8,128)(2,1)}, bf16[512,2048]{1,0:T(8,128)(2,1)}, u32[]{:S(2)}, u32[]{:S(2)}) collective-permute-start(bf16[512,2048]{1,0:T(8,128)(2,1)} %pad_maximum_fusion.20), channel_id=1, source_target_pairs={{0,8},{8,0},{1,9},{9,1},{2,10},{10,2},{3,11},{11,3},{4,12},{12,4},... | collective-permute-start | bytes 6291464 | tf_op jit(solution)/shard_map/ppermute | solution.py:549
  1357.7 31.4 %collective-permute-start.68 = (bf16[256,2048]{1,0:T(8,128)(2,1)}, bf16[256,2048]{1,0:T(8,128)(2,1)}, u32[]{:S(2)}, u32[]{:S(2)}) collective-permute-start(bf16[256,2048]{1,0:T(8,128)(2,1)} %get-tuple-element.239), channel_id=1, source_target_pairs={{2,0},{0,2},{10,4},{8,6},{6,8},{4,10},{14,12},{12,14},{3,1},{1,3},... | collective-permute-start | bytes 3145736 | tf_op jit(solution)/shard_map/ppermute | solution.py:678
  1359.7 29.5 %collective-permute-start.67 = (bf16[256,2048]{1,0:T(8,128)(2,1)}, bf16[256,2048]{1,0:T(8,128)(2,1)S(1)}, u32[]{:S(2)}, u32[]{:S(2)}) collective-permute-start(bf16[256,2048]{1,0:T(8,128)(2,1)} %get-tuple-element.240), channel_id=1, source_target_pairs={{0,0},{2,2},{8,4},{10,6},{4,8},{6,10},{12,12},{14,14},{1,1},{3,3},... | collective-permute-start | bytes 3145736 | tf_op jit(solution)/shard_map/ppermute | solution.py:678
  1381.6 61.0 %collective-permute-start.76 = (bf16[256,2048]{1,0:T(8,128)(2,1)}, bf16[256,2048]{1,0:T(8,128)(2,1)}, u32[]{:S(2)}, u32[]{:S(2)}) collective-permute-start(bf16[256,2048]{1,0:T(8,128)(2,1)} %get-tuple-element.237), channel_id=1, source_target_pairs={{2,0},{0,2},{10,4},{8,6},{6,8},{4,10},{14,12},{12,14},{3,1},{1,3},... | collective-permute-start | bytes 3145736 | tf_op jit(solution)/shard_map/ppermute | solution.py:678
  1381.6 60.9 %collective-permute-start.75 = (bf16[256,2048]{1,0:T(8,128)(2,1)}, bf16[256,2048]{1,0:T(8,128)(2,1)S(1)}, u32[]{:S(2)}, u32[]{:S(2)}) collective-permute-start(bf16[256,2048]{1,0:T(8,128)(2,1)} %get-tuple-element.238), channel_id=1, source_target_pairs={{0,0},{2,2},{8,4},{10,6},{4,8},{6,10},{12,12},{14,14},{1,1},{3,3},... | collective-permute-start | bytes 3145736 | tf_op jit(solution)/shard_map/ppermute | solution.py:678
  1383.5 91.4 %all-to-all-start.5 = ((bf16[4,64,1024]{2,1,0:T(8,128)(2,1)}), bf16[4,64,1024]{2,1,0:T(8,128)(2,1)S(1)}, u32[]{:S(2)}, u32[]{:S(2)}) async-start(bf16[4,64,1024]{2,1,0:T(8,128)(2,1)} %bitcast.283), calls=%async_computation.9 | async-start | bytes 1048576 | tf_op jit(solution)/shard_map/all_to_all | solution.py:742
  1474.9 39.9 %all-to-all-start.4 = ((bf16[4,64,2432]{2,1,0:T(8,128)(2,1)}), bf16[4,64,2432]{2,1,0:T(8,128)(2,1)S(1)}, u32[]{:S(2)}, u32[]{:S(2)}) async-start(bf16[4,64,2432]{2,1,0:T(8,128)(2,1)} %bitcast.272), calls=%async_computation.7 | async-start | bytes 2490368 | tf_op jit(solution)/shard_map/all_to_all | solution.py:742
  (143 other events, 3432.5 us)
Sparse Core Ops, SparseCore 0:
  88.2 124.2 all-gather.3
  295.5 170.4 all-gather.5
  487.8 93.8 all-gather.7
  888.1 108.2 reduce-scatter.4
  1000.3 170.5 reduce-scatter.6
  1174.7 87.1 reduce-scatter.10
  1265.6 209.2 reduce-scatter.8
